TPU v7x, 32 devices: a whole 2x2x4 slice. The times are simulated.
32 devices in a mesh: dp: 16 (over z, x, core), space: 2 (over y).
Axes of the slice: x: 2, y: 2, z: 4, core: 2. Of those that a mesh axis runs over, the one named last changes fastest.
Arguments:
- field_in: bfloat16 [1, 512, 512, 128], P(None, 'space', 'dp'), may hold values from -6 to 6
- pre_act: bfloat16 [1, 512, 512, 128], P(None, 'space', 'dp'), may hold values from -8 to 8
- cotangent: bfloat16 [1, 512, 512, 128], P(None, 'space', 'dp'), may hold values from -6 to 6
- spec_weight: bfloat16 [64, 64, 2, 128, 128], P('dp', 'space'), may hold values from -0.25 to 0.25
- local_weight: bfloat16 [128, 128], replicated, may hold values from -0.5 to 0.5
Outputs:
- grad_input: bfloat16 [1, 512, 512, 128], P(None, 'space', 'dp')
- grad_spectral: bfloat16 [64, 64, 2, 128, 128], P('dp', 'space')
- grad_local: float32 [128, 128], replicated
- grad_bias: float32 [128], replicated
All inputs are finite; a program needn't handle non-finite values.
Results may differ from a plain program's by a relative error of at most 0.0075.
The roundings to bfloat16 on the way count: a program that leaves them out, or rounds other values in their place, can miss the bound.
Values may be sent and summed in bfloat16 or wider, within the bound.
No kernel may reach another device: no remote copies, remote signals or barrier semaphores. Data moves between devices by JAX's collectives and lax.ppermute only.
A program may use at most 128 MiB of HBM per device.

v0:
```python
import math

import jax
import jax.numpy as jnp
from jax import lax
from jax.sharding import PartitionSpec as P

root_two_pi = 0.7978845608028654
cubic_coef = 0.044715


def gelu_slope(values):
    tangent = jnp.tanh(root_two_pi * (values + cubic_coef * values * values * values))
    return 0.5 * (1.0 + tangent) + 0.5 * values * (1.0 - tangent * tangent) * root_two_pi * (
        1.0 + 3.0 * cubic_coef * values * values
    )


def y_basis(grid_cols, ky_count):
    positions = jnp.arange(grid_cols, dtype=jnp.int32)
    frequency = jnp.arange(ky_count, dtype=jnp.int32)
    phases = positions[:, None] * frequency[None, :] % grid_cols
    angles = phases.astype(jnp.float32) * (2.0 * math.pi / grid_cols)
    basis_table = jnp.stack([jnp.cos(angles), -jnp.sin(angles)], axis=2).reshape(
        grid_cols, 2 * ky_count
    )
    return basis_table.astype(jnp.bfloat16)


def x_rows_table(positions, grid_rows, kx_count):
    mode_index = jnp.arange(kx_count, dtype=jnp.int32)
    frequency = jnp.where(mode_index < kx_count // 2, mode_index, mode_index - kx_count)
    phases = frequency[:, None] * positions[None, :] % grid_rows
    angles = phases.astype(jnp.float32) * (2.0 * math.pi / grid_rows)
    cosine = jnp.cos(angles)
    sine = jnp.sin(angles)
    upper_rows = jnp.stack([cosine, sine], axis=1)
    lower_rows = jnp.stack([-sine, cosine], axis=1)
    return jnp.stack([upper_rows, lower_rows], axis=0).astype(jnp.bfloat16)


def on_device(field_in, pre_act, cotangent, spec_weight, local_weight):
    batch_size, slab_rows, col_block, channels = field_in.shape
    space_count = lax.axis_size("space")
    data_count = lax.axis_size("dp")
    grid_rows = slab_rows * space_count
    grid_cols = col_block * data_count
    row_count = slab_rows // data_count
    held_count = space_count * row_count
    kx_local = spec_weight.shape[0]
    kx_count = kx_local * data_count
    ky_local = spec_weight.shape[1]
    ky_count = ky_local * space_count
    data_index = lax.axis_index("dp")
    space_index = lax.axis_index("space")
    y_table = y_basis(grid_cols, ky_count)
    held_rows = (
        jnp.arange(space_count, dtype=jnp.int32)[:, None] * slab_rows
        + data_index * row_count
        + jnp.arange(row_count, dtype=jnp.int32)[None, :]
    ).reshape(held_count)
    x_held = x_rows_table(held_rows, grid_rows, kx_count)
    delta_field = (cotangent.astype(jnp.float32) * gelu_slope(pre_act.astype(jnp.float32))).astype(
        jnp.bfloat16
    )
    local_term = jnp.einsum(
        "bxyc,bxyo->co", field_in, delta_field, preferred_element_type=jnp.float32
    )
    bias_term = jnp.sum(delta_field, axis=(0, 1, 2), dtype=jnp.float32)
    local_sum, bias_sum = lax.psum((local_term, bias_term), ("dp", "space"))
    stacked = jnp.stack([field_in, delta_field])
    lines = lax.all_to_all(stacked, "dp", split_axis=2, concat_axis=3, tiled=True)
    pairs = lax.all_to_all(
        jnp.einsum("fbxyc,yr->fbxrc", lines, y_table, preferred_element_type=jnp.float32).astype(
            jnp.bfloat16
        ),
        "space",
        split_axis=3,
        concat_axis=2,
        tiled=True,
    )
    field_count = pairs.shape[0]
    split_pairs = pairs.reshape(field_count, batch_size, held_count, ky_local, 2, channels)
    table = x_held
    owned = lax.psum_scatter(
        jnp.einsum("qjpx,fbxkpc->jfbkqc", table, split_pairs, preferred_element_type=jnp.float32),
        "dp",
        scatter_dimension=0,
        tiled=True,
    ).astype(jnp.bfloat16)
    input_owned = owned[:, 0]
    delta_owned = owned[:, 1]
    ky_index = space_index * ky_local + jnp.arange(ky_local, dtype=jnp.int32)
    ky_scale = jnp.where(ky_index == 0, 1.0, 2.0).astype(jnp.float32) / (grid_rows * grid_cols)
    products = jnp.einsum(
        "jbkqc,jbkpo->jkqpco", input_owned, delta_owned, preferred_element_type=jnp.float32
    )
    grad_real = products[:, :, 0, 0] + products[:, :, 1, 1]
    grad_imag = products[:, :, 0, 1] - products[:, :, 1, 0]
    grad_spectral = (
        jnp.stack([grad_real, grad_imag], axis=2)
        * (ky_scale / batch_size)[None, :, None, None, None]
    ).astype(jnp.bfloat16)
    adjoint = jnp.einsum(
        "jbkpo,jkqco->bjkpqc", delta_owned, spec_weight, preferred_element_type=jnp.float32
    )
    back_real = adjoint[:, :, :, 0, 0] + adjoint[:, :, :, 1, 1]
    back_imag = adjoint[:, :, :, 1, 0] - adjoint[:, :, :, 0, 1]
    mode_back = (
        jnp.stack([back_real, back_imag], axis=3) * ky_scale[None, None, :, None, None]
    ).astype(jnp.bfloat16)
    table = x_held
    along_x = jnp.einsum(
        "qjpx,bjkqc->bxkpc",
        table,
        lax.all_gather(mode_back, "dp", axis=1, tiled=True),
        preferred_element_type=jnp.float32,
    ).astype(jnp.bfloat16)
    along_x = along_x.reshape(batch_size, held_count, 2 * ky_local, channels)
    lines_back = lax.all_to_all(along_x, "space", split_axis=1, concat_axis=2, tiled=True)
    local_part = jnp.einsum(
        "bxyo,co->bxyc", delta_field, local_weight, preferred_element_type=jnp.float32
    )
    slab_lines = lax.all_gather(lines_back, "dp", axis=1, tiled=True)
    y_block = lax.dynamic_slice_in_dim(y_table, data_index * col_block, col_block, 0)
    spectral_part = jnp.einsum(
        "bxrc,yr->bxyc", slab_lines, y_block, preferred_element_type=jnp.float32
    ).astype(jnp.bfloat16)
    grad_input = (spectral_part.astype(jnp.float32) + local_part).astype(jnp.bfloat16)
    return (grad_input, grad_spectral, local_sum / batch_size, bias_sum / batch_size)


def solution(mesh):
    placed = (
        P(None, "space", "dp", None),
        P(None, "space", "dp", None),
        P(None, "space", "dp", None),
        P("dp", "space", None, None, None),
        P(),
    )
    return jax.shard_map(
        on_device,
        mesh=mesh,
        in_specs=placed,
        out_specs=(P(None, "space", "dp", None), P("dp", "space", None, None, None), P(), P()),
        check_vma=False,
    )
```

profile of v0, /device:TPU:0, one launch (start us, length us, event | category | flops | bytes accessed | tf_op | source)
XLA Modules:
  0.0 483.1 jit_solution(306480126100655884)
XLA Ops:
  8.0 4.9 %convert_reduce_fusion = (f32[128]{0:T(128)S(1)}, bf16[1,256,32,128]{3,2,1,0:T(8,128)(2,1)S(1)}) fusion(bf16[1,256,32,128]{3,2,1,0:T(8,128)(2,1)} %param.6, bf16[1,256,32,128]{3,2,1,0:T(8,128)(2,1)} %param.7), kind=kLoop, calls=%fused_computation.29 | loop fusion | flops 24117120 | bytes 6291968 | tf_op jit(solution)/shard_map/reduce_sum | solution.py:69
  12.9 2.5 pad_maximum_fusion
  15.4 7.4 %all-to-all-start = ((bf16[2,1,256,32,128]{4,3,1,0,2:T(8,128)(2,1)}), bf16[2,1,256,32,128]{4,3,1,0,2:T(8,128)(2,1)}, u32[]{:S(2)}, u32[]{:S(2)}) async-start(bf16[2,1,256,32,128]{4,3,1,0,2:T(8,128)(2,1)} %pad_maximum_fusion), calls=%async_computation | async-start | bytes 8388608 | tf_op jit(solution)/shard_map/all_to_all | solution.py:72
  23.6 76.9 %all-to-all-done = bf16[2,1,256,32,128]{4,3,1,0,2:T(8,128)(2,1)} async-done(((bf16[2,1,256,32,128]{4,3,1,0,2:T(8,128)(2,1)}), bf16[2,1,256,32,128]{4,3,1,0,2:T(8,128)(2,1)}, u32[]{:S(2)}, u32[]{:S(2)}) %all-to-all-start) | async-done | bytes 4194336 | tf_op jit(solution)/shard_map/all_to_all | solution.py:72
  100.5 3.4 copy.66
  104.6 1.6 copy.67
  106.3 3.6 all-to-all-start.1
  110.3 14.4 %all-to-all-done.1 = bf16[2,1,16,128,128]{4,2,0,1,3:T(8,128)(2,1)S(1)} async-done(((bf16[2,1,16,128,128]{4,2,0,1,3:T(8,128)(2,1)}), bf16[2,1,16,128,128]{4,2,0,1,3:T(8,128)(2,1)S(1)}, u32[]{:S(2)}, u32[]{:S(2)}) %all-to-all-start.1) | async-done | bytes 1048608 | tf_op jit(solution)/shard_map/all_to_all | solution.py:73
  125.6 4.4 copy.69
  130.1 86.1 %reduce-scatter.2.cloned.1.call-done = f32[4,2,1,32,2,128]{5,3,4,2,1,0:T(8,128)} async-done(((f32[64,2,1,32,2,128]{5,3,4,2,1,0:T(8,128)}), f32[4,2,1,32,2,128]{5,3,4,2,1,0:T(8,128)}) %reduce-scatter.2.cloned.1.call-update) | async-done | bytes 262160 | tf_op jit(solution)/shard_map/reduce_scatter | solution.py:85
  217.4 5.6 %convolution_bitcast_fusion.2 = f32[1,4,32,2,2,128]{5,3,4,2,1,0:T(2,128)S(1)} fusion(bf16[4,32,2,128,128]{4,3,2,1,0:T(8,128)(2,1)} %param.8, bf16[4,2,1,32,2,128]{5,4,3,0,2,1:T(2,128)(2,1)S(1)} %copy.104), kind=kOutput, calls=%fused_computation.39 | convolution fusion | flops 16777216 | bytes 8716288 | tf_op jit(solution)/shard_map/jbkpo,jkqco->bjkpqc/dot_general | solution.py:104
  223.9 37.1 %all-gather.3.cloned.1.call-done = bf16[1,64,32,2,128]{4,2,1,3,0:T(8,128)(2,1)} async-done(((bf16[1,4,32,2,128]{4,2,1,3,0:T(8,128)(2,1)}), bf16[1,64,32,2,128]{4,2,1,3,0:T(8,128)(2,1)}) %all-gather.3.cloned.1.call-update) | async-done | bytes 1048592 | tf_op jit(solution)/shard_map/all_gather | solution.py:116
  261.1 1.7 fusion.21
  263.8 3.5 all-to-all-start.2
  267.5 3.0 fusion.22
  270.6 5.4 %all-to-all-done.2 = bf16[1,32,64,128]{3,2,0,1:T(8,128)(2,1)S(1)} async-done(((bf16[1,32,64,128]{3,2,0,1:T(8,128)(2,1)}), bf16[1,32,64,128]{3,2,0,1:T(8,128)(2,1)S(1)}, u32[]{:S(2)}, u32[]{:S(2)}) %all-to-all-start.2) | async-done | bytes 524320 | tf_op jit(solution)/shard_map/all_to_all | solution.py:120
  276.9 39.4 %psum.15 = f32[128]{0:T(128)} all-reduce(f32[128]{0:T(128)S(1)} %get-tuple-element.20), channel_id=1, replica_groups=mesh['dp'=16,'space'=2] {'dp','space'}, use_global_device_ids=true, to_apply=%region_3.4 | all-reduce | flops 128 | bytes 1024 | tf_op jit(solution)/shard_map/psum | solution.py:70
  316.3 110.9 %all-reduce.2.cloned.1.call-done = f32[128,128]{0,1:T(8,128)} async-done(((f32[128,128]{0,1:T(8,128)}), f32[128,128]{0,1:T(8,128)}) %all-reduce.2.cloned.1.call-update) | async-done | bytes 65552 | tf_op jit(solution)/shard_map/psum | solution.py:70
  427.2 1.6 copy.82
  428.9 11.5 %multiply_bitcast_fusion = f32[4,32,2,2,128,128]{5,4,1,0,3,2:T(8,128)} fusion(f32[4,32,2,128]{3,1,0,2:T(8,128)S(1)} %copy.80, f32[4,32,2,128]{3,1,0,2:T(8,128)S(1)} %copy.79), kind=kLoop, calls=%fused_computation | loop fusion | flops 8388608 | bytes 33816576 | tf_op jit(solution)/shard_map/jbkqc,jbkpo->jkqpco/transpose | solution.py:95
  440.4 19.1 %fusion.2 = (f32[4,32,1,128,128]{4,3,2,1,0:T(8,128)}, f32[4,32,1,128,128]{4,3,2,1,0:T(8,128)}) fusion(f32[4,32,2,2,128,128]{5,4,1,0,3,2:T(8,128)} %multiply_bitcast_fusion), kind=kLoop, calls=%fused_computation.13 | loop fusion | flops 4194304 | bytes 50331648 | tf_op jit(solution)/shard_map/add | solution.py:98
  459.5 9.7 %fusion = bf16[4,32,2,128,128]{4,3,2,1,0:T(8,128)(2,1)} fusion(f32[4,32,1,128,128]{4,3,2,1,0:T(8,128)} %get-tuple-element.23, f32[4,32,1,128,128]{4,3,2,1,0:T(8,128)} %get-tuple-element.22, f32[32]{0:T(128)S(1)} %fusion.51), kind=kLoop, calls=%fused_computation.2 | loop fusion | flops 12582912 | bytes 25165952 | tf_op jit(solution)/shard_map/convert_element_type | solution.py:103
  469.3 4.7 fusion.3
  474.0 2.0 fusion.15
  (37 shorter events, 7.2 us)
Async XLA Ops:
  8.0 466.0 %copy-start = (bf16[128,128]{1,0:T(8,128)(2,1)S(1)}, bf16[128,128]{1,0:T(8,128)(2,1)}, u32[]{:S(2)}) copy-start(bf16[128,128]{1,0:T(8,128)(2,1)} %param.9) | copy-start | bytes 98308
  8.0 4.9 %copy-start.1 = (bf16[1,256,32,128]{3,2,1,0:T(8,128)(2,1)S(1)}, bf16[1,256,32,128]{3,2,1,0:T(8,128)(2,1)}, u32[]{:S(2)}) copy-start(bf16[1,256,32,128]{3,2,1,0:T(8,128)(2,1)} %param.5) | copy-start | bytes 6291460
  15.4 85.1 %all-to-all-start = ((bf16[2,1,256,32,128]{4,3,1,0,2:T(8,128)(2,1)}), bf16[2,1,256,32,128]{4,3,1,0,2:T(8,128)(2,1)}, u32[]{:S(2)}, u32[]{:S(2)}) async-start(bf16[2,1,256,32,128]{4,3,1,0,2:T(8,128)(2,1)} %pad_maximum_fusion), calls=%async_computation | async-start | bytes 8388608 | tf_op jit(solution)/shard_map/all_to_all | solution.py:72
  106.3 18.4 %all-to-all-start.1 = ((bf16[2,1,16,128,128]{4,2,0,1,3:T(8,128)(2,1)}), bf16[2,1,16,128,128]{4,2,0,1,3:T(8,128)(2,1)S(1)}, u32[]{:S(2)}, u32[]{:S(2)}) async-start(bf16[2,1,16,128,128]{4,2,0,1,3:T(8,128)(2,1)} %copy.67), calls=%async_computation.1 | async-start | bytes 2097152 | tf_op jit(solution)/shard_map/all_to_all | solution.py:73
  109.9 106.3 %reduce-scatter.2.cloned.1.call-start = ((), (), s32[]{:S(2)}) async-start(), calls=%async_computation.4 | async-start | bytes 4456448 | tf_op jit(solution)/shard_map/reduce_scatter | solution.py:85
  130.1 131.0 %all-gather.3.cloned.1.call-start = ((), (), s32[]{:S(2)}) async-start(), calls=%async_computation.5 | async-start | bytes 1114112 | tf_op jit(solution)/shard_map/all_gather | solution.py:116
  263.8 12.2 %all-to-all-start.2 = ((bf16[1,32,64,128]{3,2,0,1:T(8,128)(2,1)}), bf16[1,32,64,128]{3,2,0,1:T(8,128)(2,1)S(1)}, u32[]{:S(2)}, u32[]{:S(2)}) async-start(bf16[1,32,64,128]{3,2,0,1:T(8,128)(2,1)} %copy.75), calls=%async_computation.3 | async-start | bytes 1048576 | tf_op jit(solution)/shard_map/all_to_all | solution.py:120
  267.3 159.9 %all-reduce.2.cloned.1.call-start = ((), (), s32[]{:S(2)}) async-start(), calls=%async_computation.7 | async-start | bytes 131072 | tf_op jit(solution)/shard_map/psum | solution.py:70
  270.5 198.7 %all-gather.5.cloned.1.call-start = ((), (), s32[]{:S(2)}) async-start(), calls=%async_computation.6 | async-start | bytes 8912896 | tf_op jit(solution)/shard_map/all_gather | solution.py:124
Sparse Core Ops, SparseCore 0:
  130.2 85.9 reduce-scatter.1
  224.1 36.9 all-gather.2
  277.0 74.6 all-gather.4
Sparse Core Ops, SparseCore 1:
  274.9 152.3 all-reduce.1
where the time goes:
time: 485 us; the launch traced here: 483 us
  waiting for transfers between devices  331 us (68%)
  other arithmetic  49.5 us (10%)
  blocking collectives  39.4 us (8%)
  matrix products  18.5 us (4%)
  between operations  15.4 us (3%)
  starting transfers between devices  14.8 us (3%)
  local copies, waits for them, and re-layouts  14.6 us (3%)
    psum x1, waiting for transfers between devices, on_device(): local_sum, bias_sum = lax.psum((local_term, bias_term), ('dp', 'space'))  111 us
    reduce_scatter x1, waiting for transfers between devices, on_device(): lax.psum_scatter(jnp.einsum('qjpx,fbxkpc->jfbkqc', table, split_pairs, pr...  86.1 us
    all_to_all x1, waiting for transfers between devices, on_device(): lax.all_to_all(stacked, 'dp', split_axis=2, concat_axis=3, tiled=True)  76.9 us
    psum x1, blocking collectives, on_device(): local_sum, bias_sum = lax.psum((local_term, bias_term), ('dp', 'space'))  39.4 us
    all_gather x1, waiting for transfers between devices, on_device(): lax.all_gather(mode_back, 'dp', axis=1, tiled=True)  37.1 us
    add x1, other arithmetic, on_device(): grad_real = products[:, :, 0, 0] + products[:, :, 1, 1]  19.1 us
    all_to_all x1, waiting for transfers between devices, on_device(): lax.all_to_all(jnp.einsum('fbxyc,yr->fbxrc', lines, y_table, preferred_el...  14.4 us
    transpose x1, other arithmetic, on_device(): jnp.einsum('jbkqc,jbkpo->jkqpco', input_owned, delta_owned, preferred_ele...  11.5 us
  transfers between devices with their start and end apart: 7, of which 6 were waited for; matrix products, arithmetic and copies ran while one was open for 10% of the time, Pallas kernels for 0%

commit v1 on v0

v1 whole, which is shorter than its diff:
```python
import math

import jax
import jax.numpy as jnp
from jax import lax
from jax.experimental import pallas as pl
from jax.experimental.pallas import tpu as pltpu
from jax.sharding import PartitionSpec as P

root_two_pi = 0.7978845608028654
cubic_coef = 0.044715
f32 = jnp.float32
bf16 = jnp.bfloat16
vmem_bytes = 40 * 1024 * 1024


def gelu_slope(values):
    square = values * values
    tangent = jnp.tanh(root_two_pi * (values + cubic_coef * square * values))
    return 0.5 * (1.0 + tangent) + 0.5 * values * (1.0 - tangent * tangent) * root_two_pi * (
        1.0 + 3.0 * cubic_coef * square
    )


def params(steps=1):
    return pltpu.CompilerParams(
        vmem_limit_bytes=vmem_bytes, dimension_semantics=("arbitrary",) * steps
    )


def whole(shape):
    return pl.BlockSpec(shape, lambda *_: (0,) * len(shape))


def x_transform(table, wide, narrow, out_ref):
    rows, columns, channels = out_ref.shape
    grid_rows = table.shape[1]
    for y in range(0, columns, 2):
        pair = [
            wide[pl.ds(y + i, grid_rows, stride=columns), :].astype(bf16) for i in range(2)
        ]
        sums = jnp.dot(table, jnp.concatenate(pair, axis=1), preferred_element_type=f32)
        for i in range(2):
            narrow[pl.ds(y + i, rows, stride=columns), :] = sums[:, i * channels : (i + 1) * channels]
    out_ref[...] = narrow[...].reshape(rows, columns, channels).astype(bf16)


def delta_kernel(table_ref, pre_ref, cot_ref, delta_ref, out_ref, wide, narrow):
    grid_rows, columns, channels = pre_ref.shape
    step = 8

    def slab(i, carry):
        rows = pl.ds(pl.multiple_of(i * step, step), step)
        slope = gelu_slope(pre_ref[rows].astype(f32))
        delta = (cot_ref[rows].astype(f32) * slope).astype(bf16)
        delta_ref[rows] = delta
        wide[pl.ds(pl.multiple_of(i * step * columns, step * columns), step * columns), :] = (
            delta.astype(f32).reshape(step * columns, channels)
        )
        return carry

    lax.fori_loop(0, grid_rows // step, slab, 0, unroll=2)
    x_transform(table_ref[...], wide, narrow, out_ref)


def delta_call(table, pre_act, cotangent):
    grid_rows, columns, channels = pre_act.shape
    rows = table.shape[0]
    block = min(16, columns)
    field = pl.BlockSpec((grid_rows, block, channels), lambda i: (0, i, 0))
    return pl.pallas_call(
        delta_kernel,
        grid=(columns // block,),
        in_specs=[whole(table.shape), field, field],
        out_specs=[field, pl.BlockSpec((rows, block, channels), lambda i: (0, i, 0))],
        out_shape=[
            jax.ShapeDtypeStruct(pre_act.shape, bf16),
            jax.ShapeDtypeStruct((rows, columns, channels), bf16),
        ],
        scratch_shapes=[
            pltpu.VMEM((grid_rows * block, channels), f32),
            pltpu.VMEM((rows * block, channels), f32),
        ],
        compiler_params=params(),
        cost_estimate=pl.CostEstimate(
            flops=2 * rows * pre_act.size, bytes_accessed=8 * pre_act.size, transcendentals=pre_act.size
        ),
        name="delta_and_x_sums",
    )(table, pre_act, cotangent)


def input_kernel(table_ref, field_ref, delta_ref, out_ref, local_ref, bias_ref, wide, narrow):
    grid_rows, columns, channels = field_ref.shape
    field = field_ref[...].reshape(grid_rows * columns, channels)
    delta = delta_ref[...].reshape(grid_rows * columns, channels)
    wide[...] = field.astype(f32)
    x_transform(table_ref[...], wide, narrow, out_ref)
    local = lax.dot_general(field, delta, (((0,), (0,)), ((), ())), preferred_element_type=f32)
    bias = jnp.sum(delta.astype(f32).reshape(-1, 8, channels), axis=0)

    @pl.when(pl.program_id(0) == 0)
    def _():
        local_ref[...] = local
        bias_ref[...] = bias

    @pl.when(pl.program_id(0) > 0)
    def _():
        local_ref[...] += local
        bias_ref[...] += bias


def input_call(table, field_in, delta):
    grid_rows, columns, channels = field_in.shape
    rows = table.shape[0]
    block = min(16, columns)
    field = pl.BlockSpec((grid_rows, block, channels), lambda i: (0, i, 0))
    return pl.pallas_call(
        input_kernel,
        grid=(columns // block,),
        in_specs=[whole(table.shape), field, field],
        out_specs=[
            pl.BlockSpec((rows, block, channels), lambda i: (0, i, 0)),
            whole((channels, channels)),
            whole((8, channels)),
        ],
        out_shape=[
            jax.ShapeDtypeStruct((rows, columns, channels), bf16),
            jax.ShapeDtypeStruct((channels, channels), f32),
            jax.ShapeDtypeStruct((8, channels), f32),
        ],
        scratch_shapes=[
            pltpu.VMEM((grid_rows * block, channels), f32),
            pltpu.VMEM((rows * block, channels), f32),
        ],
        compiler_params=params(),
        cost_estimate=pl.CostEstimate(
            flops=2 * (rows + channels) * field_in.size, bytes_accessed=4 * field_in.size, transcendentals=0
        ),
        name="input_x_sums_and_local",
    )(table, field_in, delta)


def y_transform_kernel(table_ref, lines_ref, *out_refs):
    sources, rows, columns, channels = lines_ref.shape
    frequencies = rows // 2
    own = len(out_refs) // 2
    size = out_refs[0].shape[1]
    table = table_ref[...]
    for t in range(frequencies):
        lines = jnp.concatenate(
            [
                lines_ref[:, 2 * t + part].reshape(sources * columns, channels)
                for part in range(2)
            ],
            axis=0,
        )
        sums = jnp.dot(table, lines, preferred_element_type=f32).astype(bf16)
        for block, out_ref in enumerate(out_refs):
            held = t if block < own else frequencies - 1 - t
            if 0 <= held < frequencies - 1:
                out_ref[held] = sums[block * size : (block + 1) * size]


def y_transform_call(table, lines, blocks, size):
    sources, rows, columns, channels = lines.shape
    held = rows // 2 - 1
    return pl.pallas_call(
        y_transform_kernel,
        out_shape=[jax.ShapeDtypeStruct((held, size, channels), bf16)] * blocks,
        compiler_params=pltpu.CompilerParams(vmem_limit_bytes=vmem_bytes),
        cost_estimate=pl.CostEstimate(
            flops=rows * table.size * channels, bytes_accessed=4 * lines.size, transcendentals=0
        ),
        name="y_sums",
    )(table, lines)


def turned(values):
    rows = values.shape[0]
    even = lax.broadcasted_iota(jnp.int32, values.shape, 0) % 2 == 0
    up = pltpu.roll(values, rows - 1, 0)
    down = pltpu.roll(values, 1, 0)
    return jnp.concatenate([values, jnp.where(even, up, -down)], axis=1)


def back_kernel(scale_ref, weight_ref, *refs):
    part_refs, (back_ref, delta_ref) = refs[:-2], refs[-2:]
    modes = weight_ref.shape[1]
    total = part_refs[0][0].astype(f32)
    for ref in part_refs[1:]:
        total = total + ref[0].astype(f32)
    delta = total.astype(bf16)
    delta_ref[0] = delta
    both = turned(delta.astype(f32)).astype(bf16)
    rows = []
    for mode in range(modes):
        weight = jnp.concatenate([weight_ref[0, mode, 0], weight_ref[0, mode, 1]], axis=1)
        rows.append(
            lax.dot_general(
                both[2 * mode : 2 * mode + 2],
                weight,
                (((1,), (1,)), ((), ())),
                preferred_element_type=f32,
            )
        )
    back_ref[0] = (jnp.concatenate(rows, axis=0) * scale_ref[...]).astype(bf16)


def back_call(scale_rows, weight, parts):
    held, modes, _, channels, _ = weight.shape
    block = min(16, modes)
    part = pl.BlockSpec((1, 2 * block, channels), lambda j, k: (j, k, 0))
    shape = jax.ShapeDtypeStruct((held, 2 * modes, channels), bf16)
    return pl.pallas_call(
        back_kernel,
        grid=(held, modes // block),
        in_specs=[
            pl.BlockSpec((2 * block, channels), lambda j, k: (k, 0)),
            pl.BlockSpec((1, block, 2, channels, channels), lambda j, k: (j, k, 0, 0, 0)),
        ]
        + [part] * len(parts),
        out_specs=[part, part],
        out_shape=[shape, shape],
        compiler_params=params(2),
        cost_estimate=pl.CostEstimate(
            flops=4 * weight.size, bytes_accessed=2 * weight.size, transcendentals=0
        ),
        name="mode_back",
    )(scale_rows, weight, *parts)


def outer_kernel(scale_ref, delta_ref, *refs):
    part_refs, out_ref = refs[:-1], refs[-1]
    modes = out_ref.shape[1]
    channels = out_ref.shape[-1]
    total = part_refs[0][0].astype(f32)
    for ref in part_refs[1:]:
        total = total + ref[0].astype(f32)
    field = total.astype(bf16).astype(f32) * scale_ref[...]
    across = field.T
    delta = turned(delta_ref[0].astype(f32))
    for mode in range(modes):
        real = across[:, 2 * mode : 2 * mode + 1]
        imag = across[:, 2 * mode + 1 : 2 * mode + 2]
        first = delta[2 * mode : 2 * mode + 1]
        second = delta[2 * mode + 1 : 2 * mode + 2]
        product = (real * first + imag * second).astype(bf16)
        out_ref[0, mode, 0] = product[:, :channels]
        out_ref[0, mode, 1] = product[:, channels:]


def outer_call(scale_rows, delta, parts):
    held, rows, channels = delta.shape
    modes = rows // 2
    block = min(16, modes)
    part = pl.BlockSpec((1, 2 * block, channels), lambda j, k: (j, k, 0))
    return pl.pallas_call(
        outer_kernel,
        grid=(held, modes // block),
        in_specs=[pl.BlockSpec((2 * block, channels), lambda j, k: (k, 0))]
        + [part] * (1 + len(parts)),
        out_specs=pl.BlockSpec(
            (1, block, 2, channels, channels), lambda j, k: (j, k, 0, 0, 0)
        ),
        out_shape=jax.ShapeDtypeStruct((held, modes, 2, channels, channels), bf16),
        compiler_params=params(2),
        cost_estimate=pl.CostEstimate(
            flops=6 * held * modes * channels * channels,
            bytes_accessed=4 * held * modes * channels * channels,
            transcendentals=0,
        ),
        name="grad_spectral",
    )(scale_rows, delta, *parts)


def y_inverse_kernel(table_ref, *refs):
    part_refs, out_ref = refs[:-1], refs[-1]
    targets, rows, columns, channels = out_ref.shape
    frequencies = rows // 2
    own = len(part_refs) // 2
    size = part_refs[0].shape[1]
    table = table_ref[...]
    for t in range(frequencies):
        first = 0 if t < frequencies - 1 else own
        last = 2 * own if t > 0 else own
        modes = jnp.concatenate(
            [
                part_refs[block][t if block < own else frequencies - 1 - t]
                for block in range(first, last)
            ],
            axis=0,
        )
        sums = lax.dot_general(
            table[first * size : last * size],
            modes,
            (((0,), (0,)), ((), ())),
            preferred_element_type=f32,
        ).astype(bf16)
        for part in range(2):
            out_ref[:, 2 * t + part] = sums[
                part * targets * columns : (part + 1) * targets * columns
            ].reshape(targets, columns, channels)


def y_inverse_call(table, parts, targets, columns):
    held, size, channels = parts[0].shape
    rows = 2 * (held + 1)
    return pl.pallas_call(
        y_inverse_kernel,
        out_shape=jax.ShapeDtypeStruct((targets, rows, columns, channels), bf16),
        compiler_params=pltpu.CompilerParams(vmem_limit_bytes=vmem_bytes),
        cost_estimate=pl.CostEstimate(
            flops=rows * table.size * channels,
            bytes_accessed=4 * targets * rows * columns * channels,
            transcendentals=0,
        ),
        name="y_inverse",
    )(table, *parts)


def final_kernel(table_ref, lines_ref, delta_ref, local_ref, out_ref, narrow, wide):
    rows, columns, channels = lines_ref.shape
    grid_rows = out_ref.shape[0]
    narrow[...] = lines_ref[...].reshape(rows * columns, channels).astype(f32)
    table = table_ref[...]
    for y in range(0, columns, 2):
        pair = [narrow[pl.ds(y + i, rows, stride=columns), :].astype(bf16) for i in range(2)]
        sums = lax.dot_general(
            table,
            jnp.concatenate(pair, axis=1),
            (((0,), (0,)), ((), ())),
            preferred_element_type=f32,
        )
        for i in range(2):
            wide[pl.ds(y + i, grid_rows, stride=columns), :] = sums[
                :, i * channels : (i + 1) * channels
            ]
    weight = local_ref[...]
    step = 16

    def slab(i, carry):
        rows_here = pl.ds(pl.multiple_of(i * step, step), step)
        flat = pl.ds(pl.multiple_of(i * step * columns, step * columns), step * columns)
        local = lax.dot_general(
            delta_ref[rows_here].reshape(step * columns, channels),
            weight,
            (((1,), (1,)), ((), ())),
            preferred_element_type=f32,
        )
        spectral = wide[flat, :].astype(bf16).astype(f32)
        out_ref[rows_here] = (spectral + local).astype(bf16).reshape(step, columns, channels)
        return carry

    lax.fori_loop(0, grid_rows // step, slab, 0, unroll=2)


def final_call(table, lines, delta, local_weight):
    rows, columns, channels = lines.shape
    grid_rows = delta.shape[0]
    block = min(16, columns)
    field = pl.BlockSpec((grid_rows, block, channels), lambda i: (0, i, 0))
    return pl.pallas_call(
        final_kernel,
        grid=(columns // block,),
        in_specs=[
            whole(table.shape),
            pl.BlockSpec((rows, block, channels), lambda i: (0, i, 0)),
            field,
            whole(local_weight.shape),
        ],
        out_specs=field,
        out_shape=jax.ShapeDtypeStruct(delta.shape, bf16),
        scratch_shapes=[
            pltpu.VMEM((rows * block, channels), f32),
            pltpu.VMEM((grid_rows * block, channels), f32),
        ],
        compiler_params=params(),
        cost_estimate=pl.CostEstimate(
            flops=2 * (rows + channels) * delta.size, bytes_accessed=5 * delta.size, transcendentals=0
        ),
        name="x_inverse_and_local",
    )(table, lines, delta, local_weight)


def on_device(field_in, pre_act, cotangent, spec_weight, local_weight):
    batch_size, slab_rows, col_block, channels = field_in.shape
    space_count = lax.axis_size("space")
    data_count = lax.axis_size("dp")
    grid_rows = slab_rows * space_count
    grid_cols = col_block * data_count
    kx_local, ky_local = spec_weight.shape[:2]
    half = data_count // 2
    half_cols = half * col_block
    row_count = 2 * (kx_local + 1)
    data_index = lax.axis_index("dp")
    space_index = lax.axis_index("space")
    upper = data_index // half

    row = jnp.arange(half * row_count, dtype=jnp.int32)
    member, inner = row // row_count, row % row_count
    t = inner // 2
    frequency = jnp.where(
        upper == 0, kx_local * member + t, kx_local * (half - 1 - member) + kx_local - t
    )
    positions = space_index * slab_rows + jnp.arange(slab_rows, dtype=jnp.int32)
    phases = frequency[:, None] * positions[None, :] % grid_rows
    angles = phases.astype(f32) * (2.0 * math.pi / grid_rows)
    x_table = jnp.where((inner % 2 == 0)[:, None], jnp.cos(angles), jnp.sin(angles)).astype(bf16)

    blocks = 2 * space_count
    size = 2 * ky_local
    row = jnp.arange(blocks * size, dtype=jnp.int32)
    block, inner = row // size, row % size
    shift = block % space_count
    sign = jnp.where((block // space_count) == upper, 1.0, -1.0).astype(f32)
    ky_index = (space_index + shift) % space_count * ky_local + inner // 2
    imaginary = inner % 2 == 1
    positions = upper * half_cols + jnp.arange(half_cols, dtype=jnp.int32)
    phases = ky_index[:, None] * positions[None, :] % grid_cols
    angles = phases.astype(f32) * (2.0 * math.pi / grid_cols)
    cosine = jnp.cos(angles)
    minus_sine = -jnp.sin(angles)
    left = jnp.where(imaginary[:, None], minus_sine, cosine)
    right = sign[:, None] * jnp.where(imaginary[:, None], -cosine, minus_sine)
    y_table = jnp.concatenate([left, right], axis=1).astype(bf16)

    ky_row = space_index * ky_local + jnp.arange(size, dtype=jnp.int32) // 2
    scale = jnp.where(ky_row == 0, 1.0, 2.0).astype(f32) / (grid_rows * grid_cols)
    scale_rows = jnp.broadcast_to(scale[:, None], (size, channels))

    halves = [list(range(half)), list(range(half, data_count))]

    def exchange(values):
        return lax.all_to_all(
            values, "dp", split_axis=0, concat_axis=0, tiled=True, axis_index_groups=halves
        )

    def pairs(mirror, shift):
        moves = []
        for d in range(data_count):
            for s in range(space_count):
                target = data_count - 1 - d if mirror else d
                moves.append(
                    (d * space_count + s, target * space_count + (s + shift) % space_count)
                )
        return moves

    order = [(mirror, shift) for mirror in (1, 0) for shift in reversed(range(space_count))][:-1]

    def gathered(parts):
        held = [parts[0]]
        for mirror, shift in order:
            held.append(
                lax.ppermute(
                    parts[mirror * space_count + shift], ("dp", "space"), pairs(mirror, shift)
                )
            )
        return held

    def spectrum_parts(x_sums):
        lines = exchange(x_sums.reshape(half, row_count, col_block, channels))
        return gathered(y_transform_call(y_table, lines, blocks, size))

    delta, delta_sums = delta_call(x_table, pre_act[0], cotangent[0])
    delta_parts = spectrum_parts(delta_sums)
    back, delta_owned = back_call(scale_rows, spec_weight, delta_parts)
    received = {(0, 0): back}
    for mirror, shift in order:
        received[(mirror, -shift % space_count)] = lax.ppermute(
            back, ("dp", "space"), pairs(mirror, shift)
        )
    modes = [received[(mirror, shift)] for mirror in (0, 1) for shift in range(space_count)]
    columns = exchange(y_inverse_call(y_table, modes, half, col_block))
    grad_input = final_call(
        x_table, columns.reshape(half * row_count, col_block, channels), delta, local_weight
    )

    input_sums, local_term, bias_term = input_call(x_table, field_in[0], delta)
    input_parts = spectrum_parts(input_sums)
    grad_spectral = outer_call(scale_rows, delta_owned, input_parts)

    device_count = data_count * space_count
    bias_row = jnp.sum(bias_term, axis=0, keepdims=True)
    share = -(-(channels + 1) // device_count)
    filler = jnp.zeros((share * device_count - channels - 1, channels), f32)
    stacked = jnp.concatenate([local_term, bias_row, filler], axis=0)
    shares = lax.all_to_all(
        stacked.reshape(device_count, share, channels), ("dp", "space"), 0, 0, tiled=True
    )
    total = jnp.sum(shares, axis=0)
    spread = jnp.broadcast_to(total[None], (device_count, share, channels))
    totals = lax.all_to_all(spread, ("dp", "space"), 0, 0, tiled=True)
    totals = totals.reshape(device_count * share, channels)
    return (grad_input[None], grad_spectral, totals[:channels], totals[channels])


def solution(mesh):
    placed = (
        P(None, "space", "dp", None),
        P(None, "space", "dp", None),
        P(None, "space", "dp", None),
        P("dp", "space", None, None, None),
        P(),
    )
    return jax.shard_map(
        on_device,
        mesh=mesh,
        in_specs=placed,
        out_specs=(P(None, "space", "dp", None), P("dp", "space", None, None, None), P(), P()),
        check_vma=False,
    )
```

time: 485 us -> 124 us (0.26)
  waiting for transfers between devices: 331 us -> 15.5 us
  other arithmetic: 49.5 us -> 2.01 us
  Pallas kernels: 0 us -> 27.7 us
  matrix products: 18.5 us -> 0 us
  between operations: 15.4 us -> 0.83 us
  starting transfers between devices: 14.8 us -> 25.1 us
    psum x1 -> x0, waiting for transfers between devices: 111 us -> none  [on_device(): local_sum, bias_sum = lax.psum((local_term, bias_term), ('dp', 'space'))]
    all_to_all x3 -> x2, waiting for transfers between devices: 96.7 us -> 0.01 us  [exchange(): lax.all_to_all(values, 'dp', split_axis=0, concat_axis=0, tiled=True, axi...]
    reduce_scatter x1 -> x0, waiting for transfers between devices: 86.1 us -> none  [on_device(): lax.psum_scatter(jnp.einsum('qjpx,fbxkpc->jfbkqc', table, split_pairs, pr...]
    all_to_all x0 -> x3, blocking collectives: none -> 40 us  [the longest x1 15.7 us: on_device(): lax.all_to_all(stacked.reshape(device_count, share, channels), ('dp', 'sp...]
    psum x1 -> x0, blocking collectives: 39.4 us -> none  [on_device(): local_sum, bias_sum = lax.psum((local_term, bias_term), ('dp', 'space'))]
    all_gather x2 -> x0, waiting for transfers between devices: 37.1 us -> none  [the longest x1 37.1 us: on_device(): lax.all_gather(mode_back, 'dp', axis=1, tiled=True)]
    pallas_call x0 -> x8, Pallas kernels: none -> 27.7 us  [the longest x1 7.8 us: outer_call(): pl.pallas_call(outer_kernel, grid=(held, modes // block), in_specs=[pl.Bl...]
    add x3 -> x2, other arithmetic: 19.2 us -> 0.02 us  [the longest x1 0.02 us: on_device(): ky_index = (space_index + shift) % space_count * ky_local + inner // 2]
  transfers between devices with their start and end apart: 7 -> 11, of which waited for: 6 -> 7; matrix products, arithmetic and copies ran while one was open for 10% -> 2% of each run, Pallas kernels for 0% -> 10%
where the time goes in v1:
time: 124 us; the launch traced here: 123 us
  blocking collectives  40 us (32%)
  Pallas kernels  27.7 us (22%)
  starting transfers between devices  25.1 us (20%)
  waiting for transfers between devices  15.5 us (12%)
  local copies, waits for them, and re-layouts  11.7 us (9%)
  other arithmetic  2.01 us (2%)
    all_to_all x1, blocking collectives, on_device(): lax.all_to_all(stacked.reshape(device_count, share, channels), ('dp', 'sp...  15.7 us
    all_to_all x1, blocking collectives, exchange(): lax.all_to_all(values, 'dp', split_axis=0, concat_axis=0, tiled=True, axi...  14 us
    ppermute x6, starting transfers between devices, gathered(): lax.ppermute(parts[mirror * space_count + shift], ('dp', 'space'), pairs(...  11.9 us
    ppermute x6, waiting for transfers between devices, gathered(): lax.ppermute(parts[mirror * space_count + shift], ('dp', 'space'), pairs(...  11.8 us
    unnamed x18, local copies, waits for them, and re-layouts  10.4 us
    all_to_all x1, blocking collectives, on_device(): totals = lax.all_to_all(spread, ('dp', 'space'), 0, 0, tiled=True)  10.3 us
    pallas_call x1, Pallas kernels, outer_call(): pl.pallas_call(outer_kernel, grid=(held, modes // block), in_specs=[pl.Bl...  7.8 us
    all_to_all x2, starting transfers between devices, exchange(): lax.all_to_all(values, 'dp', split_axis=0, concat_axis=0, tiled=True, axi...  7.21 us
  transfers between devices with their start and end apart: 11, of which 7 were waited for; matrix products, arithmetic and copies ran while one was open for 2% of the time, Pallas kernels for 10%

profile of v1, /device:TPU:0, one launch (start us, length us, event | category | flops | bytes accessed | tf_op | source)
XLA Modules:
  0.0 123.0 jit_solution(16291792453413298528)
XLA Ops:
  1.1 1.6 %copy-done.5 = bf16[1,256,32,128]{3,2,1,0:T(8,128)(2,1)S(1)} copy-done((bf16[1,256,32,128]{3,2,1,0:T(8,128)(2,1)S(1)}, bf16[1,256,32,128]{3,2,1,0:T(8,128)(2,1)}, u32[]{:S(2)}) %copy-start.5) | copy-done | bytes 2097176
  2.7 1.6 %copy-done.6 = bf16[1,256,32,128]{3,2,1,0:T(8,128)(2,1)S(1)} copy-done((bf16[1,256,32,128]{3,2,1,0:T(8,128)(2,1)S(1)}, bf16[1,256,32,128]{3,2,1,0:T(8,128)(2,1)}, u32[]{:S(2)}) %copy-start.6) | copy-done | bytes 2097176
  4.3 5.3 %delta_and_x_sums.1 = (bf16[256,32,128]{2,1,0:T(8,128)(2,1)S(1)}, bf16[80,32,128]{2,1,0:T(8,128)(2,1)S(1)}) custom-call(bf16[80,256]{1,0:T(8,128)(2,1)S(1)} %select_convert_fusion.1.table_ref, bf16[256,32,128]{2,1,0:T(8,128)(2,1)S(1)} %bitcast.11, bf16[256,32,128]{2,1,0:T(8,128)(2,1)S(1)} %bitcast.12), custom_call_target="tpu_custom_call" | custom-call | flops 167772160 | bytes 8388608 | tf_op jit(solution)/shard_map/delta_and_x_sums/pallas_call | solution.py:71
  9.7 4.0 %input_x_sums_and_local.1 = (bf16[80,32,128]{2,1,0:T(8,128)(2,1)}, f32[128,128]{1,0:T(8,128)S(1)}, f32[8,128]{1,0:T(8,128)S(1)}) custom-call(bf16[80,256]{1,0:T(8,128)(2,1)S(1)} %select_convert_fusion.1.table_ref, bf16[256,32,128]{2,1,0:T(8,128)(2,1)S(1)} %bitcast.13, bf16[256,32,128]{2,1,0:T(8,128)(2,1)S(1)} %get-tuple-element.25.delta_ref), custom_call_target="tpu_custom_call" | custom-call | flops 436207616 | bytes 4194304 | tf_op jit(solution)/shard_map/input_x_sums_and_local/pallas_call | solution.py:117
  13.8 15.7 %all_to_all.25 = f32[32,5,128]{2,1,0:T(8,128)S(1)} all-to-all(f32[32,5,128]{2,1,0:T(8,128)S(1)} %reshape.200), channel_id=1, replica_groups=mesh['dp'=16,'space'=2] {'dp','space'}, dimensions={0} | all-to-all | bytes 163840 | tf_op jit(solution)/shard_map/all_to_all | solution.py:487
  29.6 10.3 %all_to_all.26 = f32[32,5,128]{2,1,0:T(8,128)S(1)} all-to-all(f32[32,5,128]{2,1,0:T(8,128)S(1)} %broadcast_in_dim.76), channel_id=1, replica_groups=mesh['dp'=16,'space'=2] {'dp','space'}, dimensions={0} | all-to-all | bytes 163840 | tf_op jit(solution)/shard_map/all_to_all | solution.py:492
  40.0 14.0 %all_to_all.27.lines_ref = bf16[8,10,32,128]{3,2,1,0:T(8,128)(2,1)} all-to-all(bf16[8,10,32,128]{3,2,1,0:T(8,128)(2,1)S(1)} %bitcast.14), channel_id=1, replica_groups={{0,2,4,6,8,10,12,14},{16,18,20,22,24,26,28,30},{1,3,5,7,9,11,13,15},{17..., dimensions={0} | all-to-all | bytes 1310720 | tf_op jit(solution)/shard_map/all_to_all | solution.py:434
  53.9 3.5 %all-to-all-start.2 = ((bf16[8,10,32,128]{3,2,1,0:T(8,128)(2,1)}), bf16[8,10,32,128]{3,2,1,0:T(8,128)(2,1)S(1)}, u32[]{:S(2)}, u32[]{:S(2)}) async-start(bf16[8,10,32,128]{3,2,1,0:T(8,128)(2,1)} %bitcast.6), calls=%async_computation.2 | async-start | bytes 1310720 | tf_op jit(solution)/shard_map/all_to_all | solution.py:434
  57.5 1.4 %select_convert_fusion = (bf16[256,256]{1,0:T(8,128)(2,1)S(1)}, bf16[256,256]{1,0:T(8,128)(2,1)S(1)}) fusion(s32[256]{0:T(256)S(1)} %get-tuple-element.37, s32[256]{0:T(256)S(1)} %get-tuple-element.36, pred[256]{0:T(512)(128)(4,1)S(1)} %fusion.12, f32[256]{0:T(256)S(1)} %compare_select_fusion.3), kind=kLoop, calls=%fused_computation.10 | loop fusion | flops 1376256 | bytes 265472 | tf_op jit(solution)/shard_map/convert
  60.5 2.6 %collective-permute-start = (bf16[4,64,128]{2,1,0:T(8,128)(2,1)S(1)}, bf16[4,64,128]{2,1,0:T(8,128)(2,1)S(1)}, u32[]{:S(2)}, u32[]{:S(2)}) collective-permute-start(bf16[4,64,128]{2,1,0:T(8,128)(2,1)S(1)} %get-tuple-element.21), channel_id=1, source_target_pairs={{0,31},{1,30},{2,29},{3,28},{4,27},{5,26},{6,25},{7,24},{8,23},{9,... | collective-permute-start | bytes 196616 | tf_op jit(solution)/shard_map/ppermute | solution.py:454
  63.1 1.7 %collective-permute-start.1 = (bf16[4,64,128]{2,1,0:T(8,128)(2,1)S(1)}, bf16[4,64,128]{2,1,0:T(8,128)(2,1)S(1)}, u32[]{:S(2)}, u32[]{:S(2)}) collective-permute-start(bf16[4,64,128]{2,1,0:T(8,128)(2,1)S(1)} %get-tuple-element.22), channel_id=1, source_target_pairs={{0,30},{1,31},{2,28},{3,29},{4,26},{5,27},{6,24},{7,25},{8,22},{9,... | collective-permute-start | bytes 196616 | tf_op jit(solution)/shard_map/ppermute | solution.py:454
  64.8 1.7 %collective-permute-start.2 = (bf16[4,64,128]{2,1,0:T(8,128)(2,1)S(1)}, bf16[4,64,128]{2,1,0:T(8,128)(2,1)S(1)}, u32[]{:S(2)}, u32[]{:S(2)}) collective-permute-start(bf16[4,64,128]{2,1,0:T(8,128)(2,1)S(1)} %get-tuple-element.23), channel_id=1, source_target_pairs={{0,1},{1,0},{2,3},{3,2},{4,5},{5,4},{6,7},{7,6},{8,9},{9,8},{10,11... | collective-permute-start | bytes 196616 | tf_op jit(solution)/shard_map/ppermute | solution.py:454
  66.5 3.1 %collective-permute-done.refs_1_ = bf16[4,64,128]{2,1,0:T(8,128)(2,1)S(1)} collective-permute-done((bf16[4,64,128]{2,1,0:T(8,128)(2,1)S(1)}, bf16[4,64,128]{2,1,0:T(8,128)(2,1)S(1)}, u32[]{:S(2)}, u32[]{:S(2)}) %collective-permute-start) | collective-permute-done | bytes 65568 | tf_op jit(solution)/shard_map/ppermute | solution.py:454
  70.7 3.4 %copy-done = bf16[4,32,2,128,128]{4,3,2,1,0:T(8,128)(2,1)S(1)} copy-done((bf16[4,32,2,128,128]{4,3,2,1,0:T(8,128)(2,1)S(1)}, bf16[4,32,2,128,128]{4,3,2,1,0:T(8,128)(2,1)}, u32[]{:S(2)}) %copy-start) | copy-done | bytes 8388632
  74.1 3.1 %mode_back.1 = (bf16[4,64,128]{2,1,0:T(8,128)(2,1)S(1)}, bf16[4,64,128]{2,1,0:T(8,128)(2,1)S(1)}) custom-call(f32[64,128]{1,0:T(8,128)S(1)} %broadcast_in_dim.72.scale_ref, bf16[4,32,2,128,128]{4,3,2,1,0:T(8,128)(2,1)S(1)} %copy-done, bf16[4,64,128]{2,1,0:T(8,128)(2,1)S(1)} %get-tuple-element.20.refs_0_, ...), custom_call_target="tpu_custom_call" | custom-call | flops 16777216 | bytes 8388608 | tf_op jit(solution)/shard_map/mode_back/pallas_call | solution.py:214
  77.2 2.6 %collective-permute-start.5 = (bf16[4,64,128]{2,1,0:T(8,128)(2,1)S(1)}, bf16[4,64,128]{2,1,0:T(8,128)(2,1)S(1)}, u32[]{:S(2)}, u32[]{:S(2)}) collective-permute-start(bf16[4,64,128]{2,1,0:T(8,128)(2,1)S(1)} %get-tuple-element.24.refs_0_), channel_id=1, source_target_pairs={{0,31},{1,30},{2,29},{3,28},{4,27},{5,26},{6,25},{7,24},{8,23},{9,... | collective-permute-start | bytes 196616 | tf_op jit(solution)/shard_map/ppermute | solution.py:469
  79.8 2.9 %collective-permute-start.4 = (bf16[4,64,128]{2,1,0:T(8,128)(2,1)S(1)}, bf16[4,64,128]{2,1,0:T(8,128)(2,1)S(1)}, u32[]{:S(2)}, u32[]{:S(2)}) collective-permute-start(bf16[4,64,128]{2,1,0:T(8,128)(2,1)S(1)} %get-tuple-element.24.refs_0_), channel_id=1, source_target_pairs={{0,30},{1,31},{2,28},{3,29},{4,26},{5,27},{6,24},{7,25},{8,22},{9,... | collective-permute-start | bytes 196616 | tf_op jit(solution)/shard_map/ppermute | solution.py:469
  83.2 1.8 %collective-permute-done.5.refs_3_ = bf16[4,64,128]{2,1,0:T(8,128)(2,1)S(1)} collective-permute-done((bf16[4,64,128]{2,1,0:T(8,128)(2,1)S(1)}, bf16[4,64,128]{2,1,0:T(8,128)(2,1)S(1)}, u32[]{:S(2)}, u32[]{:S(2)}) %collective-permute-start.5) | collective-permute-done | bytes 65568 | tf_op jit(solution)/shard_map/ppermute | solution.py:469
  89.1 3.7 %all-to-all-start.1 = ((bf16[8,10,32,128]{3,2,1,0:T(8,128)(2,1)}), bf16[8,10,32,128]{3,2,1,0:T(8,128)(2,1)S(1)}, u32[]{:S(2)}, u32[]{:S(2)}) async-start(bf16[8,10,32,128]{3,2,1,0:T(8,128)(2,1)} %copy-done.3), calls=%async_computation.1 | async-start | bytes 1310720 | tf_op jit(solution)/shard_map/all_to_all | solution.py:434
  94.3 4.0 %collective-permute-start.6 = (bf16[4,64,128]{2,1,0:T(8,128)(2,1)S(1)}, bf16[4,64,128]{2,1,0:T(8,128)(2,1)S(1)}, u32[]{:S(2)}, u32[]{:S(2)}) collective-permute-start(bf16[4,64,128]{2,1,0:T(8,128)(2,1)S(1)} %get-tuple-element.29), channel_id=1, source_target_pairs={{0,31},{1,30},{2,29},{3,28},{4,27},{5,26},{6,25},{7,24},{8,23},{9,... | collective-permute-start | bytes 196616 | tf_op jit(solution)/shard_map/ppermute | solution.py:454
  101.5 4.9 %collective-permute-done.6.refs_1_ = bf16[4,64,128]{2,1,0:T(8,128)(2,1)S(1)} collective-permute-done((bf16[4,64,128]{2,1,0:T(8,128)(2,1)S(1)}, bf16[4,64,128]{2,1,0:T(8,128)(2,1)S(1)}, u32[]{:S(2)}, u32[]{:S(2)}) %collective-permute-start.6) | collective-permute-done | bytes 65568 | tf_op jit(solution)/shard_map/ppermute | solution.py:454
  106.4 2.7 %collective-permute-done.7.refs_2_ = bf16[4,64,128]{2,1,0:T(8,128)(2,1)S(1)} collective-permute-done((bf16[4,64,128]{2,1,0:T(8,128)(2,1)S(1)}, bf16[4,64,128]{2,1,0:T(8,128)(2,1)S(1)}, u32[]{:S(2)}, u32[]{:S(2)}) %collective-permute-start.7) | collective-permute-done | bytes 65568 | tf_op jit(solution)/shard_map/ppermute | solution.py:454
  109.1 7.8 %grad_spectral.1 = bf16[4,32,2,128,128]{4,3,2,1,0:T(8,128)(2,1)} custom-call(f32[64,128]{1,0:T(8,128)S(1)} %broadcast_in_dim.72.scale_ref, bf16[4,64,128]{2,1,0:T(8,128)(2,1)S(1)} %get-tuple-element.26.delta_ref, bf16[4,64,128]{2,1,0:T(8,128)(2,1)S(1)} %get-tuple-element.28.refs_0_, bf16[4,64,128]{2,1,0:T(8,128)(2,1)S(1)} %collective-permute-done.6.refs_1_, ...), custom_call_target="tpu_custom_call" | custom-call | flops 12582912 | bytes 8388608 | tf_op jit(solution)/shard_map/grad_spectral/pallas_call | solution.py:257
  116.9 6.1 %x_inverse_and_local.1 = bf16[256,32,128]{2,1,0:T(8,128)(2,1)} custom-call(bf16[80,256]{1,0:T(8,128)(2,1)S(1)} %select_convert_fusion.1.table_ref, bf16[80,32,128]{2,1,0:T(8,128)(2,1)S(1)} %bitcast.10, bf16[256,32,128]{2,1,0:T(8,128)(2,1)S(1)} %get-tuple-element.25.delta_ref, bf16[128,128]{1,0:T(8,128)(2,1)S(1)} %copy-done.8), custom_call_target="tpu_custom_call" | custom-call | flops 436207616 | bytes 5242880 | tf_op jit(solution)/shard_map/x_inverse_and_local/pallas_call | solution.py:362
  (48 shorter events, 12.8 us)
Async XLA Ops:
  1.1 1.6 %copy-start.5 = (bf16[1,256,32,128]{3,2,1,0:T(8,128)(2,1)S(1)}, bf16[1,256,32,128]{3,2,1,0:T(8,128)(2,1)}, u32[]{:S(2)}) copy-start(bf16[1,256,32,128]{3,2,1,0:T(8,128)(2,1)} %param.6) | copy-start | bytes 6291460
  2.7 1.6 %copy-start.6 = (bf16[1,256,32,128]{3,2,1,0:T(8,128)(2,1)S(1)}, bf16[1,256,32,128]{3,2,1,0:T(8,128)(2,1)}, u32[]{:S(2)}) copy-start(bf16[1,256,32,128]{3,2,1,0:T(8,128)(2,1)} %param.7) | copy-start | bytes 6291460
  4.3 5.4 %copy-start.7 = (bf16[1,256,32,128]{3,2,1,0:T(8,128)(2,1)S(1)}, bf16[1,256,32,128]{3,2,1,0:T(8,128)(2,1)}, u32[]{:S(2)}) copy-start(bf16[1,256,32,128]{3,2,1,0:T(8,128)(2,1)} %param.5) | copy-start | bytes 6291460
  53.9 34.3 %all-to-all-start.2 = ((bf16[8,10,32,128]{3,2,1,0:T(8,128)(2,1)}), bf16[8,10,32,128]{3,2,1,0:T(8,128)(2,1)S(1)}, u32[]{:S(2)}, u32[]{:S(2)}) async-start(bf16[8,10,32,128]{3,2,1,0:T(8,128)(2,1)} %bitcast.6), calls=%async_computation.2 | async-start | bytes 1310720 | tf_op jit(solution)/shard_map/all_to_all | solution.py:434
  58.9 1.1 copy-start.4
  60.5 9.1 %collective-permute-start = (bf16[4,64,128]{2,1,0:T(8,128)(2,1)S(1)}, bf16[4,64,128]{2,1,0:T(8,128)(2,1)S(1)}, u32[]{:S(2)}, u32[]{:S(2)}) collective-permute-start(bf16[4,64,128]{2,1,0:T(8,128)(2,1)S(1)} %get-tuple-element.21), channel_id=1, source_target_pairs={{0,31},{1,30},{2,29},{3,28},{4,27},{5,26},{6,25},{7,24},{8,23},{9,... | collective-permute-start | bytes 196616 | tf_op jit(solution)/shard_map/ppermute | solution.py:454
  63.1 7.5 %collective-permute-start.1 = (bf16[4,64,128]{2,1,0:T(8,128)(2,1)S(1)}, bf16[4,64,128]{2,1,0:T(8,128)(2,1)S(1)}, u32[]{:S(2)}, u32[]{:S(2)}) collective-permute-start(bf16[4,64,128]{2,1,0:T(8,128)(2,1)S(1)} %get-tuple-element.22), channel_id=1, source_target_pairs={{0,30},{1,31},{2,28},{3,29},{4,26},{5,27},{6,24},{7,25},{8,22},{9,... | collective-permute-start | bytes 196616 | tf_op jit(solution)/shard_map/ppermute | solution.py:454
  64.8 5.8 %collective-permute-start.2 = (bf16[4,64,128]{2,1,0:T(8,128)(2,1)S(1)}, bf16[4,64,128]{2,1,0:T(8,128)(2,1)S(1)}, u32[]{:S(2)}, u32[]{:S(2)}) collective-permute-start(bf16[4,64,128]{2,1,0:T(8,128)(2,1)S(1)} %get-tuple-element.23), channel_id=1, source_target_pairs={{0,1},{1,0},{2,3},{3,2},{4,5},{5,4},{6,7},{7,6},{8,9},{9,8},{10,11... | collective-permute-start | bytes 196616 | tf_op jit(solution)/shard_map/ppermute | solution.py:454
  70.7 3.4 %copy-start = (bf16[4,32,2,128,128]{4,3,2,1,0:T(8,128)(2,1)S(1)}, bf16[4,32,2,128,128]{4,3,2,1,0:T(8,128)(2,1)}, u32[]{:S(2)}) copy-start(bf16[4,32,2,128,128]{4,3,2,1,0:T(8,128)(2,1)} %weight_ref.1) | copy-start | bytes 25165828
  77.2 7.7 %collective-permute-start.5 = (bf16[4,64,128]{2,1,0:T(8,128)(2,1)S(1)}, bf16[4,64,128]{2,1,0:T(8,128)(2,1)S(1)}, u32[]{:S(2)}, u32[]{:S(2)}) collective-permute-start(bf16[4,64,128]{2,1,0:T(8,128)(2,1)S(1)} %get-tuple-element.24.refs_0_), channel_id=1, source_target_pairs={{0,31},{1,30},{2,29},{3,28},{4,27},{5,26},{6,25},{7,24},{8,23},{9,... | collective-permute-start | bytes 196616 | tf_op jit(solution)/shard_map/ppermute | solution.py:469
  79.8 6.4 %collective-permute-start.4 = (bf16[4,64,128]{2,1,0:T(8,128)(2,1)S(1)}, bf16[4,64,128]{2,1,0:T(8,128)(2,1)S(1)}, u32[]{:S(2)}, u32[]{:S(2)}) collective-permute-start(bf16[4,64,128]{2,1,0:T(8,128)(2,1)S(1)} %get-tuple-element.24.refs_0_), channel_id=1, source_target_pairs={{0,30},{1,31},{2,28},{3,29},{4,26},{5,27},{6,24},{7,25},{8,22},{9,... | collective-permute-start | bytes 196616 | tf_op jit(solution)/shard_map/ppermute | solution.py:469
  82.7 4.3 %collective-permute-start.3 = (bf16[4,64,128]{2,1,0:T(8,128)(2,1)S(1)}, bf16[4,64,128]{2,1,0:T(8,128)(2,1)S(1)}, u32[]{:S(2)}, u32[]{:S(2)}) collective-permute-start(bf16[4,64,128]{2,1,0:T(8,128)(2,1)S(1)} %get-tuple-element.24.refs_0_), channel_id=1, source_target_pairs={{0,1},{1,0},{2,3},{3,2},{4,5},{5,4},{6,7},{7,6},{8,9},{9,8},{10,11... | collective-permute-start | bytes 196616 | tf_op jit(solution)/shard_map/ppermute | solution.py:469
  87.4 0.8 copy-start.3
  88.2 0.8 copy-start.1
  89.1 27.8 %all-to-all-start.1 = ((bf16[8,10,32,128]{3,2,1,0:T(8,128)(2,1)}), bf16[8,10,32,128]{3,2,1,0:T(8,128)(2,1)S(1)}, u32[]{:S(2)}, u32[]{:S(2)}) async-start(bf16[8,10,32,128]{3,2,1,0:T(8,128)(2,1)} %copy-done.3), calls=%async_computation.1 | async-start | bytes 1310720 | tf_op jit(solution)/shard_map/all_to_all | solution.py:434
  92.8 1.1 copy-start.2
  94.3 12.1 %collective-permute-start.6 = (bf16[4,64,128]{2,1,0:T(8,128)(2,1)S(1)}, bf16[4,64,128]{2,1,0:T(8,128)(2,1)S(1)}, u32[]{:S(2)}, u32[]{:S(2)}) collective-permute-start(bf16[4,64,128]{2,1,0:T(8,128)(2,1)S(1)} %get-tuple-element.29), channel_id=1, source_target_pairs={{0,31},{1,30},{2,29},{3,28},{4,27},{5,26},{6,25},{7,24},{8,23},{9,... | collective-permute-start | bytes 196616 | tf_op jit(solution)/shard_map/ppermute | solution.py:454
  98.3 10.8 %collective-permute-start.7 = (bf16[4,64,128]{2,1,0:T(8,128)(2,1)S(1)}, bf16[4,64,128]{2,1,0:T(8,128)(2,1)S(1)}, u32[]{:S(2)}, u32[]{:S(2)}) collective-permute-start(bf16[4,64,128]{2,1,0:T(8,128)(2,1)S(1)} %get-tuple-element.30), channel_id=1, source_target_pairs={{0,30},{1,31},{2,28},{3,29},{4,26},{5,27},{6,24},{7,25},{8,22},{9,... | collective-permute-start | bytes 196616 | tf_op jit(solution)/shard_map/ppermute | solution.py:454
  99.5 9.6 %collective-permute-start.8 = (bf16[4,64,128]{2,1,0:T(8,128)(2,1)S(1)}, bf16[4,64,128]{2,1,0:T(8,128)(2,1)S(1)}, u32[]{:S(2)}, u32[]{:S(2)}) collective-permute-start(bf16[4,64,128]{2,1,0:T(8,128)(2,1)S(1)} %get-tuple-element.31), channel_id=1, source_target_pairs={{0,1},{1,0},{2,3},{3,2},{4,5},{5,4},{6,7},{7,6},{8,9},{9,8},{10,11... | collective-permute-start | bytes 196616 | tf_op jit(solution)/shard_map/ppermute | solution.py:454
  109.1 7.8 %copy-start.8 = (bf16[128,128]{1,0:T(8,128)(2,1)S(1)}, bf16[128,128]{1,0:T(8,128)(2,1)}, u32[]{:S(2)}) copy-start(bf16[128,128]{1,0:T(8,128)(2,1)} %local_ref.1) | copy-start | bytes 98308

commit v2 on v1

v2 whole, which is shorter than its diff:
```python
import functools
import math

import jax
import jax.numpy as jnp
from jax import lax
from jax.experimental import pallas as pl
from jax.experimental.pallas import tpu as pltpu
from jax.sharding import PartitionSpec as P

root_two_pi = 0.7978845608028654
cubic_coef = 0.044715
f32 = jnp.float32
bf16 = jnp.bfloat16
mebi = 1024 * 1024


def gelu_slope(values):
    square = values * values
    cubic = root_two_pi * cubic_coef
    tangent = jnp.tanh(values * (root_two_pi + cubic * square))
    inner = values * (1.0 - tangent * tangent)
    return 0.5 * ((1.0 + tangent) + inner * (root_two_pi + (3.0 * cubic) * square))


def cosine_table(phases, period):
    quarter = period // 4
    if period & (period - 1) == 0:
        turns = (phases + quarter // 2) >> (quarter.bit_length() - 1)
    else:
        turns = (phases + quarter // 2) // quarter
    angle = (phases - turns * quarter).astype(f32) * (2.0 * math.pi / period)
    square = angle * angle
    cosine = 1.0 + square * (
        -0.5 + square * (1.0 / 24.0 + square * (-1.0 / 720.0 + square * (1.0 / 40320.0)))
    )
    sine = angle * (
        1.0
        + square
        * (-1.0 / 6.0 + square * (1.0 / 120.0 + square * (-1.0 / 5040.0 + square * (1.0 / 362880.0))))
    )
    turns = turns & 3
    magnitude = jnp.where((turns & 1) == 0, cosine, sine)
    return jnp.where((turns == 1) | (turns == 2), -magnitude, magnitude).astype(bf16)


def params(mebibytes=16):
    return pltpu.CompilerParams(vmem_limit_bytes=mebibytes * mebi)


def whole(shape):
    return pl.BlockSpec(shape, lambda *_: (0,) * len(shape))


def matrix_per_column(table, columns_of):
    channels = columns_of[0].shape[1]
    results = []
    for y in range(0, len(columns_of), 2):
        pair = jnp.concatenate(columns_of[y : y + 2], axis=1)
        sums = jnp.dot(table, pair, preferred_element_type=f32).astype(bf16)
        results += [sums[:, :channels], sums[:, channels:]]
    return jnp.swapaxes(jnp.stack(results, axis=0), 0, 1)


def two_terms(values):
    high = values.astype(bf16)
    return high, (values - high.astype(f32)).astype(bf16)


def extra_rows(channels, half):
    return -(-(2 * (channels // half) + 2) // 8) * 8


def pack_share(share, bias):
    rows, channels = share.shape
    filler = extra_rows(channels, channels // rows) - 2 * rows - 2
    parts = list(two_terms(share) + two_terms(bias))
    if filler:
        parts.append(jnp.zeros((filler, channels), bf16))
    return jnp.concatenate([part.astype(f32) for part in parts], axis=0).astype(bf16)


def unpack_share(rows, message):
    message = message.astype(f32)
    share = message[:rows] + message[rows : 2 * rows]
    bias = message[2 * rows : 2 * rows + 1] + message[2 * rows + 1 : 2 * rows + 2]
    return share, bias


def delta_kernel(
    table_ref, upper_ref, pre_ref, cot_ref, field_ref, delta_ref, out_ref, lines, local, bias
):
    grid_rows, columns, channels = pre_ref.shape
    half = out_ref.shape[0]
    block = pl.program_id(0)
    all_columns = columns * pl.num_programs(0)
    step = 16

    @pl.when(block == 0)
    def _():
        local[...] = jnp.zeros_like(local)
        bias[...] = jnp.zeros_like(bias)

    def slab(i, carry):
        rows = pl.ds(pl.multiple_of(i * step, step), step)
        slope = gelu_slope(pre_ref[rows].astype(f32))
        delta = (cot_ref[rows].astype(f32) * slope).astype(bf16)
        delta_ref[rows] = delta
        lines[:, rows, :] = jnp.swapaxes(delta, 0, 1)
        bias[...] += jnp.sum(delta.astype(f32).reshape(-1, 8, channels), axis=0)
        return carry

    lax.fori_loop(0, grid_rows // step, slab, 0, unroll=2)
    local[...] += lax.dot_general(
        field_ref[...].reshape(grid_rows * columns, channels),
        delta_ref[...].reshape(grid_rows * columns, channels),
        (((0,), (0,)), ((), ())),
        preferred_element_type=f32,
    )
    sums = matrix_per_column(table_ref[...], [lines[y] for y in range(columns)])
    per_target = sums.shape[0] // half
    first = pl.multiple_of(block * columns, columns)
    for target in range(half):
        for row in range(per_target):
            out_ref[target, pl.ds(row * all_columns + first, columns), :] = sums[
                target * per_target + row
            ]

    @pl.when(block == pl.num_programs(0) - 1)
    def _():
        upper = upper_ref[:1] > 0.0
        share = channels // half
        total = jnp.sum(bias[...], axis=0, keepdims=True)
        for target in range(half):
            mine = local[target * share : (target + 1) * share]
            mirrored = local[(half - 1 - target) * share : (half - target) * share]
            rows = pack_share(jnp.where(upper, mirrored, mine), total)
            out_ref[target, per_target * all_columns :] = rows


def delta_call(table, upper, pre_act, cotangent, field_in, half):
    grid_rows, columns, channels = pre_act.shape
    rows = table.shape[0]
    block = min(16, columns)
    field = pl.BlockSpec((grid_rows, block, channels), lambda i: (0, i, 0))
    message = (half, rows // half * columns + extra_rows(channels, half), channels)
    return pl.pallas_call(
        delta_kernel,
        grid=(columns // block,),
        in_specs=[whole(table.shape), whole(upper.shape), field, field, field],
        out_specs=[field, whole(message)],
        out_shape=[
            jax.ShapeDtypeStruct(pre_act.shape, bf16),
            jax.ShapeDtypeStruct(message, bf16),
        ],
        scratch_shapes=[
            pltpu.VMEM((block, grid_rows, channels), bf16),
            pltpu.VMEM((channels, channels), f32),
            pltpu.VMEM((8, channels), f32),
        ],
        compiler_params=params(60),
        cost_estimate=pl.CostEstimate(
            flops=4 * rows * pre_act.size, bytes_accessed=8 * pre_act.size, transcendentals=pre_act.size
        ),
        name="delta_and_x_sums",
    )(table, upper, pre_act, cotangent, field_in)


def input_kernel(table_ref, field_ref, out_ref):
    lines = jnp.swapaxes(field_ref[...], 0, 1)
    out_ref[...] = matrix_per_column(
        table_ref[...], [lines[y] for y in range(field_ref.shape[1])]
    )


def input_call(table, field_in):
    grid_rows, columns, channels = field_in.shape
    rows = table.shape[0]
    block = min(16, columns)
    return pl.pallas_call(
        input_kernel,
        grid=(columns // block,),
        in_specs=[
            whole(table.shape),
            pl.BlockSpec((grid_rows, block, channels), lambda i: (0, i, 0)),
        ],
        out_specs=pl.BlockSpec((rows, block, channels), lambda i: (0, i, 0)),
        out_shape=jax.ShapeDtypeStruct((rows, columns, channels), bf16),
        compiler_params=params(60),
        cost_estimate=pl.CostEstimate(
            flops=2 * rows * field_in.size, bytes_accessed=4 * field_in.size, transcendentals=0
        ),
        name="input_x_sums",
    )(table, field_in)


def y_transform_kernel(columns, extra, blocks, table_ref, lines_ref, *out_refs):
    sources, total_rows, channels = lines_ref.shape
    frequencies = (total_rows - extra) // columns // 2
    own = blocks // 2
    size = table_ref.shape[0] // blocks
    table = table_ref[...]
    for t in range(frequencies):
        lines = jnp.concatenate(
            [
                lines_ref[:, row * columns : (row + 1) * columns].reshape(
                    sources * columns, channels
                )
                for row in (2 * t, 2 * t + 1)
            ],
            axis=0,
        )
        sums = jnp.dot(table, lines, preferred_element_type=f32).astype(bf16)
        for block in range(blocks):
            held = t if block < own else frequencies - 1 - t
            if 0 <= held < frequencies - 1:
                first = (block // len(out_refs)) * (frequencies - 1) + held
                out_refs[block % len(out_refs)][first * size : (first + 1) * size] = sums[
                    block * size : (block + 1) * size
                ]
    if extra:
        rows = channels // sources
        pieces = [unpack_share(rows, lines_ref[i, total_rows - extra :]) for i in range(sources)]
        packed = pack_share(sum(p[0] for p in pieces), sum(p[1] for p in pieces))
        for out_ref in out_refs:
            out_ref[(frequencies - 1) * size :] = packed


def y_transform_call(table, lines, blocks, outputs, columns, extra):
    sources, total_rows, channels = lines.shape
    held = (total_rows - extra) // columns // 2 - 1
    size = table.shape[0] // blocks
    return pl.pallas_call(
        functools.partial(y_transform_kernel, columns, extra, blocks),
        out_shape=[
            jax.ShapeDtypeStruct((blocks // outputs * held * size + extra, channels), bf16)
        ]
        * outputs,
        compiler_params=params(),
        cost_estimate=pl.CostEstimate(
            flops=2 * (held + 1) * table.size * channels, bytes_accessed=4 * lines.size, transcendentals=0
        ),
        name="y_sums",
    )(table, lines)


def turned(values):
    rows = values.shape[0]
    even = lax.broadcasted_iota(jnp.int32, values.shape, 0) % 2 == 0
    up = pltpu.roll(values, rows - 1, 0)
    down = pltpu.roll(values, 1, 0)
    return jnp.concatenate([values, jnp.where(even, up, -down)], axis=1)


def load_kernel(source_ref, target_ref, semaphores):
    copies = [
        pltpu.make_async_copy(source_ref.at[j, k], target_ref.at[j, k], semaphores.at[j, k])
        for j in range(source_ref.shape[0])
        for k in range(source_ref.shape[1])
    ]
    for copy in copies:
        copy.start()
    for copy in copies:
        copy.wait()


def load_call(weight):
    held, modes, _, channels, _ = weight.shape
    parts = weight.reshape(held, 2, modes // 2, 2, channels, channels)
    loaded = pl.pallas_call(
        load_kernel,
        in_specs=[pl.BlockSpec(memory_space=pl.ANY)],
        out_specs=pl.BlockSpec(memory_space=pl.ANY),
        out_shape=pltpu.VMEM(parts.shape, bf16),
        scratch_shapes=[pltpu.SemaphoreType.DMA((held, 2))],
        compiler_params=params(50),
        cost_estimate=pl.CostEstimate(flops=0, bytes_accessed=4 * weight.size, transcendentals=0),
        name="weights_to_vmem",
    )(parts)
    return loaded.reshape(weight.shape)


def back_kernel(share, scale_ref, weight_ref, *refs):
    part_refs, (back_ref, delta_ref, share_ref) = refs[:-3], refs[-3:]
    held, rows, channels = delta_ref.shape
    block = weight_ref.shape[1]
    j, k = pl.program_id(0), pl.program_id(1)
    first = pl.multiple_of((j * (rows // (2 * block)) + k) * 2 * block, 2 * block)
    here = pl.ds(first, 2 * block)
    inner = pl.ds(pl.multiple_of(k * 2 * block, 2 * block), 2 * block)
    total = part_refs[0][here].astype(f32)
    for ref in part_refs[1:]:
        total = total + ref[here].astype(f32)
    delta = total.astype(bf16)
    delta_ref[j, inner] = delta
    both = turned(delta.astype(f32)).astype(bf16)
    sums = []
    for mode in range(block):
        weight = jnp.concatenate([weight_ref[0, mode, 0], weight_ref[0, mode, 1]], axis=1)
        sums.append(
            lax.dot_general(
                both[2 * mode : 2 * mode + 2],
                weight,
                (((1,), (1,)), ((), ())),
                preferred_element_type=f32,
            )
        )
    back_ref[j, inner] = (jnp.concatenate(sums, axis=0) * scale_ref[inner]).astype(bf16)

    @pl.when((j == 0) & (k == 0))
    def _():
        pieces = [unpack_share(share, ref[held * rows :]) for ref in part_refs]
        share_ref[...] = pack_share(sum(p[0] for p in pieces), sum(p[1] for p in pieces))


def back_call(scale_rows, weight, parts, share):
    held, modes, _, channels, _ = weight.shape
    block = min(16, modes)
    shape = (held, 2 * modes, channels)
    extra = (parts[0].shape[0] - held * 2 * modes, channels)
    return pl.pallas_call(
        functools.partial(back_kernel, share),
        grid=(held, modes // block),
        in_specs=[
            whole(scale_rows.shape),
            pl.BlockSpec((1, block, 2, channels, channels), lambda j, k: (j, k, 0, 0, 0)),
        ]
        + [whole(part.shape) for part in parts],
        out_specs=[whole(shape), whole(shape), whole(extra)],
        out_shape=[
            jax.ShapeDtypeStruct(shape, bf16),
            jax.ShapeDtypeStruct(shape, bf16),
            jax.ShapeDtypeStruct(extra, bf16),
        ],
        compiler_params=params(),
        cost_estimate=pl.CostEstimate(
            flops=4 * weight.size, bytes_accessed=2 * weight.size, transcendentals=0
        ),
        name="mode_back",
    )(scale_rows, weight, *parts)


def outer_kernel(scale_ref, delta_ref, *refs):
    part_refs, out_ref = refs[:-1], refs[-1]
    modes = out_ref.shape[1]
    channels = out_ref.shape[-1]
    total = part_refs[0][...].astype(f32)
    for ref in part_refs[1:]:
        total = total + ref[...].astype(f32)
    field = (total.astype(bf16).astype(f32) * scale_ref[...]).astype(bf16).astype(f32)
    delta = turned(delta_ref[0].astype(f32))
    group = 4
    mode_of_row = lax.broadcasted_iota(jnp.int32, (2 * group, 2 * channels), 0) // 2
    for first in range(0, modes, group):
        rows = slice(2 * first, 2 * (first + group))
        alone = [jnp.where(mode_of_row == i, delta[rows], 0.0) for i in range(group)]
        product = lax.dot_general(
            field[rows].astype(bf16),
            jnp.concatenate(alone, axis=1).astype(bf16),
            (((0,), (0,)), ((), ())),
            preferred_element_type=f32,
        ).astype(bf16)
        for i in range(2 * group):
            out_ref[0, first + i // 2, i % 2] = product[:, i * channels : (i + 1) * channels]


def outer_call(scale_rows, delta, parts):
    held, rows, channels = delta.shape
    modes = rows // 2
    part = pl.BlockSpec((1, rows, channels), lambda j: (j, 0, 0))
    return pl.pallas_call(
        outer_kernel,
        grid=(held,),
        in_specs=[whole((rows, channels)), part]
        + [pl.BlockSpec((rows, channels), lambda j: (j, 0))] * len(parts),
        out_specs=pl.BlockSpec((1, modes, 2, channels, channels), lambda j: (j, 0, 0, 0, 0)),
        out_shape=jax.ShapeDtypeStruct((held, modes, 2, channels, channels), bf16),
        compiler_params=params(),
        cost_estimate=pl.CostEstimate(
            flops=6 * held * modes * channels * channels,
            bytes_accessed=4 * held * modes * channels * channels,
            transcendentals=0,
        ),
        name="grad_spectral",
    )(scale_rows, delta, *parts)


def y_inverse_kernel(columns, table_ref, share_ref, *refs):
    part_refs, out_ref = refs[:-1], refs[-1]
    targets, total_rows, channels = out_ref.shape
    extra = share_ref.shape[0]
    frequencies = (total_rows - extra) // columns // 2
    own = len(part_refs) // 2
    size = part_refs[0].shape[1]
    table = table_ref[...]
    for t in range(frequencies):
        first = 0 if t < frequencies - 1 else own
        last = 2 * own if t > 0 else own
        modes = jnp.concatenate(
            [
                part_refs[block][t if block < own else frequencies - 1 - t]
                for block in range(first, last)
            ],
            axis=0,
        )
        sums = lax.dot_general(
            table[first * size : last * size],
            modes,
            (((0,), (0,)), ((), ())),
            preferred_element_type=f32,
        ).astype(bf16)
        for part in range(2):
            row = 2 * t + part
            out_ref[:, row * columns : (row + 1) * columns] = sums[
                part * targets * columns : (part + 1) * targets * columns
            ].reshape(targets, columns, channels)
    for target in range(targets):
        out_ref[target, total_rows - extra :] = share_ref[...]


def y_inverse_call(table, share, parts, targets, columns):
    held, size, channels = parts[0].shape
    rows = 2 * (held + 1)
    return pl.pallas_call(
        functools.partial(y_inverse_kernel, columns),
        out_shape=jax.ShapeDtypeStruct(
            (targets, rows * columns + share.shape[0], channels), bf16
        ),
        compiler_params=params(),
        cost_estimate=pl.CostEstimate(
            flops=rows * table.size * channels,
            bytes_accessed=4 * targets * rows * columns * channels,
            transcendentals=0,
        ),
        name="y_inverse",
    )(table, share, *parts)


def final_kernel(
    table_ref, upper_ref, lines_ref, delta_ref, weight_ref, out_ref, local_ref, bias_ref
):
    grid_rows, columns, channels = out_ref.shape
    half = lines_ref.shape[0]
    block = pl.program_id(0)
    all_columns = columns * pl.num_programs(0)
    per_source = table_ref.shape[0] // half
    first = pl.multiple_of(block * columns, columns)
    lines = jnp.stack(
        [
            lines_ref[source, pl.ds(row * all_columns + first, columns), :]
            for source in range(half)
            for row in range(per_source)
        ],
        axis=0,
    )
    lines = jnp.swapaxes(lines, 0, 1)
    spectral = matrix_per_column(table_ref[...].T, [lines[y] for y in range(columns)])
    local = lax.dot_general(
        delta_ref[...].reshape(grid_rows * columns, channels),
        weight_ref[...],
        (((1,), (1,)), ((), ())),
        preferred_element_type=f32,
    ).reshape(grid_rows, columns, channels)
    out_ref[...] = (spectral.astype(f32) + local).astype(bf16)

    @pl.when(block == 0)
    def _():
        upper = upper_ref[:1] > 0.0
        share = channels // half
        pieces = [
            unpack_share(share, lines_ref[source, per_source * all_columns :])
            for source in range(half)
        ]
        for source in range(half):
            local_ref[source * share : (source + 1) * share] = jnp.where(
                upper, pieces[half - 1 - source][0], pieces[source][0]
            )
        bias_ref[...] = pieces[0][1]


def final_call(table, upper, lines, delta, local_weight):
    grid_rows, columns, channels = delta.shape
    block = min(16, columns)
    field = pl.BlockSpec((grid_rows, block, channels), lambda i: (0, i, 0))
    return pl.pallas_call(
        final_kernel,
        grid=(columns // block,),
        in_specs=[
            whole(table.shape),
            whole(upper.shape),
            whole(lines.shape),
            field,
            whole(local_weight.shape),
        ],
        out_specs=[field, whole((channels, channels)), whole((1, channels))],
        out_shape=[
            jax.ShapeDtypeStruct(delta.shape, bf16),
            jax.ShapeDtypeStruct((channels, channels), f32),
            jax.ShapeDtypeStruct((1, channels), f32),
        ],
        compiler_params=params(),
        cost_estimate=pl.CostEstimate(
            flops=2 * (table.shape[0] + channels) * delta.size,
            bytes_accessed=5 * delta.size,
            transcendentals=0,
        ),
        name="x_inverse_and_local",
    )(table, upper, lines, delta, local_weight)


def on_device(field_in, pre_act, cotangent, spec_weight, local_weight):
    batch_size, slab_rows, col_block, channels = field_in.shape
    space_count = lax.axis_size("space")
    data_count = lax.axis_size("dp")
    grid_rows = slab_rows * space_count
    grid_cols = col_block * data_count
    kx_local, ky_local = spec_weight.shape[:2]
    half = data_count // 2
    half_cols = half * col_block
    row_count = 2 * (kx_local + 1)
    data_index = lax.axis_index("dp")
    space_index = lax.axis_index("space")
    upper = data_index // half

    row = jnp.arange(half * row_count, dtype=jnp.int32)
    member, inner = row // row_count, row % row_count
    t = inner // 2
    frequency = jnp.where(
        upper == 0, kx_local * member + t, kx_local * (half - 1 - member) + kx_local - t
    )
    positions = space_index * slab_rows + jnp.arange(slab_rows, dtype=jnp.int32)
    quarter = grid_rows // 4
    x_table = cosine_table(
        frequency[:, None] * positions[None, :] - (inner % 2 * quarter)[:, None], grid_rows
    )

    blocks = 2 * space_count
    size = 2 * ky_local
    row = jnp.arange(blocks * size, dtype=jnp.int32)
    block, inner = row // size, row % size
    shift = block % space_count
    ky_index = (space_index + shift) % space_count * ky_local + inner // 2
    positions = upper * half_cols + jnp.arange(half_cols, dtype=jnp.int32)
    quarter = grid_cols // 4
    cosine_turn = inner % 2
    sine_turn = jnp.where((block // space_count) == upper, 1 + inner % 2, 3 * (1 - inner % 2))
    turn = jnp.concatenate(
        [
            jnp.broadcast_to(cosine_turn[:, None], (blocks * size, half_cols)),
            jnp.broadcast_to(sine_turn[:, None], (blocks * size, half_cols)),
        ],
        axis=1,
    )
    positions = jnp.concatenate([positions, positions])
    y_table = cosine_table(ky_index[:, None] * positions[None, :] + quarter * turn, grid_cols)

    ky_row = space_index * ky_local + jnp.arange(size, dtype=jnp.int32) // 2
    scale = jnp.where(ky_row == 0, 1.0, 2.0).astype(f32) / (grid_rows * grid_cols)
    scale_rows = jnp.broadcast_to(scale[:, None], (size, channels))

    halves = [list(range(half)), list(range(half, data_count))]

    def exchange(values):
        return lax.all_to_all(
            values, "dp", split_axis=0, concat_axis=0, tiled=True, axis_index_groups=halves
        )

    def pairs(mirror, shift):
        moves = []
        for d in range(data_count):
            for s in range(space_count):
                target = data_count - 1 - d if mirror else d
                moves.append(
                    (d * space_count + s, target * space_count + (s + shift) % space_count)
                )
        return moves

    order = [(mirror, shift) for mirror in (1, 0) for shift in reversed(range(space_count))][:-1]

    def gathered(parts):
        held = [parts[0]]
        for mirror, shift in order:
            held.append(
                lax.ppermute(
                    parts[mirror * space_count + shift], ("dp", "space"), pairs(mirror, shift)
                )
            )
        return held

    tied = lax.optimization_barrier

    share = channels // half
    extra = extra_rows(channels, half)
    flag = jnp.broadcast_to(upper.astype(f32), (8, channels))

    input_sums = input_call(x_table, field_in[0])
    input_lines = exchange(input_sums.reshape(half, row_count * col_block, channels))
    delta, delta_sums = delta_call(x_table, flag, pre_act[0], cotangent[0], field_in[0], half)
    delta_lines = exchange(delta_sums)
    input_parts = list(
        y_transform_call(y_table, input_lines, blocks, space_count, col_block, 0)
    )
    for shift in range(1, space_count):
        input_parts[shift] = lax.ppermute(input_parts[shift], ("dp", "space"), pairs(0, shift))
    held_rows = kx_local * size
    mirrored = sum(part[held_rows:].astype(f32) for part in input_parts).astype(bf16)
    delta_lines, mirrored = tied((delta_lines, mirrored))
    input_held = [part[:held_rows] for part in input_parts]
    input_held.append(lax.ppermute(mirrored, ("dp", "space"), pairs(1, 0)))

    delta_parts = y_transform_call(y_table, delta_lines, blocks, blocks, col_block, extra)
    weight, delta_parts = tied((spec_weight, delta_parts))
    weight = load_call(weight)
    delta_held, input_held[-1] = tied((gathered(delta_parts), input_held[-1]))
    back, delta_owned, share_rows = back_call(scale_rows, weight, delta_held, share)
    received = {(0, 0): back}
    for mirror, shift in order:
        received[(mirror, -shift % space_count)] = lax.ppermute(
            back, ("dp", "space"), pairs(mirror, shift)
        )
    modes = [received[(mirror, shift)] for mirror in (0, 1) for shift in range(space_count)]
    column_sums = y_inverse_call(y_table, share_rows, modes, half, col_block)
    column_sums, delta_owned = tied((column_sums, delta_owned))
    columns = exchange(column_sums)
    grad_spectral = outer_call(scale_rows, delta_owned, input_held)
    columns, grad_spectral = tied((columns, grad_spectral))
    grad_input, grad_local, bias_rows = final_call(x_table, flag, columns, delta, local_weight)
    return (grad_input[None], grad_spectral, grad_local, bias_rows.reshape(channels))


def solution(mesh):
    placed = (
        P(None, "space", "dp", None),
        P(None, "space", "dp", None),
        P(None, "space", "dp", None),
        P("dp", "space", None, None, None),
        P(),
    )
    return jax.shard_map(
        on_device,
        mesh=mesh,
        in_specs=placed,
        out_specs=(P(None, "space", "dp", None), P("dp", "space", None, None, None), P(), P()),
        check_vma=False,
    )
```

time: 124 us -> 80.1 us (0.65)
  blocking collectives: 40 us -> 0 us
  local copies, waits for them, and re-layouts: 11.7 us -> 0.89 us
  waiting for transfers between devices: 15.5 us -> 19.8 us
  starting transfers between devices: 25.1 us -> 28.6 us
    all_to_all x3 -> x0, blocking collectives: 40 us -> none  [the longest x1 15.7 us: on_device(): lax.all_to_all(stacked.reshape(device_count, share, channels), ('dp', 'sp...]
    all_to_all x2 -> x3, waiting for transfers between devices: 0.01 us -> 10.9 us  [exchange(): lax.all_to_all(values, 'dp', split_axis=0, concat_axis=0, tiled=True, axi...]
    ppermute x6 -> x3, waiting for transfers between devices: 11.8 us -> 1.09 us  [gathered(): lax.ppermute(parts[mirror * space_count + shift], ('dp', 'space'), pairs(...]
    unnamed x18 -> x8, local copies, waits for them, and re-layouts: 10.4 us -> 0.02 us
    ppermute x6 -> x3, starting transfers between devices: 11.9 us -> 5.91 us  [gathered(): lax.ppermute(parts[mirror * space_count + shift], ('dp', 'space'), pairs(...]
    all_to_all x2 -> x3, starting transfers between devices: 7.21 us -> 12.4 us  [exchange(): lax.all_to_all(values, 'dp', split_axis=0, concat_axis=0, tiled=True, axi...]
    ppermute x0 -> x2, starting transfers between devices: none -> 4.37 us  [the longest x1 2.78 us: on_device(): input_held.append(lax.ppermute(mirrored, ('dp', 'space'), pairs(1, 0)))]
    ppermute x0 -> x2, waiting for transfers between devices: none -> 4.31 us  [the longest x1 4.31 us: on_device(): lax.ppermute(input_parts[shift], ('dp', 'space'), pairs(0, shift))]
  transfers between devices with their start and end apart: 11 -> 11, of which waited for: 7 -> 9; matrix products, arithmetic and copies ran while one was open for 2% -> 2% of each run, Pallas kernels for 10% -> 22%
where the time goes in v2:
time: 80.1 us; the launch traced here: 79.7 us
  starting transfers between devices  28.6 us (36%)
  Pallas kernels  28 us (35%)
  waiting for transfers between devices  19.8 us (25%)
  other arithmetic  1.56 us (2%)
  local copies, waits for them, and re-layouts  0.89 us (1%)
  between operations  0.84 us (1%)
    all_to_all x3, starting transfers between devices, exchange(): lax.all_to_all(values, 'dp', split_axis=0, concat_axis=0, tiled=True, axi...  12.4 us
    all_to_all x3, waiting for transfers between devices, exchange(): lax.all_to_all(values, 'dp', split_axis=0, concat_axis=0, tiled=True, axi...  10.9 us
    pallas_call x1, Pallas kernels, delta_call(): pl.pallas_call(delta_kernel, grid=(columns // block,), in_specs=[whole(ta...  8.6 us
    ppermute x3, starting transfers between devices, on_device(): lax.ppermute(back, ('dp', 'space'), pairs(mirror, shift))  5.94 us
    ppermute x3, starting transfers between devices, gathered(): lax.ppermute(parts[mirror * space_count + shift], ('dp', 'space'), pairs(...  5.91 us
    pallas_call x1, Pallas kernels, outer_call(): pl.pallas_call(outer_kernel, grid=(held,), in_specs=[whole((rows, channel...  4.9 us
    ppermute x1, waiting for transfers between devices, on_device(): lax.ppermute(input_parts[shift], ('dp', 'space'), pairs(0, shift))  4.31 us
    ppermute x3, waiting for transfers between devices, on_device(): lax.ppermute(back, ('dp', 'space'), pairs(mirror, shift))  3.49 us
  transfers between devices with their start and end apart: 11, of which 9 were waited for; matrix products, arithmetic and copies ran while one was open for 2% of the time, Pallas kernels for 22%

profile of v2, /device:TPU:0, one launch (start us, length us, event | category | flops | bytes accessed | tf_op | source)
XLA Modules:
  0.0 79.7 jit_solution(9347697446646587025)
XLA Ops:
  0.7 0.8 fusion.9.table_ref
  1.5 2.8 %input_x_sums.1 = bf16[80,32,128]{2,1,0:T(8,128)(2,1)} custom-call(bf16[80,256]{1,0:T(8,128)(2,1)} %fusion.9.table_ref, bf16[256,32,128]{2,1,0:T(8,128)(2,1)} %bitcast.10), custom_call_target="tpu_custom_call" | custom-call | flops 167772160 | bytes 4194304 | tf_op jit(solution)/shard_map/input_x_sums/pallas_call | solution.py:180
  4.3 5.2 %all-to-all-start.1 = ((bf16[8,320,128]{2,1,0:T(8,128)(2,1)}), bf16[8,320,128]{2,1,0:T(8,128)(2,1)S(1)}, u32[]{:S(2)}, u32[]{:S(2)}) async-start(bf16[8,320,128]{2,1,0:T(8,128)(2,1)} %bitcast.12), calls=%async_computation.1 | async-start | bytes 1310720 | tf_op jit(solution)/shard_map/all_to_all | solution.py:564
  10.1 8.6 %delta_and_x_sums.1 = (bf16[256,32,128]{2,1,0:T(8,128)(2,1)}, bf16[8,360,128]{2,1,0:T(8,128)(2,1)}) custom-call(bf16[80,256]{1,0:T(8,128)(2,1)} %fusion.9.table_ref, f32[8,128]{1,0:T(8,128)} %broadcast_in_dim.18.upper_ref, bf16[256,32,128]{2,1,0:T(8,128)(2,1)} %bitcast.13, bf16[256,32,128]{2,1,0:T(8,128)(2,1)} %bitcast.14, bf16[256,32,128]{2,1,0:T(8,128)(2,1)} %bitcast.11), custom_call_target="tpu_custom_call" | custom-call | flops 335544320 | bytes 8388608 | tf_op jit(solution)/shard_map/delta_and_x_sums/pallas_call | solution.py:147
  18.7 1.1 %all-to-all-done.1.lines_ref = bf16[8,320,128]{2,1,0:T(8,128)(2,1)S(1)} async-done(((bf16[8,320,128]{2,1,0:T(8,128)(2,1)}), bf16[8,320,128]{2,1,0:T(8,128)(2,1)S(1)}, u32[]{:S(2)}, u32[]{:S(2)}) %all-to-all-start.1) | async-done | bytes 655392 | tf_op jit(solution)/shard_map/all_to_all | solution.py:564
  19.8 3.5 %all-to-all-start = ((bf16[8,360,128]{2,1,0:T(8,128)(2,1)}), bf16[8,360,128]{2,1,0:T(8,128)(2,1)S(1)}, u32[]{:S(2)}, u32[]{:S(2)}) async-start(bf16[8,360,128]{2,1,0:T(8,128)(2,1)} %get-tuple-element.34), calls=%async_computation | async-start | bytes 1474560 | tf_op jit(solution)/shard_map/all_to_all | solution.py:564
  24.8 1.6 %collective-permute-start = (bf16[512,128]{1,0:T(8,128)(2,1)S(1)}, bf16[512,128]{1,0:T(8,128)(2,1)S(1)}, u32[]{:S(2)}, u32[]{:S(2)}) collective-permute-start(bf16[512,128]{1,0:T(8,128)(2,1)S(1)} %get-tuple-element.36), channel_id=1, source_target_pairs={{0,1},{1,0},{2,3},{3,2},{4,5},{5,4},{6,7},{7,6},{8,9},{9,8},{10,11... | collective-permute-start | bytes 393224 | tf_op jit(solution)/shard_map/ppermute | solution.py:604
  26.4 4.3 %collective-permute-done = bf16[512,128]{1,0:T(8,128)(2,1)S(1)} collective-permute-done((bf16[512,128]{1,0:T(8,128)(2,1)S(1)}, bf16[512,128]{1,0:T(8,128)(2,1)S(1)}, u32[]{:S(2)}, u32[]{:S(2)}) %collective-permute-start) | collective-permute-done | bytes 131104 | tf_op jit(solution)/shard_map/ppermute | solution.py:604
  30.7 3.7 %all-to-all-done.lines_ref = bf16[8,360,128]{2,1,0:T(8,128)(2,1)S(1)} async-done(((bf16[8,360,128]{2,1,0:T(8,128)(2,1)}), bf16[8,360,128]{2,1,0:T(8,128)(2,1)S(1)}, u32[]{:S(2)}, u32[]{:S(2)}) %all-to-all-start) | async-done | bytes 737312 | tf_op jit(solution)/shard_map/all_to_all | solution.py:564
  34.9 2.8 %collective-permute-start.4 = (bf16[256,128]{1,0:T(8,128)(2,1)S(1)}, bf16[256,128]{1,0:T(8,128)(2,1)S(1)}, u32[]{:S(2)}, u32[]{:S(2)}) collective-permute-start(bf16[256,128]{1,0:T(8,128)(2,1)S(1)} %add_convert_fusion), channel_id=1, source_target_pairs={{0,30},{1,31},{2,28},{3,29},{4,26},{5,27},{6,24},{7,25},{8,22},{9,... | collective-permute-start | bytes 196616 | tf_op jit(solution)/shard_map/ppermute | solution.py:609
  37.7 2.7 %collective-permute-start.1 = (bf16[296,128]{1,0:T(8,128)(2,1)S(1)}, bf16[296,128]{1,0:T(8,128)(2,1)S(1)}, u32[]{:S(2)}, u32[]{:S(2)}) collective-permute-start(bf16[296,128]{1,0:T(8,128)(2,1)S(1)} %get-tuple-element.44), channel_id=1, source_target_pairs={{0,31},{1,30},{2,29},{3,28},{4,27},{5,26},{6,25},{7,24},{8,23},{9,... | collective-permute-start | bytes 227336 | tf_op jit(solution)/shard_map/ppermute | solution.py:584
  40.3 2.7 %collective-permute-start.2 = (bf16[296,128]{1,0:T(8,128)(2,1)S(1)}, bf16[296,128]{1,0:T(8,128)(2,1)S(1)}, u32[]{:S(2)}, u32[]{:S(2)}) collective-permute-start(bf16[296,128]{1,0:T(8,128)(2,1)S(1)} %get-tuple-element.45), channel_id=1, source_target_pairs={{0,30},{1,31},{2,28},{3,29},{4,26},{5,27},{6,24},{7,25},{8,22},{9,... | collective-permute-start | bytes 227336 | tf_op jit(solution)/shard_map/ppermute | solution.py:584
  43.6 3.5 %weights_to_vmem.1 = bf16[4,2,16,2,128,128]{5,4,3,2,1,0:T(8,128)(2,1)S(1)} custom-call(bf16[4,2,16,2,128,128]{5,4,3,2,1,0:T(8,128)(2,1)} %bitcast.9), custom_call_target="tpu_custom_call" | custom-call | bytes 16777216 | tf_op jit(solution)/shard_map/weights_to_vmem/pallas_call | solution.py:270
  48.2 3.2 %mode_back.1 = (bf16[4,64,128]{2,1,0:T(8,128)(2,1)S(1)}, bf16[4,64,128]{2,1,0:T(8,128)(2,1)S(1)}, bf16[40,128]{1,0:T(8,128)(2,1)S(1)}) custom-call(f32[64,128]{1,0:T(8,128)S(1)} %broadcast_in_dim.42.scale_ref, bf16[4,32,2,128,128]{4,3,2,1,0:T(8,128)(2,1)S(1)} %bitcast.8, bf16[296,128]{1,0:T(8,128)(2,1)S(1)} %get-tuple-element.48.refs_0_, ...), custom_call_target="tpu_custom_call" | custom-call | flops 16777216 | bytes 8388608 | tf_op jit(solution)/shard_map/mode_back/pallas_call | solution.py:321
  51.4 2.3 %collective-permute-start.7 = (bf16[4,64,128]{2,1,0:T(8,128)(2,1)S(1)}, bf16[4,64,128]{2,1,0:T(8,128)(2,1)S(1)}, u32[]{:S(2)}, u32[]{:S(2)}) collective-permute-start(bf16[4,64,128]{2,1,0:T(8,128)(2,1)S(1)} %get-tuple-element.53.refs_0_), channel_id=1, source_target_pairs={{0,31},{1,30},{2,29},{3,28},{4,27},{5,26},{6,25},{7,24},{8,23},{9,... | collective-permute-start | bytes 196616 | tf_op jit(solution)/shard_map/ppermute | solution.py:618
  53.7 2.7 %collective-permute-start.6 = (bf16[4,64,128]{2,1,0:T(8,128)(2,1)S(1)}, bf16[4,64,128]{2,1,0:T(8,128)(2,1)S(1)}, u32[]{:S(2)}, u32[]{:S(2)}) collective-permute-start(bf16[4,64,128]{2,1,0:T(8,128)(2,1)S(1)} %get-tuple-element.53.refs_0_), channel_id=1, source_target_pairs={{0,30},{1,31},{2,28},{3,29},{4,26},{5,27},{6,24},{7,25},{8,22},{9,... | collective-permute-start | bytes 196616 | tf_op jit(solution)/shard_map/ppermute | solution.py:618
  56.4 0.9 %collective-permute-start.5 = (bf16[4,64,128]{2,1,0:T(8,128)(2,1)S(1)}, bf16[4,64,128]{2,1,0:T(8,128)(2,1)S(1)}, u32[]{:S(2)}, u32[]{:S(2)}) collective-permute-start(bf16[4,64,128]{2,1,0:T(8,128)(2,1)S(1)} %get-tuple-element.53.refs_0_), channel_id=1, source_target_pairs={{0,1},{1,0},{2,3},{3,2},{4,5},{5,4},{6,7},{7,6},{8,9},{9,8},{10,11... | collective-permute-start | bytes 196616 | tf_op jit(solution)/shard_map/ppermute | solution.py:618
  57.3 1.9 %collective-permute-done.7.refs_3_ = bf16[4,64,128]{2,1,0:T(8,128)(2,1)S(1)} collective-permute-done((bf16[4,64,128]{2,1,0:T(8,128)(2,1)S(1)}, bf16[4,64,128]{2,1,0:T(8,128)(2,1)S(1)}, u32[]{:S(2)}, u32[]{:S(2)}) %collective-permute-start.7) | collective-permute-done | bytes 65568 | tf_op jit(solution)/shard_map/ppermute | solution.py:618
  59.2 0.9 %collective-permute-done.6.refs_2_ = bf16[4,64,128]{2,1,0:T(8,128)(2,1)S(1)} collective-permute-done((bf16[4,64,128]{2,1,0:T(8,128)(2,1)S(1)}, bf16[4,64,128]{2,1,0:T(8,128)(2,1)S(1)}, u32[]{:S(2)}, u32[]{:S(2)}) %collective-permute-start.6) | collective-permute-done | bytes 65568 | tf_op jit(solution)/shard_map/ppermute | solution.py:618
  60.8 1.3 %y_inverse.1 = bf16[8,360,128]{2,1,0:T(8,128)(2,1)} custom-call(bf16[256,512]{1,0:T(8,128)(2,1)S(1)} %fusion.table_ref, bf16[40,128]{1,0:T(8,128)(2,1)S(1)} %get-tuple-element.52.share_ref, bf16[4,64,128]{2,1,0:T(8,128)(2,1)S(1)} %get-tuple-element.53.refs_0_, bf16[4,64,128]{2,1,0:T(8,128)(2,1)S(1)} %collective-permute-done.5.refs_1_, ...), custom_call_target="tpu_custom_call" | custom-call | flops 167772160 | bytes 1310720 | tf_op jit(solution)/shard_map/y_inverse/pallas_call | solution.py:424
  62.2 3.6 %all-to-all-start.2 = ((bf16[8,360,128]{2,1,0:T(8,128)(2,1)}), bf16[8,360,128]{2,1,0:T(8,128)(2,1)S(1)}, u32[]{:S(2)}, u32[]{:S(2)}) async-start(bf16[8,360,128]{2,1,0:T(8,128)(2,1)} %y_inverse.1), calls=%async_computation.2 | async-start | bytes 1474560 | tf_op jit(solution)/shard_map/all_to_all | solution.py:564
  65.9 4.9 %grad_spectral.1 = bf16[4,32,2,128,128]{4,3,2,1,0:T(8,128)(2,1)} custom-call(f32[64,128]{1,0:T(8,128)S(1)} %broadcast_in_dim.42.scale_ref, bf16[4,64,128]{2,1,0:T(8,128)(2,1)S(1)} %get-tuple-element.56.delta_ref, bf16[256,128]{1,0:T(8,128)(2,1)S(1)} %slice.14.refs_0_, bf16[256,128]{1,0:T(8,128)(2,1)S(1)} %slice.17.refs_1_, ...), custom_call_target="tpu_custom_call" | custom-call | flops 12582912 | bytes 8388608 | tf_op jit(solution)/shard_map/grad_spectral/pallas_call | solution.py:371
  70.8 6.2 %all-to-all-done.2.lines_ref = bf16[8,360,128]{2,1,0:T(8,128)(2,1)S(1)} async-done(((bf16[8,360,128]{2,1,0:T(8,128)(2,1)}), bf16[8,360,128]{2,1,0:T(8,128)(2,1)S(1)}, u32[]{:S(2)}, u32[]{:S(2)}) %all-to-all-start.2) | async-done | bytes 737312 | tf_op jit(solution)/shard_map/all_to_all | solution.py:564
  76.9 2.8 %x_inverse_and_local.1 = (bf16[256,32,128]{2,1,0:T(8,128)(2,1)}, f32[128,128]{1,0:T(8,128)}, f32[1,128]{1,0:T(1,128)}) custom-call(bf16[80,256]{1,0:T(8,128)(2,1)S(1)} %copy-done.1, f32[8,128]{1,0:T(8,128)S(1)} %copy-done.2, bf16[8,360,128]{2,1,0:T(8,128)(2,1)S(1)} %all-to-all-done.2.lines_ref, bf16[256,32,128]{2,1,0:T(8,128)(2,1)S(1)} %copy-done, ...), custom_call_target="tpu_custom_call" | custom-call | flops 436207616 | bytes 5242880 | tf_op jit(solution)/shard_map/x_inverse_and_local/pallas_call | solution.py:485
  (32 shorter events, 5.0 us)
Async XLA Ops:
  4.3 15.5 %all-to-all-start.1 = ((bf16[8,320,128]{2,1,0:T(8,128)(2,1)}), bf16[8,320,128]{2,1,0:T(8,128)(2,1)S(1)}, u32[]{:S(2)}, u32[]{:S(2)}) async-start(bf16[8,320,128]{2,1,0:T(8,128)(2,1)} %bitcast.12), calls=%async_computation.1 | async-start | bytes 1310720 | tf_op jit(solution)/shard_map/all_to_all | solution.py:564
  19.8 14.6 %all-to-all-start = ((bf16[8,360,128]{2,1,0:T(8,128)(2,1)}), bf16[8,360,128]{2,1,0:T(8,128)(2,1)S(1)}, u32[]{:S(2)}, u32[]{:S(2)}) async-start(bf16[8,360,128]{2,1,0:T(8,128)(2,1)} %get-tuple-element.34), calls=%async_computation | async-start | bytes 1474560 | tf_op jit(solution)/shard_map/all_to_all | solution.py:564
  24.8 5.9 %collective-permute-start = (bf16[512,128]{1,0:T(8,128)(2,1)S(1)}, bf16[512,128]{1,0:T(8,128)(2,1)S(1)}, u32[]{:S(2)}, u32[]{:S(2)}) collective-permute-start(bf16[512,128]{1,0:T(8,128)(2,1)S(1)} %get-tuple-element.36), channel_id=1, source_target_pairs={{0,1},{1,0},{2,3},{3,2},{4,5},{5,4},{6,7},{7,6},{8,9},{9,8},{10,11... | collective-permute-start | bytes 393224 | tf_op jit(solution)/shard_map/ppermute | solution.py:604
  34.9 12.2 %collective-permute-start.4 = (bf16[256,128]{1,0:T(8,128)(2,1)S(1)}, bf16[256,128]{1,0:T(8,128)(2,1)S(1)}, u32[]{:S(2)}, u32[]{:S(2)}) collective-permute-start(bf16[256,128]{1,0:T(8,128)(2,1)S(1)} %add_convert_fusion), channel_id=1, source_target_pairs={{0,30},{1,31},{2,28},{3,29},{4,26},{5,27},{6,24},{7,25},{8,22},{9,... | collective-permute-start | bytes 196616 | tf_op jit(solution)/shard_map/ppermute | solution.py:609
  37.7 9.4 %collective-permute-start.1 = (bf16[296,128]{1,0:T(8,128)(2,1)S(1)}, bf16[296,128]{1,0:T(8,128)(2,1)S(1)}, u32[]{:S(2)}, u32[]{:S(2)}) collective-permute-start(bf16[296,128]{1,0:T(8,128)(2,1)S(1)} %get-tuple-element.44), channel_id=1, source_target_pairs={{0,31},{1,30},{2,29},{3,28},{4,27},{5,26},{6,25},{7,24},{8,23},{9,... | collective-permute-start | bytes 227336 | tf_op jit(solution)/shard_map/ppermute | solution.py:584
  40.3 7.3 %collective-permute-start.2 = (bf16[296,128]{1,0:T(8,128)(2,1)S(1)}, bf16[296,128]{1,0:T(8,128)(2,1)S(1)}, u32[]{:S(2)}, u32[]{:S(2)}) collective-permute-start(bf16[296,128]{1,0:T(8,128)(2,1)S(1)} %get-tuple-element.45), channel_id=1, source_target_pairs={{0,30},{1,31},{2,28},{3,29},{4,26},{5,27},{6,24},{7,25},{8,22},{9,... | collective-permute-start | bytes 227336 | tf_op jit(solution)/shard_map/ppermute | solution.py:584
  43.0 5.1 %collective-permute-start.3 = (bf16[296,128]{1,0:T(8,128)(2,1)S(1)}, bf16[296,128]{1,0:T(8,128)(2,1)S(1)}, u32[]{:S(2)}, u32[]{:S(2)}) collective-permute-start(bf16[296,128]{1,0:T(8,128)(2,1)S(1)} %get-tuple-element.46), channel_id=1, source_target_pairs={{0,1},{1,0},{2,3},{3,2},{4,5},{5,4},{6,7},{7,6},{8,9},{9,8},{10,11... | collective-permute-start | bytes 227336 | tf_op jit(solution)/shard_map/ppermute | solution.py:584
  51.4 7.8 %collective-permute-start.7 = (bf16[4,64,128]{2,1,0:T(8,128)(2,1)S(1)}, bf16[4,64,128]{2,1,0:T(8,128)(2,1)S(1)}, u32[]{:S(2)}, u32[]{:S(2)}) collective-permute-start(bf16[4,64,128]{2,1,0:T(8,128)(2,1)S(1)} %get-tuple-element.53.refs_0_), channel_id=1, source_target_pairs={{0,31},{1,30},{2,29},{3,28},{4,27},{5,26},{6,25},{7,24},{8,23},{9,... | collective-permute-start | bytes 196616 | tf_op jit(solution)/shard_map/ppermute | solution.py:618
  53.7 6.4 %collective-permute-start.6 = (bf16[4,64,128]{2,1,0:T(8,128)(2,1)S(1)}, bf16[4,64,128]{2,1,0:T(8,128)(2,1)S(1)}, u32[]{:S(2)}, u32[]{:S(2)}) collective-permute-start(bf16[4,64,128]{2,1,0:T(8,128)(2,1)S(1)} %get-tuple-element.53.refs_0_), channel_id=1, source_target_pairs={{0,30},{1,31},{2,28},{3,29},{4,26},{5,27},{6,24},{7,25},{8,22},{9,... | collective-permute-start | bytes 196616 | tf_op jit(solution)/shard_map/ppermute | solution.py:618
  56.4 4.4 %collective-permute-start.5 = (bf16[4,64,128]{2,1,0:T(8,128)(2,1)S(1)}, bf16[4,64,128]{2,1,0:T(8,128)(2,1)S(1)}, u32[]{:S(2)}, u32[]{:S(2)}) collective-permute-start(bf16[4,64,128]{2,1,0:T(8,128)(2,1)S(1)} %get-tuple-element.53.refs_0_), channel_id=1, source_target_pairs={{0,1},{1,0},{2,3},{3,2},{4,5},{5,4},{6,7},{7,6},{8,9},{9,8},{10,11... | collective-permute-start | bytes 196616 | tf_op jit(solution)/shard_map/ppermute | solution.py:618
  62.2 14.7 %all-to-all-start.2 = ((bf16[8,360,128]{2,1,0:T(8,128)(2,1)}), bf16[8,360,128]{2,1,0:T(8,128)(2,1)S(1)}, u32[]{:S(2)}, u32[]{:S(2)}) async-start(bf16[8,360,128]{2,1,0:T(8,128)(2,1)} %y_inverse.1), calls=%async_computation.2 | async-start | bytes 1474560 | tf_op jit(solution)/shard_map/all_to_all | solution.py:564
  65.8 11.1 %copy-start = (bf16[256,32,128]{2,1,0:T(8,128)(2,1)S(1)}, bf16[256,32,128]{2,1,0:T(8,128)(2,1)}, u32[]{:S(2)}) copy-start(bf16[256,32,128]{2,1,0:T(8,128)(2,1)} %get-tuple-element.59.delta_ref) | copy-start | bytes 6291460
  65.8 11.1 %copy-start.1 = (bf16[80,256]{1,0:T(8,128)(2,1)S(1)}, bf16[80,256]{1,0:T(8,128)(2,1)}, u32[]{:S(2)}) copy-start(bf16[80,256]{1,0:T(8,128)(2,1)} %fusion.9.table_ref) | copy-start | bytes 122884
  65.8 11.1 %copy-start.2 = (f32[8,128]{1,0:T(8,128)S(1)}, f32[8,128]{1,0:T(8,128)}, u32[]{:S(2)}) copy-start(f32[8,128]{1,0:T(8,128)} %broadcast_in_dim.18.upper_ref) | copy-start | bytes 12292
  65.9 11.1 %copy-start.3 = (bf16[128,128]{1,0:T(8,128)(2,1)S(1)}, bf16[128,128]{1,0:T(8,128)(2,1)}, u32[]{:S(2)}) copy-start(bf16[128,128]{1,0:T(8,128)(2,1)} %weight_ref.1) | copy-start | bytes 98308

commit v3 on v2

--- a/solution.py
+++ b/solution.py
@@ -44,6 +44,25 @@
     return jnp.where((turns == 1) | (turns == 2), -magnitude, magnitude).astype(bf16)
 
 
+def x_table(sizes, transposed=False):
+    half, kx_local, slab_rows, grid_rows = sizes
+    row_count = 2 * (kx_local + 1)
+    upper = (lax.axis_index("dp") >= half).astype(jnp.int32)
+    shape = (half * row_count, slab_rows)
+    if transposed:
+        shape = shape[::-1]
+    row = lax.broadcasted_iota(jnp.int32, shape, 1 if transposed else 0)
+    position = lax.axis_index("space") * slab_rows + lax.broadcasted_iota(
+        jnp.int32, shape, 0 if transposed else 1
+    )
+    member = sum((row >= i * row_count).astype(jnp.int32) for i in range(1, half))
+    inner = row - member * row_count
+    ascending = member * kx_local + (inner >> 1)
+    frequency = ascending + upper * (half * kx_local - 2 * ascending)
+    quarter = grid_rows // 4
+    return cosine_table(frequency * position - (inner & 1) * quarter, grid_rows)
+
+
 def params(mebibytes=16):
     return pltpu.CompilerParams(vmem_limit_bytes=mebibytes * mebi)
 
@@ -88,7 +107,7 @@
 
 
 def delta_kernel(
-    table_ref, upper_ref, pre_ref, cot_ref, field_ref, delta_ref, out_ref, lines, local, bias
+    sizes, pre_ref, cot_ref, field_ref, delta_ref, out_ref, lines, local, bias, table
 ):
     grid_rows, columns, channels = pre_ref.shape
     half = out_ref.shape[0]
@@ -100,6 +119,7 @@
     def _():
         local[...] = jnp.zeros_like(local)
         bias[...] = jnp.zeros_like(bias)
+        table[...] = x_table(sizes)
 
     def slab(i, carry):
         rows = pl.ds(pl.multiple_of(i * step, step), step)
@@ -117,7 +137,7 @@
         (((0,), (0,)), ((), ())),
         preferred_element_type=f32,
     )
-    sums = matrix_per_column(table_ref[...], [lines[y] for y in range(columns)])
+    sums = matrix_per_column(table[...], [lines[y] for y in range(columns)])
     per_target = sums.shape[0] // half
     first = pl.multiple_of(block * columns, columns)
     for target in range(half):
@@ -128,7 +148,7 @@
 
     @pl.when(block == pl.num_programs(0) - 1)
     def _():
-        upper = upper_ref[:1] > 0.0
+        upper = lax.axis_index("dp") >= half
         share = channels // half
         total = jnp.sum(bias[...], axis=0, keepdims=True)
         for target in range(half):
@@ -138,16 +158,17 @@
             out_ref[target, per_target * all_columns :] = rows
 
 
-def delta_call(table, upper, pre_act, cotangent, field_in, half):
+def delta_call(sizes, pre_act, cotangent, field_in):
     grid_rows, columns, channels = pre_act.shape
-    rows = table.shape[0]
+    half = sizes[0]
+    rows = 2 * half * (sizes[1] + 1)
     block = min(16, columns)
     field = pl.BlockSpec((grid_rows, block, channels), lambda i: (0, i, 0))
     message = (half, rows // half * columns + extra_rows(channels, half), channels)
     return pl.pallas_call(
-        delta_kernel,
+        functools.partial(delta_kernel, sizes),
         grid=(columns // block,),
-        in_specs=[whole(table.shape), whole(upper.shape), field, field, field],
+        in_specs=[field, field, field],
         out_specs=[field, whole(message)],
         out_shape=[
             jax.ShapeDtypeStruct(pre_act.shape, bf16),
@@ -157,44 +178,57 @@
             pltpu.VMEM((block, grid_rows, channels), bf16),
             pltpu.VMEM((channels, channels), f32),
             pltpu.VMEM((8, channels), f32),
+            pltpu.VMEM((rows, grid_rows), bf16),
         ],
         compiler_params=params(60),
         cost_estimate=pl.CostEstimate(
             flops=4 * rows * pre_act.size, bytes_accessed=8 * pre_act.size, transcendentals=pre_act.size
         ),
         name="delta_and_x_sums",
-    )(table, upper, pre_act, cotangent, field_in)
-
-
-def input_kernel(table_ref, field_ref, out_ref):
-    lines = jnp.swapaxes(field_ref[...], 0, 1)
+    )(pre_act, cotangent, field_in)
+
+
+def input_kernel(sizes, *refs):
+    field_refs, (out_ref, table) = refs[:-2], refs[-2:]
+
+    @pl.when(pl.program_id(0) == 0)
+    def _():
+        table[...] = x_table(sizes)
+
+    lines = [jnp.swapaxes(ref[...], 0, 1) for ref in field_refs]
     out_ref[...] = matrix_per_column(
-        table_ref[...], [lines[y] for y in range(field_ref.shape[1])]
-    )
-
-
-def input_call(table, field_in):
+        table[...],
+        [jnp.concatenate([part[y] for part in lines], axis=0) for y in range(out_ref.shape[1])],
+    )
+
+
+def input_call(sizes, field_in):
     grid_rows, columns, channels = field_in.shape
-    rows = table.shape[0]
+    rows = 2 * sizes[0] * (sizes[1] + 1)
     block = min(16, columns)
+    pieces = 4
     return pl.pallas_call(
-        input_kernel,
+        functools.partial(input_kernel, sizes),
         grid=(columns // block,),
         in_specs=[
-            whole(table.shape),
-            pl.BlockSpec((grid_rows, block, channels), lambda i: (0, i, 0)),
+            pl.BlockSpec(
+                (grid_rows // pieces, block, channels), lambda i, piece=piece: (piece, i, 0)
+            )
+            for piece in range(pieces)
         ],
         out_specs=pl.BlockSpec((rows, block, channels), lambda i: (0, i, 0)),
         out_shape=jax.ShapeDtypeStruct((rows, columns, channels), bf16),
+        scratch_shapes=[pltpu.VMEM((rows, grid_rows), bf16)],
         compiler_params=params(60),
         cost_estimate=pl.CostEstimate(
             flops=2 * rows * field_in.size, bytes_accessed=4 * field_in.size, transcendentals=0
         ),
         name="input_x_sums",
-    )(table, field_in)
-
-
-def y_transform_kernel(columns, extra, blocks, table_ref, lines_ref, *out_refs):
+    )(*[field_in] * pieces)
+
+
+def y_transform_kernel(columns, extra, blocks, tails, table_ref, lines_ref, *refs):
+    tail_refs, out_refs = refs[:tails], refs[tails:]
     sources, total_rows, channels = lines_ref.shape
     frequencies = (total_rows - extra) // columns // 2
     own = blocks // 2
@@ -223,25 +257,28 @@
         pieces = [unpack_share(rows, lines_ref[i, total_rows - extra :]) for i in range(sources)]
         packed = pack_share(sum(p[0] for p in pieces), sum(p[1] for p in pieces))
         for out_ref in out_refs:
-            out_ref[(frequencies - 1) * size :] = packed
-
-
-def y_transform_call(table, lines, blocks, outputs, columns, extra):
+            out_ref[out_ref.shape[0] - extra :] = packed
+    for tail_ref in tail_refs:
+        rows = tail_ref.shape[0]
+        out_refs[own][rows : 2 * rows] = tail_ref[...]
+
+
+def y_transform_call(table, lines, blocks, outputs, columns, extra, tails=()):
     sources, total_rows, channels = lines.shape
     held = (total_rows - extra) // columns // 2 - 1
     size = table.shape[0] // blocks
+    out_rows = [blocks // outputs * held * size + extra] * outputs
+    for tail in tails:
+        out_rows[blocks // 2] += tail.shape[0]
     return pl.pallas_call(
-        functools.partial(y_transform_kernel, columns, extra, blocks),
-        out_shape=[
-            jax.ShapeDtypeStruct((blocks // outputs * held * size + extra, channels), bf16)
-        ]
-        * outputs,
+        functools.partial(y_transform_kernel, columns, extra, blocks, len(tails)),
+        out_shape=[jax.ShapeDtypeStruct((rows, channels), bf16) for rows in out_rows],
         compiler_params=params(),
         cost_estimate=pl.CostEstimate(
             flops=2 * (held + 1) * table.size * channels, bytes_accessed=4 * lines.size, transcendentals=0
         ),
         name="y_sums",
-    )(table, lines)
+    )(table, lines, *tails)
 
 
 def turned(values):
@@ -309,7 +346,8 @@
 
     @pl.when((j == 0) & (k == 0))
     def _():
-        pieces = [unpack_share(share, ref[held * rows :]) for ref in part_refs]
+        extra = share_ref.shape[0]
+        pieces = [unpack_share(share, ref[ref.shape[0] - extra :]) for ref in part_refs]
         share_ref[...] = pack_share(sum(p[0] for p in pieces), sum(p[1] for p in pieces))
 
 
@@ -372,7 +410,10 @@
         outer_kernel,
         grid=(held,),
         in_specs=[whole((rows, channels)), part]
-        + [pl.BlockSpec((rows, channels), lambda j: (j, 0))] * len(parts),
+        + [
+            pl.BlockSpec((rows, channels), lambda j, first=first: (j + first, 0))
+            for _, first in parts
+        ],
         out_specs=pl.BlockSpec((1, modes, 2, channels, channels), lambda j: (j, 0, 0, 0, 0)),
         out_shape=jax.ShapeDtypeStruct((held, modes, 2, channels, channels), bf16),
         compiler_params=params(),
@@ -382,7 +423,7 @@
             transcendentals=0,
         ),
         name="grad_spectral",
-    )(scale_rows, delta, *parts)
+    )(scale_rows, delta, *[part for part, _ in parts])
 
 
 def y_inverse_kernel(columns, table_ref, share_ref, *refs):
@@ -437,14 +478,19 @@
 
 
 def final_kernel(
-    table_ref, upper_ref, lines_ref, delta_ref, weight_ref, out_ref, local_ref, bias_ref
+    sizes, lines_ref, delta_ref, weight_ref, out_ref, local_ref, bias_ref, table
 ):
     grid_rows, columns, channels = out_ref.shape
     half = lines_ref.shape[0]
     block = pl.program_id(0)
     all_columns = columns * pl.num_programs(0)
-    per_source = table_ref.shape[0] // half
+    per_source = table.shape[1] // half
     first = pl.multiple_of(block * columns, columns)
+
+    @pl.when(block == 0)
+    def _():
+        table[...] = x_table(sizes, transposed=True)
+
     lines = jnp.stack(
         [
             lines_ref[source, pl.ds(row * all_columns + first, columns), :]
@@ -454,7 +500,7 @@
         axis=0,
     )
     lines = jnp.swapaxes(lines, 0, 1)
-    spectral = matrix_per_column(table_ref[...].T, [lines[y] for y in range(columns)])
+    spectral = matrix_per_column(table[...], [lines[y] for y in range(columns)])
     local = lax.dot_general(
         delta_ref[...].reshape(grid_rows * columns, channels),
         weight_ref[...],
@@ -465,7 +511,7 @@
 
     @pl.when(block == 0)
     def _():
-        upper = upper_ref[:1] > 0.0
+        upper = lax.axis_index("dp") >= half
         share = channels // half
         pieces = [
             unpack_share(share, lines_ref[source, per_source * all_columns :])
@@ -478,16 +524,15 @@
         bias_ref[...] = pieces[0][1]
 
 
-def final_call(table, upper, lines, delta, local_weight):
+def final_call(sizes, lines, delta, local_weight):
     grid_rows, columns, channels = delta.shape
+    rows = 2 * sizes[0] * (sizes[1] + 1)
     block = min(16, columns)
     field = pl.BlockSpec((grid_rows, block, channels), lambda i: (0, i, 0))
     return pl.pallas_call(
-        final_kernel,
+        functools.partial(final_kernel, sizes),
         grid=(columns // block,),
         in_specs=[
-            whole(table.shape),
-            whole(upper.shape),
             whole(lines.shape),
             field,
             whole(local_weight.shape),
@@ -498,14 +543,15 @@
             jax.ShapeDtypeStruct((channels, channels), f32),
             jax.ShapeDtypeStruct((1, channels), f32),
         ],
+        scratch_shapes=[pltpu.VMEM((grid_rows, rows), bf16)],
         compiler_params=params(),
         cost_estimate=pl.CostEstimate(
-            flops=2 * (table.shape[0] + channels) * delta.size,
+            flops=2 * (rows + channels) * delta.size,
             bytes_accessed=5 * delta.size,
             transcendentals=0,
         ),
         name="x_inverse_and_local",
-    )(table, upper, lines, delta, local_weight)
+    )(lines, delta, local_weight)
 
 
 def on_device(field_in, pre_act, cotangent, spec_weight, local_weight):
@@ -522,17 +568,7 @@
     space_index = lax.axis_index("space")
     upper = data_index // half
 
-    row = jnp.arange(half * row_count, dtype=jnp.int32)
-    member, inner = row // row_count, row % row_count
-    t = inner // 2
-    frequency = jnp.where(
-        upper == 0, kx_local * member + t, kx_local * (half - 1 - member) + kx_local - t
-    )
-    positions = space_index * slab_rows + jnp.arange(slab_rows, dtype=jnp.int32)
-    quarter = grid_rows // 4
-    x_table = cosine_table(
-        frequency[:, None] * positions[None, :] - (inner % 2 * quarter)[:, None], grid_rows
-    )
+    sizes = (half, kx_local, slab_rows, grid_rows)
 
     blocks = 2 * space_count
     size = 2 * ky_local
@@ -591,11 +627,10 @@
 
     share = channels // half
     extra = extra_rows(channels, half)
-    flag = jnp.broadcast_to(upper.astype(f32), (8, channels))
-
-    input_sums = input_call(x_table, field_in[0])
+
+    input_sums = input_call(sizes, field_in[0])
     input_lines = exchange(input_sums.reshape(half, row_count * col_block, channels))
-    delta, delta_sums = delta_call(x_table, flag, pre_act[0], cotangent[0], field_in[0], half)
+    delta, delta_sums = delta_call(sizes, pre_act[0], cotangent[0], field_in[0])
     delta_lines = exchange(delta_sums)
     input_parts = list(
         y_transform_call(y_table, input_lines, blocks, space_count, col_block, 0)
@@ -605,13 +640,15 @@
     held_rows = kx_local * size
     mirrored = sum(part[held_rows:].astype(f32) for part in input_parts).astype(bf16)
     delta_lines, mirrored = tied((delta_lines, mirrored))
-    input_held = [part[:held_rows] for part in input_parts]
-    input_held.append(lax.ppermute(mirrored, ("dp", "space"), pairs(1, 0)))
-
-    delta_parts = y_transform_call(y_table, delta_lines, blocks, blocks, col_block, extra)
+
+    delta_parts = y_transform_call(
+        y_table, delta_lines, blocks, blocks, col_block, extra, (mirrored,)
+    )
     weight, delta_parts = tied((spec_weight, delta_parts))
     weight = load_call(weight)
-    delta_held, input_held[-1] = tied((gathered(delta_parts), input_held[-1]))
+    delta_held = gathered(delta_parts)
+    input_held = [(part, 0) for part in input_parts]
+    input_held.append((delta_held[1 + order.index((1, 0))], kx_local))
     back, delta_owned, share_rows = back_call(scale_rows, weight, delta_held, share)
     received = {(0, 0): back}
     for mirror, shift in order:
@@ -624,7 +661,7 @@
     columns = exchange(column_sums)
     grad_spectral = outer_call(scale_rows, delta_owned, input_held)
     columns, grad_spectral = tied((columns, grad_spectral))
-    grad_input, grad_local, bias_rows = final_call(x_table, flag, columns, delta, local_weight)
+    grad_input, grad_local, bias_rows = final_call(sizes, columns, delta, local_weight)
     return (grad_input[None], grad_spectral, grad_local, bias_rows.reshape(channels))
 
 

time: 80.1 us -> 78.3 us (0.978)
  starting transfers between devices: 28.6 us -> 26.7 us
  waiting for transfers between devices: 19.8 us -> 21.1 us
  other arithmetic: 1.56 us -> 0.74 us
    ppermute x1 -> x0, starting transfers between devices: 2.78 us -> none  [on_device(): input_held.append(lax.ppermute(mirrored, ('dp', 'space'), pairs(1, 0)))]
    ppermute x3, waiting for transfers between devices: 1.09 us -> 2.01 us  [gathered(): lax.ppermute(parts[mirror * space_count + shift], ('dp', 'space'), pairs(...]
  transfers between devices with their start and end apart: 11 -> 10, of which waited for: 9 -> 9; matrix products, arithmetic and copies ran while one was open for 2% -> 1% of each run, Pallas kernels for 22% -> 23%
where the time goes in v3:
time: 78.3 us; the launch traced here: 78 us
  Pallas kernels  28.4 us (36%)
  starting transfers between devices  26.7 us (34%)
  waiting for transfers between devices  21.1 us (27%)
    all_to_all x3, starting transfers between devices, exchange(): lax.all_to_all(values, 'dp', split_axis=0, concat_axis=0, tiled=True, axi...  13.1 us
    all_to_all x3, waiting for transfers between devices, exchange(): lax.all_to_all(values, 'dp', split_axis=0, concat_axis=0, tiled=True, axi...  11.4 us
    pallas_call x1, Pallas kernels, delta_call(): pl.pallas_call(functools.partial(delta_kernel, sizes), grid=(columns // b...  8.75 us
    ppermute x3, starting transfers between devices, gathered(): lax.ppermute(parts[mirror * space_count + shift], ('dp', 'space'), pairs(...  5.97 us
    ppermute x3, starting transfers between devices, on_device(): lax.ppermute(back, ('dp', 'space'), pairs(mirror, shift))  5.94 us
    pallas_call x1, Pallas kernels, outer_call(): pl.pallas_call(outer_kernel, grid=(held,), in_specs=[whole((rows, channel...  4.89 us
    ppermute x1, waiting for transfers between devices, on_device(): lax.ppermute(input_parts[shift], ('dp', 'space'), pairs(0, shift))  4.24 us
    pallas_call x1, Pallas kernels, load_call(): pl.pallas_call(load_kernel, in_specs=[pl.BlockSpec(memory_space=pl.ANY)],...  3.47 us
  transfers between devices with their start and end apart: 10, of which 9 were waited for; matrix products, arithmetic and copies ran while one was open for 1% of the time, Pallas kernels for 23%

profile of v3, /device:TPU:0, one launch (start us, length us, event | category | flops | bytes accessed | tf_op | source)
XLA Modules:
  0.0 78.0 jit_solution(17221586489451363270)
XLA Ops:
  0.6 2.9 %input_x_sums.1 = bf16[80,32,128]{2,1,0:T(8,128)(2,1)} custom-call(bf16[256,32,128]{2,1,0:T(8,128)(2,1)} %bitcast.9, bf16[256,32,128]{2,1,0:T(8,128)(2,1)} %bitcast.10, bf16[256,32,128]{2,1,0:T(8,128)(2,1)} %bitcast.11, bf16[256,32,128]{2,1,0:T(8,128)(2,1)} %bitcast.12), custom_call_target="tpu_custom_call" | custom-call | flops 167772160 | bytes 4194304 | tf_op jit(solution)/shard_map/input_x_sums/pallas_call | solution.py:210
  3.5 5.2 %all-to-all-start.1 = ((bf16[8,320,128]{2,1,0:T(8,128)(2,1)}), bf16[8,320,128]{2,1,0:T(8,128)(2,1)S(1)}, u32[]{:S(2)}, u32[]{:S(2)}) async-start(bf16[8,320,128]{2,1,0:T(8,128)(2,1)} %bitcast.15), calls=%async_computation.1 | async-start | bytes 1310720 | tf_op jit(solution)/shard_map/all_to_all | solution.py:600
  8.8 8.7 %delta_and_x_sums.1 = (bf16[256,32,128]{2,1,0:T(8,128)(2,1)}, bf16[8,360,128]{2,1,0:T(8,128)(2,1)}) custom-call(bf16[256,32,128]{2,1,0:T(8,128)(2,1)} %bitcast.16, bf16[256,32,128]{2,1,0:T(8,128)(2,1)} %bitcast.17, bf16[256,32,128]{2,1,0:T(8,128)(2,1)} %bitcast.13), custom_call_target="tpu_custom_call" | custom-call | flops 335544320 | bytes 8388608 | tf_op jit(solution)/shard_map/delta_and_x_sums/pallas_call | solution.py:168
  17.5 1.5 %all-to-all-done.1.lines_ref = bf16[8,320,128]{2,1,0:T(8,128)(2,1)S(1)} async-done(((bf16[8,320,128]{2,1,0:T(8,128)(2,1)}), bf16[8,320,128]{2,1,0:T(8,128)(2,1)S(1)}, u32[]{:S(2)}, u32[]{:S(2)}) %all-to-all-start.1) | async-done | bytes 655392 | tf_op jit(solution)/shard_map/all_to_all | solution.py:600
  19.0 3.5 %all-to-all-start = ((bf16[8,360,128]{2,1,0:T(8,128)(2,1)}), bf16[8,360,128]{2,1,0:T(8,128)(2,1)S(1)}, u32[]{:S(2)}, u32[]{:S(2)}) async-start(bf16[8,360,128]{2,1,0:T(8,128)(2,1)} %get-tuple-element.29), calls=%async_computation | async-start | bytes 1474560 | tf_op jit(solution)/shard_map/all_to_all | solution.py:600
  24.0 1.6 %collective-permute-start = (bf16[512,128]{1,0:T(8,128)(2,1)S(1)}, bf16[512,128]{1,0:T(8,128)(2,1)S(1)}, u32[]{:S(2)}, u32[]{:S(2)}) collective-permute-start(bf16[512,128]{1,0:T(8,128)(2,1)S(1)} %get-tuple-element.31), channel_id=1, source_target_pairs={{0,1},{1,0},{2,3},{3,2},{4,5},{5,4},{6,7},{7,6},{8,9},{9,8},{10,11... | collective-permute-start | bytes 393224 | tf_op jit(solution)/shard_map/ppermute | solution.py:639
  25.6 4.2 %collective-permute-done.refs_1_ = bf16[512,128]{1,0:T(8,128)(2,1)S(1)} collective-permute-done((bf16[512,128]{1,0:T(8,128)(2,1)S(1)}, bf16[512,128]{1,0:T(8,128)(2,1)S(1)}, u32[]{:S(2)}, u32[]{:S(2)}) %collective-permute-start) | collective-permute-done | bytes 131104 | tf_op jit(solution)/shard_map/ppermute | solution.py:639
  29.9 3.7 %all-to-all-done.lines_ref = bf16[8,360,128]{2,1,0:T(8,128)(2,1)S(1)} async-done(((bf16[8,360,128]{2,1,0:T(8,128)(2,1)}), bf16[8,360,128]{2,1,0:T(8,128)(2,1)S(1)}, u32[]{:S(2)}, u32[]{:S(2)}) %all-to-all-start) | async-done | bytes 737312 | tf_op jit(solution)/shard_map/all_to_all | solution.py:600
  34.1 2.8 %collective-permute-start.2 = (bf16[552,128]{1,0:T(8,128)(2,1)S(1)}, bf16[552,128]{1,0:T(8,128)(2,1)S(1)}, u32[]{:S(2)}, u32[]{:S(2)}) collective-permute-start(bf16[552,128]{1,0:T(8,128)(2,1)S(1)} %get-tuple-element.41), channel_id=1, source_target_pairs={{0,30},{1,31},{2,28},{3,29},{4,26},{5,27},{6,24},{7,25},{8,22},{9,... | collective-permute-start | bytes 423944 | tf_op jit(solution)/shard_map/ppermute | solution.py:620
  36.9 2.7 %collective-permute-start.1 = (bf16[296,128]{1,0:T(8,128)(2,1)S(1)}, bf16[296,128]{1,0:T(8,128)(2,1)S(1)}, u32[]{:S(2)}, u32[]{:S(2)}) collective-permute-start(bf16[296,128]{1,0:T(8,128)(2,1)S(1)} %get-tuple-element.40), channel_id=1, source_target_pairs={{0,31},{1,30},{2,29},{3,28},{4,27},{5,26},{6,25},{7,24},{8,23},{9,... | collective-permute-start | bytes 227336 | tf_op jit(solution)/shard_map/ppermute | solution.py:620
  40.1 3.5 %weights_to_vmem.1 = bf16[4,2,16,2,128,128]{5,4,3,2,1,0:T(8,128)(2,1)S(1)} custom-call(bf16[4,2,16,2,128,128]{5,4,3,2,1,0:T(8,128)(2,1)} %bitcast.14), custom_call_target="tpu_custom_call" | custom-call | bytes 16777216 | tf_op jit(solution)/shard_map/weights_to_vmem/pallas_call | solution.py:307
  43.6 1.1 %collective-permute-done.1.refs_1_ = bf16[296,128]{1,0:T(8,128)(2,1)S(1)} collective-permute-done((bf16[296,128]{1,0:T(8,128)(2,1)S(1)}, bf16[296,128]{1,0:T(8,128)(2,1)S(1)}, u32[]{:S(2)}, u32[]{:S(2)}) %collective-permute-start.1) | collective-permute-done | bytes 75808 | tf_op jit(solution)/shard_map/ppermute | solution.py:620
  44.7 0.9 %collective-permute-done.3.refs_3_ = bf16[296,128]{1,0:T(8,128)(2,1)S(1)} collective-permute-done((bf16[296,128]{1,0:T(8,128)(2,1)S(1)}, bf16[296,128]{1,0:T(8,128)(2,1)S(1)}, u32[]{:S(2)}, u32[]{:S(2)}) %collective-permute-start.3) | collective-permute-done | bytes 75808 | tf_op jit(solution)/shard_map/ppermute | solution.py:620
  45.6 3.2 %mode_back.1 = (bf16[4,64,128]{2,1,0:T(8,128)(2,1)S(1)}, bf16[4,64,128]{2,1,0:T(8,128)(2,1)S(1)}, bf16[40,128]{1,0:T(8,128)(2,1)S(1)}) custom-call(f32[64,128]{1,0:T(8,128)S(1)} %broadcast_in_dim.35.scale_ref, bf16[4,32,2,128,128]{4,3,2,1,0:T(8,128)(2,1)S(1)} %bitcast.8, bf16[296,128]{1,0:T(8,128)(2,1)S(1)} %get-tuple-element.39.refs_0_, ...), custom_call_target="tpu_custom_call" | custom-call | flops 16777216 | bytes 8388608 | tf_op jit(solution)/shard_map/mode_back/pallas_call | solution.py:359
  48.8 2.7 %collective-permute-start.6 = (bf16[4,64,128]{2,1,0:T(8,128)(2,1)S(1)}, bf16[4,64,128]{2,1,0:T(8,128)(2,1)S(1)}, u32[]{:S(2)}, u32[]{:S(2)}) collective-permute-start(bf16[4,64,128]{2,1,0:T(8,128)(2,1)S(1)} %get-tuple-element.44.refs_0_), channel_id=1, source_target_pairs={{0,31},{1,30},{2,29},{3,28},{4,27},{5,26},{6,25},{7,24},{8,23},{9,... | collective-permute-start | bytes 196616 | tf_op jit(solution)/shard_map/ppermute | solution.py:655
  51.5 1.5 %collective-permute-start.5 = (bf16[4,64,128]{2,1,0:T(8,128)(2,1)S(1)}, bf16[4,64,128]{2,1,0:T(8,128)(2,1)S(1)}, u32[]{:S(2)}, u32[]{:S(2)}) collective-permute-start(bf16[4,64,128]{2,1,0:T(8,128)(2,1)S(1)} %get-tuple-element.44.refs_0_), channel_id=1, source_target_pairs={{0,30},{1,31},{2,28},{3,29},{4,26},{5,27},{6,24},{7,25},{8,22},{9,... | collective-permute-start | bytes 196616 | tf_op jit(solution)/shard_map/ppermute | solution.py:655
  53.1 1.7 %collective-permute-start.4 = (bf16[4,64,128]{2,1,0:T(8,128)(2,1)S(1)}, bf16[4,64,128]{2,1,0:T(8,128)(2,1)S(1)}, u32[]{:S(2)}, u32[]{:S(2)}) collective-permute-start(bf16[4,64,128]{2,1,0:T(8,128)(2,1)S(1)} %get-tuple-element.44.refs_0_), channel_id=1, source_target_pairs={{0,1},{1,0},{2,3},{3,2},{4,5},{5,4},{6,7},{7,6},{8,9},{9,8},{10,11... | collective-permute-start | bytes 196616 | tf_op jit(solution)/shard_map/ppermute | solution.py:655
  54.7 2.0 %collective-permute-done.6.refs_3_ = bf16[4,64,128]{2,1,0:T(8,128)(2,1)S(1)} collective-permute-done((bf16[4,64,128]{2,1,0:T(8,128)(2,1)S(1)}, bf16[4,64,128]{2,1,0:T(8,128)(2,1)S(1)}, u32[]{:S(2)}, u32[]{:S(2)}) %collective-permute-start.6) | collective-permute-done | bytes 65568 | tf_op jit(solution)/shard_map/ppermute | solution.py:655
  56.8 1.2 %collective-permute-done.5.refs_2_ = bf16[4,64,128]{2,1,0:T(8,128)(2,1)S(1)} collective-permute-done((bf16[4,64,128]{2,1,0:T(8,128)(2,1)S(1)}, bf16[4,64,128]{2,1,0:T(8,128)(2,1)S(1)}, u32[]{:S(2)}, u32[]{:S(2)}) %collective-permute-start.5) | collective-permute-done | bytes 65568 | tf_op jit(solution)/shard_map/ppermute | solution.py:655
  58.2 1.4 %y_inverse.1 = bf16[8,360,128]{2,1,0:T(8,128)(2,1)} custom-call(bf16[256,512]{1,0:T(8,128)(2,1)S(1)} %fusion.table_ref, bf16[40,128]{1,0:T(8,128)(2,1)S(1)} %get-tuple-element.43.share_ref, bf16[4,64,128]{2,1,0:T(8,128)(2,1)S(1)} %get-tuple-element.44.refs_0_, bf16[4,64,128]{2,1,0:T(8,128)(2,1)S(1)} %collective-permute-done.4.refs_1_, ...), custom_call_target="tpu_custom_call" | custom-call | flops 167772160 | bytes 1310720 | tf_op jit(solution)/shard_map/y_inverse/pallas_call | solution.py:465
  59.5 4.4 %all-to-all-start.2 = ((bf16[8,360,128]{2,1,0:T(8,128)(2,1)}), bf16[8,360,128]{2,1,0:T(8,128)(2,1)S(1)}, u32[]{:S(2)}, u32[]{:S(2)}) async-start(bf16[8,360,128]{2,1,0:T(8,128)(2,1)} %y_inverse.1), calls=%async_computation.2 | async-start | bytes 1474560 | tf_op jit(solution)/shard_map/all_to_all | solution.py:600
  63.9 4.9 %grad_spectral.1 = bf16[4,32,2,128,128]{4,3,2,1,0:T(8,128)(2,1)} custom-call(f32[64,128]{1,0:T(8,128)S(1)} %broadcast_in_dim.35.scale_ref, bf16[4,64,128]{2,1,0:T(8,128)(2,1)S(1)} %get-tuple-element.47.delta_ref, bf16[512,128]{1,0:T(8,128)(2,1)S(1)} %get-tuple-element.30.refs_0_, bf16[512,128]{1,0:T(8,128)(2,1)S(1)} %collective-permute-done.refs_1_, ...), custom_call_target="tpu_custom_call" | custom-call | flops 12582912 | bytes 8388608 | tf_op jit(solution)/shard_map/grad_spectral/pallas_call | solution.py:409
  68.8 6.2 %all-to-all-done.2.lines_ref = bf16[8,360,128]{2,1,0:T(8,128)(2,1)S(1)} async-done(((bf16[8,360,128]{2,1,0:T(8,128)(2,1)}), bf16[8,360,128]{2,1,0:T(8,128)(2,1)S(1)}, u32[]{:S(2)}, u32[]{:S(2)}) %all-to-all-start.2) | async-done | bytes 737312 | tf_op jit(solution)/shard_map/all_to_all | solution.py:600
  75.0 2.9 %x_inverse_and_local.1 = (bf16[256,32,128]{2,1,0:T(8,128)(2,1)}, f32[128,128]{1,0:T(8,128)}, f32[1,128]{1,0:T(1,128)}) custom-call(bf16[8,360,128]{2,1,0:T(8,128)(2,1)S(1)} %all-to-all-done.2.lines_ref, bf16[256,32,128]{2,1,0:T(8,128)(2,1)S(1)} %copy-done, bf16[128,128]{1,0:T(8,128)(2,1)S(1)} %copy-done.1), custom_call_target="tpu_custom_call" | custom-call | flops 436207616 | bytes 5242880 | tf_op jit(solution)/shard_map/x_inverse_and_local/pallas_call | solution.py:532
  (20 shorter events, 2.6 us)
Async XLA Ops:
  3.5 15.5 %all-to-all-start.1 = ((bf16[8,320,128]{2,1,0:T(8,128)(2,1)}), bf16[8,320,128]{2,1,0:T(8,128)(2,1)S(1)}, u32[]{:S(2)}, u32[]{:S(2)}) async-start(bf16[8,320,128]{2,1,0:T(8,128)(2,1)} %bitcast.15), calls=%async_computation.1 | async-start | bytes 1310720 | tf_op jit(solution)/shard_map/all_to_all | solution.py:600
  19.0 14.6 %all-to-all-start = ((bf16[8,360,128]{2,1,0:T(8,128)(2,1)}), bf16[8,360,128]{2,1,0:T(8,128)(2,1)S(1)}, u32[]{:S(2)}, u32[]{:S(2)}) async-start(bf16[8,360,128]{2,1,0:T(8,128)(2,1)} %get-tuple-element.29), calls=%async_computation | async-start | bytes 1474560 | tf_op jit(solution)/shard_map/all_to_all | solution.py:600
  24.0 5.8 %collective-permute-start = (bf16[512,128]{1,0:T(8,128)(2,1)S(1)}, bf16[512,128]{1,0:T(8,128)(2,1)S(1)}, u32[]{:S(2)}, u32[]{:S(2)}) collective-permute-start(bf16[512,128]{1,0:T(8,128)(2,1)S(1)} %get-tuple-element.31), channel_id=1, source_target_pairs={{0,1},{1,0},{2,3},{3,2},{4,5},{5,4},{6,7},{7,6},{8,9},{9,8},{10,11... | collective-permute-start | bytes 393224 | tf_op jit(solution)/shard_map/ppermute | solution.py:639
  34.1 11.5 %collective-permute-start.2 = (bf16[552,128]{1,0:T(8,128)(2,1)S(1)}, bf16[552,128]{1,0:T(8,128)(2,1)S(1)}, u32[]{:S(2)}, u32[]{:S(2)}) collective-permute-start(bf16[552,128]{1,0:T(8,128)(2,1)S(1)} %get-tuple-element.41), channel_id=1, source_target_pairs={{0,30},{1,31},{2,28},{3,29},{4,26},{5,27},{6,24},{7,25},{8,22},{9,... | collective-permute-start | bytes 423944 | tf_op jit(solution)/shard_map/ppermute | solution.py:620
  36.9 7.8 %collective-permute-start.1 = (bf16[296,128]{1,0:T(8,128)(2,1)S(1)}, bf16[296,128]{1,0:T(8,128)(2,1)S(1)}, u32[]{:S(2)}, u32[]{:S(2)}) collective-permute-start(bf16[296,128]{1,0:T(8,128)(2,1)S(1)} %get-tuple-element.40), channel_id=1, source_target_pairs={{0,31},{1,30},{2,29},{3,28},{4,27},{5,26},{6,25},{7,24},{8,23},{9,... | collective-permute-start | bytes 227336 | tf_op jit(solution)/shard_map/ppermute | solution.py:620
  39.6 6.0 %collective-permute-start.3 = (bf16[296,128]{1,0:T(8,128)(2,1)S(1)}, bf16[296,128]{1,0:T(8,128)(2,1)S(1)}, u32[]{:S(2)}, u32[]{:S(2)}) collective-permute-start(bf16[296,128]{1,0:T(8,128)(2,1)S(1)} %get-tuple-element.42), channel_id=1, source_target_pairs={{0,1},{1,0},{2,3},{3,2},{4,5},{5,4},{6,7},{7,6},{8,9},{9,8},{10,11... | collective-permute-start | bytes 227336 | tf_op jit(solution)/shard_map/ppermute | solution.py:620
  48.8 8.0 %collective-permute-start.6 = (bf16[4,64,128]{2,1,0:T(8,128)(2,1)S(1)}, bf16[4,64,128]{2,1,0:T(8,128)(2,1)S(1)}, u32[]{:S(2)}, u32[]{:S(2)}) collective-permute-start(bf16[4,64,128]{2,1,0:T(8,128)(2,1)S(1)} %get-tuple-element.44.refs_0_), channel_id=1, source_target_pairs={{0,31},{1,30},{2,29},{3,28},{4,27},{5,26},{6,25},{7,24},{8,23},{9,... | collective-permute-start | bytes 196616 | tf_op jit(solution)/shard_map/ppermute | solution.py:655
  51.5 6.5 %collective-permute-start.5 = (bf16[4,64,128]{2,1,0:T(8,128)(2,1)S(1)}, bf16[4,64,128]{2,1,0:T(8,128)(2,1)S(1)}, u32[]{:S(2)}, u32[]{:S(2)}) collective-permute-start(bf16[4,64,128]{2,1,0:T(8,128)(2,1)S(1)} %get-tuple-element.44.refs_0_), channel_id=1, source_target_pairs={{0,30},{1,31},{2,28},{3,29},{4,26},{5,27},{6,24},{7,25},{8,22},{9,... | collective-permute-start | bytes 196616 | tf_op jit(solution)/shard_map/ppermute | solution.py:655
  53.1 5.1 %collective-permute-start.4 = (bf16[4,64,128]{2,1,0:T(8,128)(2,1)S(1)}, bf16[4,64,128]{2,1,0:T(8,128)(2,1)S(1)}, u32[]{:S(2)}, u32[]{:S(2)}) collective-permute-start(bf16[4,64,128]{2,1,0:T(8,128)(2,1)S(1)} %get-tuple-element.44.refs_0_), channel_id=1, source_target_pairs={{0,1},{1,0},{2,3},{3,2},{4,5},{5,4},{6,7},{7,6},{8,9},{9,8},{10,11... | collective-permute-start | bytes 196616 | tf_op jit(solution)/shard_map/ppermute | solution.py:655
  59.5 15.5 %all-to-all-start.2 = ((bf16[8,360,128]{2,1,0:T(8,128)(2,1)}), bf16[8,360,128]{2,1,0:T(8,128)(2,1)S(1)}, u32[]{:S(2)}, u32[]{:S(2)}) async-start(bf16[8,360,128]{2,1,0:T(8,128)(2,1)} %y_inverse.1), calls=%async_computation.2 | async-start | bytes 1474560 | tf_op jit(solution)/shard_map/all_to_all | solution.py:600
  63.9 11.1 %copy-start = (bf16[256,32,128]{2,1,0:T(8,128)(2,1)S(1)}, bf16[256,32,128]{2,1,0:T(8,128)(2,1)}, u32[]{:S(2)}) copy-start(bf16[256,32,128]{2,1,0:T(8,128)(2,1)} %get-tuple-element.49.delta_ref) | copy-start | bytes 6291460
  63.9 11.1 %copy-start.1 = (bf16[128,128]{1,0:T(8,128)(2,1)S(1)}, bf16[128,128]{1,0:T(8,128)(2,1)}, u32[]{:S(2)}) copy-start(bf16[128,128]{1,0:T(8,128)(2,1)} %weight_ref.1) | copy-start | bytes 98308

commit v4 on v3

--- a/solution.py
+++ b/solution.py
@@ -44,7 +44,7 @@
     return jnp.where((turns == 1) | (turns == 2), -magnitude, magnitude).astype(bf16)
 
 
-def x_table(sizes, transposed=False):
+def x_table(sizes, transposed=False, relative=False):
     half, kx_local, slab_rows, grid_rows = sizes
     row_count = 2 * (kx_local + 1)
     upper = (lax.axis_index("dp") >= half).astype(jnp.int32)
@@ -57,6 +57,8 @@
     )
     member = sum((row >= i * row_count).astype(jnp.int32) for i in range(1, half))
     inner = row - member * row_count
+    if relative:
+        member = member ^ (lax.axis_index("dp") & (half - 1))
     ascending = member * kx_local + (inner >> 1)
     frequency = ascending + upper * (half * kx_local - 2 * ascending)
     quarter = grid_rows // 4
@@ -71,14 +73,20 @@
     return pl.BlockSpec(shape, lambda *_: (0,) * len(shape))
 
 
-def matrix_per_column(table, columns_of):
+def matrix_per_column(table, columns_of, rows=()):
     channels = columns_of[0].shape[1]
     results = []
+    totals = [0.0] * len(rows)
     for y in range(0, len(columns_of), 2):
         pair = jnp.concatenate(columns_of[y : y + 2], axis=1)
-        sums = jnp.dot(table, pair, preferred_element_type=f32).astype(bf16)
+        sums = jnp.dot(table, pair, preferred_element_type=f32)
+        totals = [total + sums[row : row + 1] for total, row in zip(totals, rows)]
+        sums = sums.astype(bf16)
         results += [sums[:, :channels], sums[:, channels:]]
-    return jnp.swapaxes(jnp.stack(results, axis=0), 0, 1)
+    results = jnp.swapaxes(jnp.stack(results, axis=0), 0, 1)
+    if rows:
+        return results, [total[:, :channels] + total[:, channels:] for total in totals]
+    return results
 
 
 def two_terms(values):
@@ -107,16 +115,35 @@
 
 
 def delta_kernel(
-    sizes, pre_ref, cot_ref, field_ref, delta_ref, out_ref, lines, local, bias, table
+    sizes,
+    pre_ref,
+    cot_ref,
+    field_ref,
+    delta_ref,
+    out_ref,
+    lines,
+    local,
+    bias,
+    table,
+    field,
+    semaphores,
 ):
     grid_rows, columns, channels = pre_ref.shape
     half = out_ref.shape[0]
     block = pl.program_id(0)
     all_columns = columns * pl.num_programs(0)
     step = 16
+    blocks = field.shape[0]
+
+    def arriving(i):
+        return pltpu.make_async_copy(
+            field_ref.at[:, pl.ds(i * columns, columns)], field.at[i], semaphores.at[i]
+        )
 
     @pl.when(block == 0)
     def _():
+        for i in range(blocks):
+            arriving(i).start()
         local[...] = jnp.zeros_like(local)
         bias[...] = jnp.zeros_like(bias)
         table[...] = x_table(sizes)
@@ -127,17 +154,26 @@
         delta = (cot_ref[rows].astype(f32) * slope).astype(bf16)
         delta_ref[rows] = delta
         lines[:, rows, :] = jnp.swapaxes(delta, 0, 1)
-        bias[...] += jnp.sum(delta.astype(f32).reshape(-1, 8, channels), axis=0)
         return carry
 
     lax.fori_loop(0, grid_rows // step, slab, 0, unroll=2)
+    sums, totals = matrix_per_column(
+        table[...], [lines[y] for y in range(columns)], (0, table.shape[0] - 2)
+    )
+    upper = lax.axis_index("dp") >= half
+    bias[...] += jnp.where(upper, totals[1], totals[0])
+    for i in range(blocks):
+
+        @pl.when(block == i)
+        def _(i=i):
+            arriving(i).wait()
+
     local[...] += lax.dot_general(
-        field_ref[...].reshape(grid_rows * columns, channels),
+        field[block].reshape(grid_rows * columns, channels),
         delta_ref[...].reshape(grid_rows * columns, channels),
         (((0,), (0,)), ((), ())),
         preferred_element_type=f32,
     )
-    sums = matrix_per_column(table[...], [lines[y] for y in range(columns)])
     per_target = sums.shape[0] // half
     first = pl.multiple_of(block * columns, columns)
     for target in range(half):
@@ -148,9 +184,8 @@
 
     @pl.when(block == pl.num_programs(0) - 1)
     def _():
-        upper = lax.axis_index("dp") >= half
         share = channels // half
-        total = jnp.sum(bias[...], axis=0, keepdims=True)
+        total = bias[...]
         for target in range(half):
             mine = local[target * share : (target + 1) * share]
             mirrored = local[(half - 1 - target) * share : (half - target) * share]
@@ -168,7 +203,7 @@
     return pl.pallas_call(
         functools.partial(delta_kernel, sizes),
         grid=(columns // block,),
-        in_specs=[field, field, field],
+        in_specs=[field, field, pl.BlockSpec(memory_space=pl.ANY)],
         out_specs=[field, whole(message)],
         out_shape=[
             jax.ShapeDtypeStruct(pre_act.shape, bf16),
@@ -177,8 +212,10 @@
         scratch_shapes=[
             pltpu.VMEM((block, grid_rows, channels), bf16),
             pltpu.VMEM((channels, channels), f32),
-            pltpu.VMEM((8, channels), f32),
+            pltpu.VMEM((1, channels), f32),
             pltpu.VMEM((rows, grid_rows), bf16),
+            pltpu.VMEM((columns // block, grid_rows, block, channels), bf16),
+            pltpu.SemaphoreType.DMA((columns // block,)),
         ],
         compiler_params=params(60),
         cost_estimate=pl.CostEstimate(
@@ -188,27 +225,37 @@
     )(pre_act, cotangent, field_in)
 
 
-def input_kernel(sizes, *refs):
-    field_refs, (out_ref, table) = refs[:-2], refs[-2:]
-
-    @pl.when(pl.program_id(0) == 0)
+def input_kernel(sizes, pieces, *refs):
+    field_refs, out_refs, table = refs[:pieces], refs[pieces:-1], refs[-1]
+    columns, channels = field_refs[0].shape[1:]
+    block = pl.program_id(0)
+    all_columns = columns * pl.num_programs(0)
+
+    @pl.when(block == 0)
     def _():
-        table[...] = x_table(sizes)
+        table[...] = x_table(sizes, relative=True)
 
     lines = [jnp.swapaxes(ref[...], 0, 1) for ref in field_refs]
-    out_ref[...] = matrix_per_column(
+    sums = matrix_per_column(
         table[...],
-        [jnp.concatenate([part[y] for part in lines], axis=0) for y in range(out_ref.shape[1])],
-    )
+        [jnp.concatenate([part[y] for part in lines], axis=0) for y in range(columns)],
+    )
+    first = pl.multiple_of(block * columns, columns)
+    rows = sums.shape[0] // len(out_refs)
+    for pair, out_ref in enumerate(out_refs):
+        for row in range(rows):
+            out_ref[pl.ds(row * all_columns + first, columns), :] = sums[pair * rows + row]
 
 
 def input_call(sizes, field_in):
     grid_rows, columns, channels = field_in.shape
-    rows = 2 * sizes[0] * (sizes[1] + 1)
+    half = sizes[0]
+    rows = 2 * half * (sizes[1] + 1)
     block = min(16, columns)
     pieces = 4
+    message = (2 * rows // half * columns, channels)
     return pl.pallas_call(
-        functools.partial(input_kernel, sizes),
+        functools.partial(input_kernel, sizes, pieces),
         grid=(columns // block,),
         in_specs=[
             pl.BlockSpec(
@@ -216,8 +263,8 @@
             )
             for piece in range(pieces)
         ],
-        out_specs=pl.BlockSpec((rows, block, channels), lambda i: (0, i, 0)),
-        out_shape=jax.ShapeDtypeStruct((rows, columns, channels), bf16),
+        out_specs=[whole(message)] * (half // 2),
+        out_shape=[jax.ShapeDtypeStruct(message, bf16)] * (half // 2),
         scratch_shapes=[pltpu.VMEM((rows, grid_rows), bf16)],
         compiler_params=params(60),
         cost_estimate=pl.CostEstimate(
@@ -227,9 +274,14 @@
     )(*[field_in] * pieces)
 
 
-def y_transform_kernel(columns, extra, blocks, tails, table_ref, lines_ref, *refs):
-    tail_refs, out_refs = refs[:tails], refs[tails:]
-    sources, total_rows, channels = lines_ref.shape
+def y_transform_kernel(columns, extra, blocks, total_rows, places, arrays, table_ref, *refs):
+    line_refs, out_refs = refs[:arrays], refs[arrays:]
+    sources, channels = len(places), line_refs[0].shape[-1]
+
+    def rows_of(source, first, last):
+        array, at = places[source]
+        return line_refs[array][at + first : at + last]
+
     frequencies = (total_rows - extra) // columns // 2
     own = blocks // 2
     size = table_ref.shape[0] // blocks
@@ -237,10 +289,9 @@
     for t in range(frequencies):
         lines = jnp.concatenate(
             [
-                lines_ref[:, row * columns : (row + 1) * columns].reshape(
-                    sources * columns, channels
-                )
+                rows_of(source, row * columns, (row + 1) * columns)
                 for row in (2 * t, 2 * t + 1)
+                for source in range(sources)
             ],
             axis=0,
         )
@@ -254,31 +305,32 @@
                 ]
     if extra:
         rows = channels // sources
-        pieces = [unpack_share(rows, lines_ref[i, total_rows - extra :]) for i in range(sources)]
+        pieces = [
+            unpack_share(rows, rows_of(i, total_rows - extra, total_rows)) for i in range(sources)
+        ]
         packed = pack_share(sum(p[0] for p in pieces), sum(p[1] for p in pieces))
         for out_ref in out_refs:
             out_ref[out_ref.shape[0] - extra :] = packed
-    for tail_ref in tail_refs:
-        rows = tail_ref.shape[0]
-        out_refs[own][rows : 2 * rows] = tail_ref[...]
-
-
-def y_transform_call(table, lines, blocks, outputs, columns, extra, tails=()):
-    sources, total_rows, channels = lines.shape
+
+
+def y_transform_call(table, lines, places, total_rows, blocks, outputs, columns, extra):
+    channels = lines[0].shape[-1]
     held = (total_rows - extra) // columns // 2 - 1
     size = table.shape[0] // blocks
-    out_rows = [blocks // outputs * held * size + extra] * outputs
-    for tail in tails:
-        out_rows[blocks // 2] += tail.shape[0]
+    rows = blocks // outputs * held * size + extra
     return pl.pallas_call(
-        functools.partial(y_transform_kernel, columns, extra, blocks, len(tails)),
-        out_shape=[jax.ShapeDtypeStruct((rows, channels), bf16) for rows in out_rows],
+        functools.partial(
+            y_transform_kernel, columns, extra, blocks, total_rows, places, len(lines)
+        ),
+        out_shape=[jax.ShapeDtypeStruct((rows, channels), bf16)] * outputs,
         compiler_params=params(),
         cost_estimate=pl.CostEstimate(
-            flops=2 * (held + 1) * table.size * channels, bytes_accessed=4 * lines.size, transcendentals=0
+            flops=2 * (held + 1) * table.size * channels,
+            bytes_accessed=4 * len(places) * total_rows * channels,
+            transcendentals=0,
         ),
         name="y_sums",
-    )(table, lines, *tails)
+    )(table, *lines)
 
 
 def turned(values):
@@ -576,7 +628,6 @@
     block, inner = row // size, row % size
     shift = block % space_count
     ky_index = (space_index + shift) % space_count * ky_local + inner // 2
-    positions = upper * half_cols + jnp.arange(half_cols, dtype=jnp.int32)
     quarter = grid_cols // 4
     cosine_turn = inner % 2
     sine_turn = jnp.where((block // space_count) == upper, 1 + inner % 2, 3 * (1 - inner % 2))
@@ -587,8 +638,13 @@
         ],
         axis=1,
     )
-    positions = jnp.concatenate([positions, positions])
-    y_table = cosine_table(ky_index[:, None] * positions[None, :] + quarter * turn, grid_cols)
+
+    def y_basis(flip):
+        column = jnp.arange(half_cols, dtype=jnp.int32)
+        member = (column // col_block) ^ flip
+        positions = upper * half_cols + member * col_block + column % col_block
+        positions = jnp.concatenate([positions, positions])
+        return cosine_table(ky_index[:, None] * positions[None, :] + quarter * turn, grid_cols)
 
     ky_row = space_index * ky_local + jnp.arange(size, dtype=jnp.int32) // 2
     scale = jnp.where(ky_row == 0, 1.0, 2.0).astype(f32) / (grid_rows * grid_cols)
@@ -628,12 +684,26 @@
     share = channels // half
     extra = extra_rows(channels, half)
 
-    input_sums = input_call(sizes, field_in[0])
-    input_lines = exchange(input_sums.reshape(half, row_count * col_block, channels))
+    message = row_count * col_block
+    y_table = y_basis(0)
+    input_table = y_basis(data_index % half)
+
+    chips = input_call(sizes, field_in[0])
+    arrived = [chips[0]]
+    for pair in range(1, half // 2):
+        moves = [(d, d ^ (2 * pair)) for d in range(data_count)]
+        arrived.append(lax.ppermute(chips[pair], "dp", moves))
     delta, delta_sums = delta_call(sizes, pre_act[0], cotangent[0], field_in[0])
+    delta_sums, arrived = tied((delta_sums, arrived))
     delta_lines = exchange(delta_sums)
+    mates = jnp.concatenate([part[message:] for part in arrived], axis=0)
+    arrived.append(lax.ppermute(mates, "dp", [(d, d ^ 1) for d in range(data_count)]))
+    places = [
+        (source // 2, 0) if source % 2 == 0 else (half // 2, source // 2 * message)
+        for source in range(half)
+    ]
     input_parts = list(
-        y_transform_call(y_table, input_lines, blocks, space_count, col_block, 0)
+        y_transform_call(input_table, arrived, places, message, blocks, space_count, col_block, 0)
     )
     for shift in range(1, space_count):
         input_parts[shift] = lax.ppermute(input_parts[shift], ("dp", "space"), pairs(0, shift))
@@ -641,15 +711,23 @@
     mirrored = sum(part[held_rows:].astype(f32) for part in input_parts).astype(bf16)
     delta_lines, mirrored = tied((delta_lines, mirrored))
 
+    message += extra
     delta_parts = y_transform_call(
-        y_table, delta_lines, blocks, blocks, col_block, extra, (mirrored,)
+        y_table,
+        [delta_lines.reshape(half * message, channels)],
+        [(0, source * message) for source in range(half)],
+        message,
+        blocks,
+        blocks,
+        col_block,
+        extra,
     )
     weight, delta_parts = tied((spec_weight, delta_parts))
     weight = load_call(weight)
     delta_held = gathered(delta_parts)
     input_held = [(part, 0) for part in input_parts]
-    input_held.append((delta_held[1 + order.index((1, 0))], kx_local))
     back, delta_owned, share_rows = back_call(scale_rows, weight, delta_held, share)
+    mirrored, back = tied((mirrored, back))
     received = {(0, 0): back}
     for mirror, shift in order:
         received[(mirror, -shift % space_count)] = lax.ppermute(
@@ -657,7 +735,9 @@
         )
     modes = [received[(mirror, shift)] for mirror in (0, 1) for shift in range(space_count)]
     column_sums = y_inverse_call(y_table, share_rows, modes, half, col_block)
-    column_sums, delta_owned = tied((column_sums, delta_owned))
+    mirrored = lax.ppermute(mirrored, ("dp", "space"), pairs(1, 0))
+    column_sums, delta_owned, mirrored = tied((column_sums, delta_owned, mirrored))
+    input_held.append((mirrored, 0))
     columns = exchange(column_sums)
     grad_spectral = outer_call(scale_rows, delta_owned, input_held)
     columns, grad_spectral = tied((columns, grad_spectral))

time: 78.3 us -> 76.1 us (0.972)
  waiting for transfers between devices: 21.1 us -> 16.8 us
  starting transfers between devices: 26.7 us -> 28.6 us
    ppermute x0 -> x5, starting transfers between devices: none -> 7.37 us  [the longest x3 4.52 us: on_device(): arrived.append(lax.ppermute(chips[pair], 'dp', moves))]
    all_to_all x3 -> x2, starting transfers between devices: 13.1 us -> 7.76 us  [exchange(): lax.all_to_all(values, 'dp', split_axis=0, concat_axis=0, tiled=True, axi...]
    all_to_all x3 -> x2, waiting for transfers between devices: 11.4 us -> 8.92 us  [exchange(): lax.all_to_all(values, 'dp', split_axis=0, concat_axis=0, tiled=True, axi...]
    ppermute x3, waiting for transfers between devices: 3.41 us -> 1.9 us  [on_device(): lax.ppermute(back, ('dp', 'space'), pairs(mirror, shift))]
    ppermute x3, waiting for transfers between devices: 2.01 us -> 0.88 us  [gathered(): lax.ppermute(parts[mirror * space_count + shift], ('dp', 'space'), pairs(...]
    ppermute x0 -> x5, waiting for transfers between devices: none -> 1.04 us  [the longest x1 1.03 us: on_device(): mirrored = lax.ppermute(mirrored, ('dp', 'space'), pairs(1, 0))]
  transfers between devices with their start and end apart: 10 -> 14, of which waited for: 9 -> 6; matrix products, arithmetic and copies ran while one was open for 1% -> 2% of each run, Pallas kernels for 23% -> 24%
where the time goes in v4:
time: 76.1 us; the launch traced here: 75.8 us
  starting transfers between devices  28.6 us (38%)
  Pallas kernels  27.9 us (37%)
  waiting for transfers between devices  16.8 us (22%)
  other arithmetic  1.37 us (2%)
  between operations  0.85 us (1%)
    all_to_all x2, waiting for transfers between devices, exchange(): lax.all_to_all(values, 'dp', split_axis=0, concat_axis=0, tiled=True, axi...  8.92 us
    pallas_call x1, Pallas kernels, delta_call(): pl.pallas_call(functools.partial(delta_kernel, sizes), grid=(columns // b...  8.03 us
    all_to_all x2, starting transfers between devices, exchange(): lax.all_to_all(values, 'dp', split_axis=0, concat_axis=0, tiled=True, axi...  7.76 us
    ppermute x3, starting transfers between devices, gathered(): lax.ppermute(parts[mirror * space_count + shift], ('dp', 'space'), pairs(...  5.97 us
    ppermute x3, starting transfers between devices, on_device(): lax.ppermute(back, ('dp', 'space'), pairs(mirror, shift))  5.94 us
    pallas_call x1, Pallas kernels, outer_call(): pl.pallas_call(outer_kernel, grid=(held,), in_specs=[whole((rows, channel...  4.9 us
    ppermute x3, starting transfers between devices, on_device(): arrived.append(lax.ppermute(chips[pair], 'dp', moves))  4.52 us
    ppermute x1, waiting for transfers between devices, on_device(): lax.ppermute(input_parts[shift], ('dp', 'space'), pairs(0, shift))  4.02 us
  transfers between devices with their start and end apart: 14, of which 6 were waited for; matrix products, arithmetic and copies ran while one was open for 2% of the time, Pallas kernels for 24%

profile of v4, /device:TPU:0, one launch (start us, length us, event | category | flops | bytes accessed | tf_op | source)
XLA Modules:
  0.0 75.8 jit_solution(9674083739305417964)
XLA Ops:
  0.6 3.1 %input_x_sums.1 = (bf16[640,128]{1,0:T(8,128)(2,1)}, bf16[640,128]{1,0:T(8,128)(2,1)}, bf16[640,128]{1,0:T(8,128)(2,1)}, bf16[640,128]{1,0:T(8,128)(2,1)}) custom-call(bf16[256,32,128]{2,1,0:T(8,128)(2,1)} %bitcast.10, bf16[256,32,128]{2,1,0:T(8,128)(2,1)} %bitcast.11, bf16[256,32,128]{2,1,0:T(8,128)(2,1)} %bitcast.12, bf16[256,32,128]{2,1,0:T(8,128)(2,1)} %bitcast.13), custom_call_target="tpu_custom_call" | custom-call | flops 167772160 | bytes 4194304 | tf_op jit(solution)/shard_map/input_x_sums/pallas_call | solution.py:257
  3.7 2.9 %collective-permute-start = (bf16[640,128]{1,0:T(8,128)(2,1)}, bf16[640,128]{1,0:T(8,128)(2,1)S(1)}, u32[]{:S(2)}, u32[]{:S(2)}) collective-permute-start(bf16[640,128]{1,0:T(8,128)(2,1)} %get-tuple-element.43), channel_id=1, source_target_pairs={{0,4},{2,6},{4,0},{6,2},{8,12},{10,14},{12,8},{14,10},{16,20},{18,... | collective-permute-start | bytes 491528 | tf_op jit(solution)/shard_map/ppermute | solution.py:695
  6.6 1.6 %collective-permute-start.1 = (bf16[640,128]{1,0:T(8,128)(2,1)}, bf16[640,128]{1,0:T(8,128)(2,1)S(1)}, u32[]{:S(2)}, u32[]{:S(2)}) collective-permute-start(bf16[640,128]{1,0:T(8,128)(2,1)} %get-tuple-element.44), channel_id=1, source_target_pairs={{0,8},{2,10},{4,12},{6,14},{8,0},{10,2},{12,4},{14,6},{16,24},{18,... | collective-permute-start | bytes 491528 | tf_op jit(solution)/shard_map/ppermute | solution.py:695
  8.3 8.0 %delta_and_x_sums.1 = (bf16[256,32,128]{2,1,0:T(8,128)(2,1)}, bf16[8,360,128]{2,1,0:T(8,128)(2,1)}) custom-call(bf16[256,32,128]{2,1,0:T(8,128)(2,1)} %bitcast.16, bf16[256,32,128]{2,1,0:T(8,128)(2,1)} %bitcast.17, bf16[256,32,128]{2,1,0:T(8,128)(2,1)} %bitcast.14), custom_call_target="tpu_custom_call" | custom-call | flops 335544320 | bytes 8388608 | tf_op jit(solution)/shard_map/delta_and_x_sums/pallas_call | solution.py:203
  16.3 4.2 %all-to-all-start = ((bf16[8,360,128]{2,1,0:T(8,128)(2,1)}), bf16[8,360,128]{2,1,0:T(8,128)(2,1)S(1)}, u32[]{:S(2)}, u32[]{:S(2)}) async-start(bf16[8,360,128]{2,1,0:T(8,128)(2,1)} %get-tuple-element.46), calls=%async_computation | async-start | bytes 1474560 | tf_op jit(solution)/shard_map/all_to_all | solution.py:656
  21.5 1.3 %fusion.1 = (bf16[256,512]{1,0:T(8,128)(2,1)S(1)}, bf16[256,512]{1,0:T(8,128)(2,1)S(1)}) fusion(s32[256,256]{1,0:T(8,128)S(1)} %broadcast_in_dim.17, s32[256,256]{1,0:T(8,128)S(1)} %broadcast_in_dim.16, s32[512]{0:T(512)S(1)} %pad_add_fusion.1, s32[256]{0:T(256)S(1)} %fusion.23, s32[512]{0:T(512)S(1)} %pad_add_fusion), kind=kLoop, calls=%fused_computation.3 | loop fusion | flops 9699328 | bytes 1053696 | tf_op jit(solution)/shard_map/convert_element_type | solution.py:44
  23.3 1.6 %collective-permute-start.4 = (bf16[512,128]{1,0:T(8,128)(2,1)S(1)}, bf16[512,128]{1,0:T(8,128)(2,1)S(1)}, u32[]{:S(2)}, u32[]{:S(2)}) collective-permute-start(bf16[512,128]{1,0:T(8,128)(2,1)S(1)} %get-tuple-element.52), channel_id=1, source_target_pairs={{0,1},{1,0},{2,3},{3,2},{4,5},{5,4},{6,7},{7,6},{8,9},{9,8},{10,11... | collective-permute-start | bytes 393224 | tf_op jit(solution)/shard_map/ppermute | solution.py:709
  24.8 4.0 %collective-permute-done.4.refs_1_ = bf16[512,128]{1,0:T(8,128)(2,1)S(1)} collective-permute-done((bf16[512,128]{1,0:T(8,128)(2,1)S(1)}, bf16[512,128]{1,0:T(8,128)(2,1)S(1)}, u32[]{:S(2)}, u32[]{:S(2)}) %collective-permute-start.4) | collective-permute-done | bytes 131104 | tf_op jit(solution)/shard_map/ppermute | solution.py:709
  28.9 2.8 %all-to-all-done = bf16[8,360,128]{2,1,0:T(8,128)(2,1)S(1)} async-done(((bf16[8,360,128]{2,1,0:T(8,128)(2,1)}), bf16[8,360,128]{2,1,0:T(8,128)(2,1)S(1)}, u32[]{:S(2)}, u32[]{:S(2)}) %all-to-all-start) | async-done | bytes 737312 | tf_op jit(solution)/shard_map/all_to_all | solution.py:656
  32.2 3.8 %collective-permute-start.5 = (bf16[296,128]{1,0:T(8,128)(2,1)S(1)}, bf16[296,128]{1,0:T(8,128)(2,1)S(1)}, u32[]{:S(2)}, u32[]{:S(2)}) collective-permute-start(bf16[296,128]{1,0:T(8,128)(2,1)S(1)} %get-tuple-element.60), channel_id=1, source_target_pairs={{0,31},{1,30},{2,29},{3,28},{4,27},{5,26},{6,25},{7,24},{8,23},{9,... | collective-permute-start | bytes 227336 | tf_op jit(solution)/shard_map/ppermute | solution.py:676
  35.9 1.7 %collective-permute-start.6 = (bf16[296,128]{1,0:T(8,128)(2,1)S(1)}, bf16[296,128]{1,0:T(8,128)(2,1)S(1)}, u32[]{:S(2)}, u32[]{:S(2)}) collective-permute-start(bf16[296,128]{1,0:T(8,128)(2,1)S(1)} %get-tuple-element.61), channel_id=1, source_target_pairs={{0,30},{1,31},{2,28},{3,29},{4,26},{5,27},{6,24},{7,25},{8,22},{9,... | collective-permute-start | bytes 227336 | tf_op jit(solution)/shard_map/ppermute | solution.py:676
  38.2 3.5 %weights_to_vmem.1 = bf16[4,2,16,2,128,128]{5,4,3,2,1,0:T(8,128)(2,1)S(1)} custom-call(bf16[4,2,16,2,128,128]{5,4,3,2,1,0:T(8,128)(2,1)} %bitcast.15), custom_call_target="tpu_custom_call" | custom-call | bytes 16777216 | tf_op jit(solution)/shard_map/weights_to_vmem/pallas_call | solution.py:359
  42.6 3.2 %mode_back.1 = (bf16[4,64,128]{2,1,0:T(8,128)(2,1)S(1)}, bf16[4,64,128]{2,1,0:T(8,128)(2,1)S(1)}, bf16[40,128]{1,0:T(8,128)(2,1)S(1)}) custom-call(f32[64,128]{1,0:T(8,128)S(1)} %broadcast_in_dim.20.scale_ref, bf16[4,32,2,128,128]{4,3,2,1,0:T(8,128)(2,1)S(1)} %bitcast.8, bf16[296,128]{1,0:T(8,128)(2,1)S(1)} %get-tuple-element.59.refs_0_, ...), custom_call_target="tpu_custom_call" | custom-call | flops 16777216 | bytes 8388608 | tf_op jit(solution)/shard_map/mode_back/pallas_call | solution.py:411
  45.8 3.6 %collective-permute-start.10 = (bf16[4,64,128]{2,1,0:T(8,128)(2,1)S(1)}, bf16[4,64,128]{2,1,0:T(8,128)(2,1)S(1)}, u32[]{:S(2)}, u32[]{:S(2)}) collective-permute-start(bf16[4,64,128]{2,1,0:T(8,128)(2,1)S(1)} %get-tuple-element.66.refs_0_), channel_id=1, source_target_pairs={{0,31},{1,30},{2,29},{3,28},{4,27},{5,26},{6,25},{7,24},{8,23},{9,... | collective-permute-start | bytes 196616 | tf_op jit(solution)/shard_map/ppermute | solution.py:733
  49.3 1.3 %collective-permute-start.9 = (bf16[4,64,128]{2,1,0:T(8,128)(2,1)S(1)}, bf16[4,64,128]{2,1,0:T(8,128)(2,1)S(1)}, u32[]{:S(2)}, u32[]{:S(2)}) collective-permute-start(bf16[4,64,128]{2,1,0:T(8,128)(2,1)S(1)} %get-tuple-element.66.refs_0_), channel_id=1, source_target_pairs={{0,30},{1,31},{2,28},{3,29},{4,26},{5,27},{6,24},{7,25},{8,22},{9,... | collective-permute-start | bytes 196616 | tf_op jit(solution)/shard_map/ppermute | solution.py:733
  50.7 1.0 %collective-permute-start.8 = (bf16[4,64,128]{2,1,0:T(8,128)(2,1)S(1)}, bf16[4,64,128]{2,1,0:T(8,128)(2,1)S(1)}, u32[]{:S(2)}, u32[]{:S(2)}) collective-permute-start(bf16[4,64,128]{2,1,0:T(8,128)(2,1)S(1)} %get-tuple-element.66.refs_0_), channel_id=1, source_target_pairs={{0,1},{1,0},{2,3},{3,2},{4,5},{5,4},{6,7},{7,6},{8,9},{9,8},{10,11... | collective-permute-start | bytes 196616 | tf_op jit(solution)/shard_map/ppermute | solution.py:733
  51.7 2.3 %collective-permute-start.11 = (bf16[256,128]{1,0:T(8,128)(2,1)S(1)}, bf16[256,128]{1,0:T(8,128)(2,1)S(1)}, u32[]{:S(2)}, u32[]{:S(2)}) collective-permute-start(bf16[256,128]{1,0:T(8,128)(2,1)S(1)} %add_convert_fusion), channel_id=1, source_target_pairs={{0,30},{1,31},{2,28},{3,29},{4,26},{5,27},{6,24},{7,25},{8,22},{9,... | collective-permute-start | bytes 196616 | tf_op jit(solution)/shard_map/ppermute | solution.py:738
  54.0 1.9 %collective-permute-done.9.refs_2_ = bf16[4,64,128]{2,1,0:T(8,128)(2,1)S(1)} collective-permute-done((bf16[4,64,128]{2,1,0:T(8,128)(2,1)S(1)}, bf16[4,64,128]{2,1,0:T(8,128)(2,1)S(1)}, u32[]{:S(2)}, u32[]{:S(2)}) %collective-permute-start.9) | collective-permute-done | bytes 65568 | tf_op jit(solution)/shard_map/ppermute | solution.py:733
  55.9 1.3 %y_inverse.1 = bf16[8,360,128]{2,1,0:T(8,128)(2,1)} custom-call(bf16[256,512]{1,0:T(8,128)(2,1)S(1)} %get-tuple-element.79.table_ref, bf16[40,128]{1,0:T(8,128)(2,1)S(1)} %get-tuple-element.63.share_ref, bf16[4,64,128]{2,1,0:T(8,128)(2,1)S(1)} %get-tuple-element.66.refs_0_, bf16[4,64,128]{2,1,0:T(8,128)(2,1)S(1)} %collective-permute-done.8.refs_1_, ...), custom_call_target="tpu_custom_call" | custom-call | flops 167772160 | bytes 1310720 | tf_op jit(solution)/shard_map/y_inverse/pallas_call | solution.py:517
  57.3 1.0 %collective-permute-done.11.refs_2_ = bf16[256,128]{1,0:T(8,128)(2,1)S(1)} collective-permute-done((bf16[256,128]{1,0:T(8,128)(2,1)S(1)}, bf16[256,128]{1,0:T(8,128)(2,1)S(1)}, u32[]{:S(2)}, u32[]{:S(2)}) %collective-permute-start.11) | collective-permute-done | bytes 65568 | tf_op jit(solution)/shard_map/ppermute | solution.py:738
  58.3 3.5 %all-to-all-start.1 = ((bf16[8,360,128]{2,1,0:T(8,128)(2,1)}), bf16[8,360,128]{2,1,0:T(8,128)(2,1)S(1)}, u32[]{:S(2)}, u32[]{:S(2)}) async-start(bf16[8,360,128]{2,1,0:T(8,128)(2,1)} %y_inverse.1), calls=%async_computation.1 | async-start | bytes 1474560 | tf_op jit(solution)/shard_map/all_to_all | solution.py:656
  61.9 4.9 %grad_spectral.1 = bf16[4,32,2,128,128]{4,3,2,1,0:T(8,128)(2,1)} custom-call(f32[64,128]{1,0:T(8,128)S(1)} %broadcast_in_dim.20.scale_ref, bf16[4,64,128]{2,1,0:T(8,128)(2,1)S(1)} %get-tuple-element.70.delta_ref, bf16[512,128]{1,0:T(8,128)(2,1)S(1)} %get-tuple-element.51.refs_0_, bf16[512,128]{1,0:T(8,128)(2,1)S(1)} %collective-permute-done.4.refs_1_, ...), custom_call_target="tpu_custom_call" | custom-call | flops 12582912 | bytes 8388608 | tf_op jit(solution)/shard_map/grad_spectral/pallas_call | solution.py:461
  66.8 6.1 %all-to-all-done.1.lines_ref = bf16[8,360,128]{2,1,0:T(8,128)(2,1)S(1)} async-done(((bf16[8,360,128]{2,1,0:T(8,128)(2,1)}), bf16[8,360,128]{2,1,0:T(8,128)(2,1)S(1)}, u32[]{:S(2)}, u32[]{:S(2)}) %all-to-all-start.1) | async-done | bytes 737312 | tf_op jit(solution)/shard_map/all_to_all | solution.py:656
  72.9 2.9 %x_inverse_and_local.1 = (bf16[256,32,128]{2,1,0:T(8,128)(2,1)}, f32[128,128]{1,0:T(8,128)}, f32[1,128]{1,0:T(1,128)}) custom-call(bf16[8,360,128]{2,1,0:T(8,128)(2,1)S(1)} %all-to-all-done.1.lines_ref, bf16[256,32,128]{2,1,0:T(8,128)(2,1)S(1)} %copy-done, bf16[128,128]{1,0:T(8,128)(2,1)S(1)} %copy-done.2), custom_call_target="tpu_custom_call" | custom-call | flops 436207616 | bytes 5242880 | tf_op jit(solution)/shard_map/x_inverse_and_local/pallas_call | solution.py:584
  (36 shorter events, 3.4 us)
Async XLA Ops:
  3.7 12.6 %collective-permute-start = (bf16[640,128]{1,0:T(8,128)(2,1)}, bf16[640,128]{1,0:T(8,128)(2,1)S(1)}, u32[]{:S(2)}, u32[]{:S(2)}) collective-permute-start(bf16[640,128]{1,0:T(8,128)(2,1)} %get-tuple-element.43), channel_id=1, source_target_pairs={{0,4},{2,6},{4,0},{6,2},{8,12},{10,14},{12,8},{14,10},{16,20},{18,... | collective-permute-start | bytes 491528 | tf_op jit(solution)/shard_map/ppermute | solution.py:695
  6.6 9.7 %collective-permute-start.1 = (bf16[640,128]{1,0:T(8,128)(2,1)}, bf16[640,128]{1,0:T(8,128)(2,1)S(1)}, u32[]{:S(2)}, u32[]{:S(2)}) collective-permute-start(bf16[640,128]{1,0:T(8,128)(2,1)} %get-tuple-element.44), channel_id=1, source_target_pairs={{0,8},{2,10},{4,12},{6,14},{8,0},{10,2},{12,4},{14,6},{16,24},{18,... | collective-permute-start | bytes 491528 | tf_op jit(solution)/shard_map/ppermute | solution.py:695
  8.2 8.1 %collective-permute-start.2 = (bf16[640,128]{1,0:T(8,128)(2,1)}, bf16[640,128]{1,0:T(8,128)(2,1)S(1)}, u32[]{:S(2)}, u32[]{:S(2)}) collective-permute-start(bf16[640,128]{1,0:T(8,128)(2,1)} %get-tuple-element.45), channel_id=1, source_target_pairs={{0,12},{2,14},{4,8},{6,10},{8,4},{10,6},{12,0},{14,2},{16,28},{18,... | collective-permute-start | bytes 491528 | tf_op jit(solution)/shard_map/ppermute | solution.py:695
  8.3 12.4 %copy-start.1 = (bf16[640,128]{1,0:T(8,128)(2,1)S(1)}, bf16[640,128]{1,0:T(8,128)(2,1)}, u32[]{:S(2)}) copy-start(bf16[640,128]{1,0:T(8,128)(2,1)} %get-tuple-element.47.refs_0_) | copy-start | bytes 491524
  16.3 15.3 %all-to-all-start = ((bf16[8,360,128]{2,1,0:T(8,128)(2,1)}), bf16[8,360,128]{2,1,0:T(8,128)(2,1)S(1)}, u32[]{:S(2)}, u32[]{:S(2)}) async-start(bf16[8,360,128]{2,1,0:T(8,128)(2,1)} %get-tuple-element.46), calls=%async_computation | async-start | bytes 1474560 | tf_op jit(solution)/shard_map/all_to_all | solution.py:656
  20.7 2.0 %collective-permute-start.3 = (bf16[1280,128]{1,0:T(8,128)(2,1)S(1)}, bf16[1280,128]{1,0:T(8,128)(2,1)S(1)}, u32[]{:S(2)}, u32[]{:S(2)}) collective-permute-start(bf16[1280,128]{1,0:T(8,128)(2,1)S(1)} %pad_maximum_fusion), channel_id=1, source_target_pairs={{0,2},{2,0},{4,6},{6,4},{8,10},{10,8},{12,14},{14,12},{16,18},{18,... | collective-permute-start | bytes 983048 | tf_op jit(solution)/shard_map/ppermute | solution.py:700
  23.3 5.6 %collective-permute-start.4 = (bf16[512,128]{1,0:T(8,128)(2,1)S(1)}, bf16[512,128]{1,0:T(8,128)(2,1)S(1)}, u32[]{:S(2)}, u32[]{:S(2)}) collective-permute-start(bf16[512,128]{1,0:T(8,128)(2,1)S(1)} %get-tuple-element.52), channel_id=1, source_target_pairs={{0,1},{1,0},{2,3},{3,2},{4,5},{5,4},{6,7},{7,6},{8,9},{9,8},{10,11... | collective-permute-start | bytes 393224 | tf_op jit(solution)/shard_map/ppermute | solution.py:709
  32.2 9.5 %collective-permute-start.5 = (bf16[296,128]{1,0:T(8,128)(2,1)S(1)}, bf16[296,128]{1,0:T(8,128)(2,1)S(1)}, u32[]{:S(2)}, u32[]{:S(2)}) collective-permute-start(bf16[296,128]{1,0:T(8,128)(2,1)S(1)} %get-tuple-element.60), channel_id=1, source_target_pairs={{0,31},{1,30},{2,29},{3,28},{4,27},{5,26},{6,25},{7,24},{8,23},{9,... | collective-permute-start | bytes 227336 | tf_op jit(solution)/shard_map/ppermute | solution.py:676
  35.9 6.6 %collective-permute-start.6 = (bf16[296,128]{1,0:T(8,128)(2,1)S(1)}, bf16[296,128]{1,0:T(8,128)(2,1)S(1)}, u32[]{:S(2)}, u32[]{:S(2)}) collective-permute-start(bf16[296,128]{1,0:T(8,128)(2,1)S(1)} %get-tuple-element.61), channel_id=1, source_target_pairs={{0,30},{1,31},{2,28},{3,29},{4,26},{5,27},{6,24},{7,25},{8,22},{9,... | collective-permute-start | bytes 227336 | tf_op jit(solution)/shard_map/ppermute | solution.py:676
  37.6 4.9 %collective-permute-start.7 = (bf16[296,128]{1,0:T(8,128)(2,1)S(1)}, bf16[296,128]{1,0:T(8,128)(2,1)S(1)}, u32[]{:S(2)}, u32[]{:S(2)}) collective-permute-start(bf16[296,128]{1,0:T(8,128)(2,1)S(1)} %get-tuple-element.62), channel_id=1, source_target_pairs={{0,1},{1,0},{2,3},{3,2},{4,5},{5,4},{6,7},{7,6},{8,9},{9,8},{10,11... | collective-permute-start | bytes 227336 | tf_op jit(solution)/shard_map/ppermute | solution.py:676
  45.8 8.2 %collective-permute-start.10 = (bf16[4,64,128]{2,1,0:T(8,128)(2,1)S(1)}, bf16[4,64,128]{2,1,0:T(8,128)(2,1)S(1)}, u32[]{:S(2)}, u32[]{:S(2)}) collective-permute-start(bf16[4,64,128]{2,1,0:T(8,128)(2,1)S(1)} %get-tuple-element.66.refs_0_), channel_id=1, source_target_pairs={{0,31},{1,30},{2,29},{3,28},{4,27},{5,26},{6,25},{7,24},{8,23},{9,... | collective-permute-start | bytes 196616 | tf_op jit(solution)/shard_map/ppermute | solution.py:733
  49.3 6.6 %collective-permute-start.9 = (bf16[4,64,128]{2,1,0:T(8,128)(2,1)S(1)}, bf16[4,64,128]{2,1,0:T(8,128)(2,1)S(1)}, u32[]{:S(2)}, u32[]{:S(2)}) collective-permute-start(bf16[4,64,128]{2,1,0:T(8,128)(2,1)S(1)} %get-tuple-element.66.refs_0_), channel_id=1, source_target_pairs={{0,30},{1,31},{2,28},{3,29},{4,26},{5,27},{6,24},{7,25},{8,22},{9,... | collective-permute-start | bytes 196616 | tf_op jit(solution)/shard_map/ppermute | solution.py:733
  50.7 5.2 %collective-permute-start.8 = (bf16[4,64,128]{2,1,0:T(8,128)(2,1)S(1)}, bf16[4,64,128]{2,1,0:T(8,128)(2,1)S(1)}, u32[]{:S(2)}, u32[]{:S(2)}) collective-permute-start(bf16[4,64,128]{2,1,0:T(8,128)(2,1)S(1)} %get-tuple-element.66.refs_0_), channel_id=1, source_target_pairs={{0,1},{1,0},{2,3},{3,2},{4,5},{5,4},{6,7},{7,6},{8,9},{9,8},{10,11... | collective-permute-start | bytes 196616 | tf_op jit(solution)/shard_map/ppermute | solution.py:733
  51.7 6.6 %collective-permute-start.11 = (bf16[256,128]{1,0:T(8,128)(2,1)S(1)}, bf16[256,128]{1,0:T(8,128)(2,1)S(1)}, u32[]{:S(2)}, u32[]{:S(2)}) collective-permute-start(bf16[256,128]{1,0:T(8,128)(2,1)S(1)} %add_convert_fusion), channel_id=1, source_target_pairs={{0,30},{1,31},{2,28},{3,29},{4,26},{5,27},{6,24},{7,25},{8,22},{9,... | collective-permute-start | bytes 196616 | tf_op jit(solution)/shard_map/ppermute | solution.py:738
  58.3 14.6 %all-to-all-start.1 = ((bf16[8,360,128]{2,1,0:T(8,128)(2,1)}), bf16[8,360,128]{2,1,0:T(8,128)(2,1)S(1)}, u32[]{:S(2)}, u32[]{:S(2)}) async-start(bf16[8,360,128]{2,1,0:T(8,128)(2,1)} %y_inverse.1), calls=%async_computation.1 | async-start | bytes 1474560 | tf_op jit(solution)/shard_map/all_to_all | solution.py:656
  61.8 11.0 %copy-start = (bf16[256,32,128]{2,1,0:T(8,128)(2,1)S(1)}, bf16[256,32,128]{2,1,0:T(8,128)(2,1)}, u32[]{:S(2)}) copy-start(bf16[256,32,128]{2,1,0:T(8,128)(2,1)} %get-tuple-element.73.delta_ref) | copy-start | bytes 6291460
  61.8 11.0 %copy-start.2 = (bf16[128,128]{1,0:T(8,128)(2,1)S(1)}, bf16[128,128]{1,0:T(8,128)(2,1)}, u32[]{:S(2)}) copy-start(bf16[128,128]{1,0:T(8,128)(2,1)} %weight_ref.1) | copy-start | bytes 98308

commit v5 on v4

--- a/solution.py
+++ b/solution.py
@@ -112,6 +112,17 @@
     share = message[:rows] + message[rows : 2 * rows]
     bias = message[2 * rows : 2 * rows + 1] + message[2 * rows + 1 : 2 * rows + 2]
     return share, bias
+
+
+def in_relative_order(pieces, half):
+    place = lax.axis_index("dp")
+    key = jnp.where(place >= half, 2 * half - 1 - place, place)
+    step = 1
+    while step < half:
+        flag = (key & step) != 0
+        pieces = [jnp.where(flag, pieces[i ^ step], pieces[i]) for i in range(half)]
+        step *= 2
+    return pieces
 
 
 def delta_kernel(
@@ -478,12 +489,14 @@
     )(scale_rows, delta, *[part for part, _ in parts])
 
 
-def y_inverse_kernel(columns, table_ref, share_ref, *refs):
-    part_refs, out_ref = refs[:-1], refs[-1]
-    targets, total_rows, channels = out_ref.shape
+def y_inverse_kernel(columns, parts, table_ref, share_ref, *refs):
+    part_refs, out_refs = refs[:parts], refs[parts:]
+    channels = share_ref.shape[1]
     extra = share_ref.shape[0]
-    frequencies = (total_rows - extra) // columns // 2
-    own = len(part_refs) // 2
+    message = out_refs[0].shape[0] // 2
+    targets = 2 * len(out_refs)
+    frequencies = (message - extra) // columns // 2
+    own = parts // 2
     size = part_refs[0].shape[1]
     table = table_ref[...]
     for t in range(frequencies):
@@ -503,22 +516,24 @@
             preferred_element_type=f32,
         ).astype(bf16)
         for part in range(2):
-            row = 2 * t + part
-            out_ref[:, row * columns : (row + 1) * columns] = sums[
-                part * targets * columns : (part + 1) * targets * columns
-            ].reshape(targets, columns, channels)
+            for target in range(targets):
+                at = target % 2 * message + (2 * t + part) * columns
+                piece = part * targets + target
+                out_refs[target // 2][at : at + columns] = sums[
+                    piece * columns : (piece + 1) * columns
+                ]
     for target in range(targets):
-        out_ref[target, total_rows - extra :] = share_ref[...]
+        last = (target % 2 + 1) * message
+        out_refs[target // 2][last - extra : last] = share_ref[...]
 
 
 def y_inverse_call(table, share, parts, targets, columns):
     held, size, channels = parts[0].shape
     rows = 2 * (held + 1)
+    message = (2 * (rows * columns + share.shape[0]), channels)
     return pl.pallas_call(
-        functools.partial(y_inverse_kernel, columns),
-        out_shape=jax.ShapeDtypeStruct(
-            (targets, rows * columns + share.shape[0], channels), bf16
-        ),
+        functools.partial(y_inverse_kernel, columns, len(parts)),
+        out_shape=[jax.ShapeDtypeStruct(message, bf16)] * (targets // 2),
         compiler_params=params(),
         cost_estimate=pl.CostEstimate(
             flops=rows * table.size * channels,
@@ -529,11 +544,11 @@
     )(table, share, *parts)
 
 
-def final_kernel(
-    sizes, lines_ref, delta_ref, weight_ref, out_ref, local_ref, bias_ref, table
-):
+def final_kernel(sizes, places, arrays, *refs):
+    line_refs, refs = refs[:arrays], refs[arrays:]
+    delta_ref, weight_ref, out_ref, local_ref, bias_ref, table = refs
     grid_rows, columns, channels = out_ref.shape
-    half = lines_ref.shape[0]
+    half = len(places)
     block = pl.program_id(0)
     all_columns = columns * pl.num_programs(0)
     per_source = table.shape[1] // half
@@ -541,12 +556,12 @@
 
     @pl.when(block == 0)
     def _():
-        table[...] = x_table(sizes, transposed=True)
+        table[...] = x_table(sizes, transposed=True, relative=True)
 
     lines = jnp.stack(
         [
-            lines_ref[source, pl.ds(row * all_columns + first, columns), :]
-            for source in range(half)
+            line_refs[array][pl.ds(at + row * all_columns + first, columns), :]
+            for array, at in places
             for row in range(per_source)
         ],
         axis=0,
@@ -563,32 +578,26 @@
 
     @pl.when(block == 0)
     def _():
-        upper = lax.axis_index("dp") >= half
         share = channels // half
-        pieces = [
-            unpack_share(share, lines_ref[source, per_source * all_columns :])
-            for source in range(half)
-        ]
-        for source in range(half):
-            local_ref[source * share : (source + 1) * share] = jnp.where(
-                upper, pieces[half - 1 - source][0], pieces[source][0]
-            )
+        extra = extra_rows(channels, half)
+        pieces = []
+        for array, at in places:
+            begin = at + per_source * all_columns
+            pieces.append(unpack_share(share, line_refs[array][begin : begin + extra]))
+        for source, rows in enumerate(in_relative_order([piece[0] for piece in pieces], half)):
+            local_ref[source * share : (source + 1) * share] = rows
         bias_ref[...] = pieces[0][1]
 
 
-def final_call(sizes, lines, delta, local_weight):
+def final_call(sizes, lines, places, delta, local_weight):
     grid_rows, columns, channels = delta.shape
     rows = 2 * sizes[0] * (sizes[1] + 1)
     block = min(16, columns)
     field = pl.BlockSpec((grid_rows, block, channels), lambda i: (0, i, 0))
     return pl.pallas_call(
-        functools.partial(final_kernel, sizes),
+        functools.partial(final_kernel, sizes, places, len(lines)),
         grid=(columns // block,),
-        in_specs=[
-            whole(lines.shape),
-            field,
-            whole(local_weight.shape),
-        ],
+        in_specs=[whole(line.shape) for line in lines] + [field, whole(local_weight.shape)],
         out_specs=[field, whole((channels, channels)), whole((1, channels))],
         out_shape=[
             jax.ShapeDtypeStruct(delta.shape, bf16),
@@ -598,12 +607,10 @@
         scratch_shapes=[pltpu.VMEM((grid_rows, rows), bf16)],
         compiler_params=params(),
         cost_estimate=pl.CostEstimate(
-            flops=2 * (rows + channels) * delta.size,
-            bytes_accessed=5 * delta.size,
-            transcendentals=0,
+            flops=2 * (rows + channels) * delta.size, bytes_accessed=5 * delta.size, transcendentals=0
         ),
         name="x_inverse_and_local",
-    )(lines, delta, local_weight)
+    )(*lines, delta, local_weight)
 
 
 def on_device(field_in, pre_act, cotangent, spec_weight, local_weight):
@@ -657,6 +664,23 @@
             values, "dp", split_axis=0, concat_axis=0, tiled=True, axis_index_groups=halves
         )
 
+    def to_chips(chips):
+        arrived = [chips[0]]
+        for pair in range(1, half // 2):
+            moves = [(d, d ^ (2 * pair)) for d in range(data_count)]
+            arrived.append(lax.ppermute(chips[pair], "dp", moves))
+        return arrived
+
+    def between_cores(arrived):
+        rows = arrived[0].shape[0] // 2
+        mates = jnp.concatenate([part[rows:] for part in arrived], axis=0)
+        mates = lax.ppermute(mates, "dp", [(d, d ^ 1) for d in range(data_count)])
+        places = [
+            (source // 2, 0) if source % 2 == 0 else (half // 2, source // 2 * rows)
+            for source in range(half)
+        ]
+        return arrived + [mates], places
+
     def pairs(mirror, shift):
         moves = []
         for d in range(data_count):
@@ -686,24 +710,17 @@
 
     message = row_count * col_block
     y_table = y_basis(0)
-    input_table = y_basis(data_index % half)
-
-    chips = input_call(sizes, field_in[0])
-    arrived = [chips[0]]
-    for pair in range(1, half // 2):
-        moves = [(d, d ^ (2 * pair)) for d in range(data_count)]
-        arrived.append(lax.ppermute(chips[pair], "dp", moves))
+    relative_table = y_basis(data_index % half)
+
+    arrived = to_chips(input_call(sizes, field_in[0]))
     delta, delta_sums = delta_call(sizes, pre_act[0], cotangent[0], field_in[0])
     delta_sums, arrived = tied((delta_sums, arrived))
     delta_lines = exchange(delta_sums)
-    mates = jnp.concatenate([part[message:] for part in arrived], axis=0)
-    arrived.append(lax.ppermute(mates, "dp", [(d, d ^ 1) for d in range(data_count)]))
-    places = [
-        (source // 2, 0) if source % 2 == 0 else (half // 2, source // 2 * message)
-        for source in range(half)
-    ]
+    lines, places = between_cores(arrived)
     input_parts = list(
-        y_transform_call(input_table, arrived, places, message, blocks, space_count, col_block, 0)
+        y_transform_call(
+            relative_table, lines, places, message, blocks, space_count, col_block, 0
+        )
     )
     for shift in range(1, space_count):
         input_parts[shift] = lax.ppermute(input_parts[shift], ("dp", "space"), pairs(0, shift))
@@ -722,26 +739,29 @@
         col_block,
         extra,
     )
+    delta_parts = list(delta_parts)
+    rows = delta_parts[space_count].shape[0]
+    delta_parts[space_count] = jnp.concatenate([delta_parts[space_count], mirrored], axis=0)
     weight, delta_parts = tied((spec_weight, delta_parts))
     weight = load_call(weight)
     delta_held = gathered(delta_parts)
-    input_held = [(part, 0) for part in input_parts]
+    place = 1 + order.index((1, 0))
+    input_held = [(part, 0) for part in input_parts] + [(delta_held[place][rows:], 0)]
+    delta_held[place] = delta_held[place][:rows]
     back, delta_owned, share_rows = back_call(scale_rows, weight, delta_held, share)
-    mirrored, back = tied((mirrored, back))
     received = {(0, 0): back}
     for mirror, shift in order:
         received[(mirror, -shift % space_count)] = lax.ppermute(
             back, ("dp", "space"), pairs(mirror, shift)
         )
     modes = [received[(mirror, shift)] for mirror in (0, 1) for shift in range(space_count)]
-    column_sums = y_inverse_call(y_table, share_rows, modes, half, col_block)
-    mirrored = lax.ppermute(mirrored, ("dp", "space"), pairs(1, 0))
-    column_sums, delta_owned, mirrored = tied((column_sums, delta_owned, mirrored))
-    input_held.append((mirrored, 0))
-    columns = exchange(column_sums)
+    column_sums = y_inverse_call(relative_table, share_rows, modes, half, col_block)
+    column_sums, delta_owned = tied((column_sums, delta_owned))
+    columns = to_chips(column_sums)
     grad_spectral = outer_call(scale_rows, delta_owned, input_held)
     columns, grad_spectral = tied((columns, grad_spectral))
-    grad_input, grad_local, bias_rows = final_call(sizes, columns, delta, local_weight)
+    lines, places = between_cores(columns)
+    grad_input, grad_local, bias_rows = final_call(sizes, lines, places, delta, local_weight)
     return (grad_input[None], grad_spectral, grad_local, bias_rows.reshape(channels))
 
 

time: 76.1 us -> 74.6 us (0.980)
  starting transfers between devices: 28.6 us -> 27.1 us
  waiting for transfers between devices: 16.8 us -> 17.6 us
  Pallas kernels: 27.9 us -> 27.1 us
    all_to_all x2 -> x1, waiting for transfers between devices: 8.92 us -> 2.8 us  [exchange(): lax.all_to_all(values, 'dp', split_axis=0, concat_axis=0, tiled=True, axi...]
    ppermute x5 -> x8, waiting for transfers between devices: 1.04 us -> 5.35 us  [the longest x6 3.68 us: to_chips(): arrived.append(lax.ppermute(chips[pair], 'dp', moves))]
    all_to_all x2 -> x1, starting transfers between devices: 7.76 us -> 4.21 us  [exchange(): lax.all_to_all(values, 'dp', split_axis=0, concat_axis=0, tiled=True, axi...]
    ppermute x5 -> x8, starting transfers between devices: 7.37 us -> 9.38 us  [the longest x6 8.74 us: to_chips(): arrived.append(lax.ppermute(chips[pair], 'dp', moves))]
    ppermute x3, waiting for transfers between devices: 1.9 us -> 3.41 us  [on_device(): lax.ppermute(back, ('dp', 'space'), pairs(mirror, shift))]
    ppermute x3, waiting for transfers between devices: 0.88 us -> 1.99 us  [gathered(): lax.ppermute(parts[mirror * space_count + shift], ('dp', 'space'), pairs(...]
    pallas_call x2, Pallas kernels: 4.28 us -> 3.51 us  [the longest x1 3.04 us: final_call(): pl.pallas_call(functools.partial(final_kernel, sizes, places, len(lines))...]
  transfers between devices with their start and end apart: 14 -> 16, of which waited for: 6 -> 10; matrix products, arithmetic and copies ran while one was open for 2% -> 2% of each run, Pallas kernels for 24% -> 23%
where the time goes in v5:
time: 74.6 us; the launch traced here: 74.4 us
  Pallas kernels  27.1 us (36%)
  starting transfers between devices  27.1 us (36%)
  waiting for transfers between devices  17.6 us (24%)
  other arithmetic  1.41 us (2%)
  between operations  0.9 us (1%)
    ppermute x6, starting transfers between devices, to_chips(): arrived.append(lax.ppermute(chips[pair], 'dp', moves))  8.74 us
    pallas_call x1, Pallas kernels, delta_call(): pl.pallas_call(functools.partial(delta_kernel, sizes), grid=(columns // b...  8.03 us
    ppermute x3, starting transfers between devices, gathered(): lax.ppermute(parts[mirror * space_count + shift], ('dp', 'space'), pairs(...  5.97 us
    ppermute x3, starting transfers between devices, on_device(): lax.ppermute(back, ('dp', 'space'), pairs(mirror, shift))  5.94 us
    pallas_call x1, Pallas kernels, outer_call(): pl.pallas_call(outer_kernel, grid=(held,), in_specs=[whole((rows, channel...  4.9 us
    all_to_all x1, starting transfers between devices, exchange(): lax.all_to_all(values, 'dp', split_axis=0, concat_axis=0, tiled=True, axi...  4.21 us
    ppermute x1, waiting for transfers between devices, on_device(): lax.ppermute(input_parts[shift], ('dp', 'space'), pairs(0, shift))  4.01 us
    ppermute x6, waiting for transfers between devices, to_chips(): arrived.append(lax.ppermute(chips[pair], 'dp', moves))  3.68 us
  transfers between devices with their start and end apart: 16, of which 10 were waited for; matrix products, arithmetic and copies ran while one was open for 2% of the time, Pallas kernels for 23%

profile of v5, /device:TPU:0, one launch (start us, length us, event | category | flops | bytes accessed | tf_op | source)
XLA Modules:
  0.0 74.4 jit_solution(5003294359176739095)
XLA Ops:
  0.6 3.1 %input_x_sums.1 = (bf16[640,128]{1,0:T(8,128)(2,1)}, bf16[640,128]{1,0:T(8,128)(2,1)}, bf16[640,128]{1,0:T(8,128)(2,1)}, bf16[640,128]{1,0:T(8,128)(2,1)}) custom-call(bf16[256,32,128]{2,1,0:T(8,128)(2,1)} %bitcast.10, bf16[256,32,128]{2,1,0:T(8,128)(2,1)} %bitcast.11, bf16[256,32,128]{2,1,0:T(8,128)(2,1)} %bitcast.12, bf16[256,32,128]{2,1,0:T(8,128)(2,1)} %bitcast.13), custom_call_target="tpu_custom_call" | custom-call | flops 167772160 | bytes 4194304 | tf_op jit(solution)/shard_map/input_x_sums/pallas_call | solution.py:268
  3.7 2.9 %collective-permute-start = (bf16[640,128]{1,0:T(8,128)(2,1)}, bf16[640,128]{1,0:T(8,128)(2,1)S(1)}, u32[]{:S(2)}, u32[]{:S(2)}) collective-permute-start(bf16[640,128]{1,0:T(8,128)(2,1)} %get-tuple-element.50), channel_id=1, source_target_pairs={{0,4},{2,6},{4,0},{6,2},{8,12},{10,14},{12,8},{14,10},{16,20},{18,... | collective-permute-start | bytes 491528 | tf_op jit(solution)/shard_map/ppermute | solution.py:671
  6.6 1.6 %collective-permute-start.1 = (bf16[640,128]{1,0:T(8,128)(2,1)}, bf16[640,128]{1,0:T(8,128)(2,1)S(1)}, u32[]{:S(2)}, u32[]{:S(2)}) collective-permute-start(bf16[640,128]{1,0:T(8,128)(2,1)} %get-tuple-element.51), channel_id=1, source_target_pairs={{0,8},{2,10},{4,12},{6,14},{8,0},{10,2},{12,4},{14,6},{16,24},{18,... | collective-permute-start | bytes 491528 | tf_op jit(solution)/shard_map/ppermute | solution.py:671
  8.3 8.0 %delta_and_x_sums.1 = (bf16[256,32,128]{2,1,0:T(8,128)(2,1)}, bf16[8,360,128]{2,1,0:T(8,128)(2,1)}) custom-call(bf16[256,32,128]{2,1,0:T(8,128)(2,1)} %bitcast.16, bf16[256,32,128]{2,1,0:T(8,128)(2,1)} %bitcast.17, bf16[256,32,128]{2,1,0:T(8,128)(2,1)} %bitcast.14), custom_call_target="tpu_custom_call" | custom-call | flops 335544320 | bytes 8388608 | tf_op jit(solution)/shard_map/delta_and_x_sums/pallas_call | solution.py:214
  16.3 4.2 %all-to-all-start = ((bf16[8,360,128]{2,1,0:T(8,128)(2,1)}), bf16[8,360,128]{2,1,0:T(8,128)(2,1)S(1)}, u32[]{:S(2)}, u32[]{:S(2)}) async-start(bf16[8,360,128]{2,1,0:T(8,128)(2,1)} %get-tuple-element.53), calls=%async_computation | async-start | bytes 1474560 | tf_op jit(solution)/shard_map/all_to_all | solution.py:663
  21.5 1.3 %fusion.1 = (bf16[256,512]{1,0:T(8,128)(2,1)S(1)}, bf16[256,512]{1,0:T(8,128)(2,1)S(1)}) fusion(s32[256,256]{1,0:T(8,128)S(1)} %broadcast_in_dim.17, s32[256,256]{1,0:T(8,128)S(1)} %broadcast_in_dim.16, s32[512]{0:T(512)S(1)} %pad_add_fusion.1, s32[256]{0:T(256)S(1)} %fusion.23, s32[512]{0:T(512)S(1)} %pad_add_fusion), kind=kLoop, calls=%fused_computation.3 | loop fusion | flops 9699328 | bytes 1053696 | tf_op jit(solution)/shard_map/convert_element_type | solution.py:44
  23.2 1.6 %collective-permute-start.4 = (bf16[512,128]{1,0:T(8,128)(2,1)S(1)}, bf16[512,128]{1,0:T(8,128)(2,1)S(1)}, u32[]{:S(2)}, u32[]{:S(2)}) collective-permute-start(bf16[512,128]{1,0:T(8,128)(2,1)S(1)} %get-tuple-element.59), channel_id=1, source_target_pairs={{0,1},{1,0},{2,3},{3,2},{4,5},{5,4},{6,7},{7,6},{8,9},{9,8},{10,11... | collective-permute-start | bytes 393224 | tf_op jit(solution)/shard_map/ppermute | solution.py:726
  24.8 4.0 %collective-permute-done.4.refs_1_ = bf16[512,128]{1,0:T(8,128)(2,1)S(1)} collective-permute-done((bf16[512,128]{1,0:T(8,128)(2,1)S(1)}, bf16[512,128]{1,0:T(8,128)(2,1)S(1)}, u32[]{:S(2)}, u32[]{:S(2)}) %collective-permute-start.4) | collective-permute-done | bytes 131104 | tf_op jit(solution)/shard_map/ppermute | solution.py:726
  28.9 2.8 %all-to-all-done = bf16[8,360,128]{2,1,0:T(8,128)(2,1)S(1)} async-done(((bf16[8,360,128]{2,1,0:T(8,128)(2,1)}), bf16[8,360,128]{2,1,0:T(8,128)(2,1)S(1)}, u32[]{:S(2)}, u32[]{:S(2)}) %all-to-all-start) | async-done | bytes 737312 | tf_op jit(solution)/shard_map/all_to_all | solution.py:663
  32.2 2.8 %collective-permute-start.6 = (bf16[552,128]{1,0:T(8,128)(2,1)S(1)}, bf16[552,128]{1,0:T(8,128)(2,1)S(1)}, u32[]{:S(2)}, u32[]{:S(2)}) collective-permute-start(bf16[552,128]{1,0:T(8,128)(2,1)S(1)} %pad_maximum_fusion.2), channel_id=1, source_target_pairs={{0,30},{1,31},{2,28},{3,29},{4,26},{5,27},{6,24},{7,25},{8,22},{9,... | collective-permute-start | bytes 423944 | tf_op jit(solution)/shard_map/ppermute | solution.py:700
  35.0 2.7 %collective-permute-start.5 = (bf16[296,128]{1,0:T(8,128)(2,1)S(1)}, bf16[296,128]{1,0:T(8,128)(2,1)S(1)}, u32[]{:S(2)}, u32[]{:S(2)}) collective-permute-start(bf16[296,128]{1,0:T(8,128)(2,1)S(1)} %get-tuple-element.68), channel_id=1, source_target_pairs={{0,31},{1,30},{2,29},{3,28},{4,27},{5,26},{6,25},{7,24},{8,23},{9,... | collective-permute-start | bytes 227336 | tf_op jit(solution)/shard_map/ppermute | solution.py:700
  38.2 3.5 %weights_to_vmem.1 = bf16[4,2,16,2,128,128]{5,4,3,2,1,0:T(8,128)(2,1)S(1)} custom-call(bf16[4,2,16,2,128,128]{5,4,3,2,1,0:T(8,128)(2,1)} %bitcast.15), custom_call_target="tpu_custom_call" | custom-call | bytes 16777216 | tf_op jit(solution)/shard_map/weights_to_vmem/pallas_call | solution.py:370
  43.7 3.2 %mode_back.1 = (bf16[4,64,128]{2,1,0:T(8,128)(2,1)S(1)}, bf16[4,64,128]{2,1,0:T(8,128)(2,1)S(1)}, bf16[40,128]{1,0:T(8,128)(2,1)S(1)}) custom-call(f32[64,128]{1,0:T(8,128)S(1)} %broadcast_in_dim.20.scale_ref, bf16[4,32,2,128,128]{4,3,2,1,0:T(8,128)(2,1)S(1)} %bitcast.8, bf16[296,128]{1,0:T(8,128)(2,1)S(1)} %get-tuple-element.67.refs_0_, ...), custom_call_target="tpu_custom_call" | custom-call | flops 16777216 | bytes 8388608 | tf_op jit(solution)/shard_map/mode_back/pallas_call | solution.py:422
  46.9 2.8 %collective-permute-start.10 = (bf16[4,64,128]{2,1,0:T(8,128)(2,1)S(1)}, bf16[4,64,128]{2,1,0:T(8,128)(2,1)S(1)}, u32[]{:S(2)}, u32[]{:S(2)}) collective-permute-start(bf16[4,64,128]{2,1,0:T(8,128)(2,1)S(1)} %get-tuple-element.72.refs_0_), channel_id=1, source_target_pairs={{0,31},{1,30},{2,29},{3,28},{4,27},{5,26},{6,25},{7,24},{8,23},{9,... | collective-permute-start | bytes 196616 | tf_op jit(solution)/shard_map/ppermute | solution.py:754
  49.7 1.5 %collective-permute-start.9 = (bf16[4,64,128]{2,1,0:T(8,128)(2,1)S(1)}, bf16[4,64,128]{2,1,0:T(8,128)(2,1)S(1)}, u32[]{:S(2)}, u32[]{:S(2)}) collective-permute-start(bf16[4,64,128]{2,1,0:T(8,128)(2,1)S(1)} %get-tuple-element.72.refs_0_), channel_id=1, source_target_pairs={{0,30},{1,31},{2,28},{3,29},{4,26},{5,27},{6,24},{7,25},{8,22},{9,... | collective-permute-start | bytes 196616 | tf_op jit(solution)/shard_map/ppermute | solution.py:754
  51.2 1.7 %collective-permute-start.8 = (bf16[4,64,128]{2,1,0:T(8,128)(2,1)S(1)}, bf16[4,64,128]{2,1,0:T(8,128)(2,1)S(1)}, u32[]{:S(2)}, u32[]{:S(2)}) collective-permute-start(bf16[4,64,128]{2,1,0:T(8,128)(2,1)S(1)} %get-tuple-element.72.refs_0_), channel_id=1, source_target_pairs={{0,1},{1,0},{2,3},{3,2},{4,5},{5,4},{6,7},{7,6},{8,9},{9,8},{10,11... | collective-permute-start | bytes 196616 | tf_op jit(solution)/shard_map/ppermute | solution.py:754
  52.8 2.0 %collective-permute-done.10.refs_3_ = bf16[4,64,128]{2,1,0:T(8,128)(2,1)S(1)} collective-permute-done((bf16[4,64,128]{2,1,0:T(8,128)(2,1)S(1)}, bf16[4,64,128]{2,1,0:T(8,128)(2,1)S(1)}, u32[]{:S(2)}, u32[]{:S(2)}) %collective-permute-start.10) | collective-permute-done | bytes 65568 | tf_op jit(solution)/shard_map/ppermute | solution.py:754
  54.9 1.3 %collective-permute-done.9.refs_2_ = bf16[4,64,128]{2,1,0:T(8,128)(2,1)S(1)} collective-permute-done((bf16[4,64,128]{2,1,0:T(8,128)(2,1)S(1)}, bf16[4,64,128]{2,1,0:T(8,128)(2,1)S(1)}, u32[]{:S(2)}, u32[]{:S(2)}) %collective-permute-start.9) | collective-permute-done | bytes 65568 | tf_op jit(solution)/shard_map/ppermute | solution.py:754
  56.7 1.4 %collective-permute-start.11 = (bf16[720,128]{1,0:T(8,128)(2,1)S(1)}, bf16[720,128]{1,0:T(8,128)(2,1)S(1)}, u32[]{:S(2)}, u32[]{:S(2)}) collective-permute-start(bf16[720,128]{1,0:T(8,128)(2,1)S(1)} %get-tuple-element.79), channel_id=1, source_target_pairs={{0,4},{2,6},{4,0},{6,2},{8,12},{10,14},{12,8},{14,10},{16,20},{18,... | collective-permute-start | bytes 552968 | tf_op jit(solution)/shard_map/ppermute | solution.py:671
  58.2 2.3 %collective-permute-start.12 = (bf16[720,128]{1,0:T(8,128)(2,1)S(1)}, bf16[720,128]{1,0:T(8,128)(2,1)S(1)}, u32[]{:S(2)}, u32[]{:S(2)}) collective-permute-start(bf16[720,128]{1,0:T(8,128)(2,1)S(1)} %get-tuple-element.80), channel_id=1, source_target_pairs={{0,8},{2,10},{4,12},{6,14},{8,0},{10,2},{12,4},{14,6},{16,24},{18,... | collective-permute-start | bytes 552968 | tf_op jit(solution)/shard_map/ppermute | solution.py:671
  61.0 4.9 %grad_spectral.1 = bf16[4,32,2,128,128]{4,3,2,1,0:T(8,128)(2,1)} custom-call(f32[64,128]{1,0:T(8,128)S(1)} %broadcast_in_dim.20.scale_ref, bf16[4,64,128]{2,1,0:T(8,128)(2,1)S(1)} %get-tuple-element.82.delta_ref, bf16[512,128]{1,0:T(8,128)(2,1)S(1)} %get-tuple-element.58.refs_0_, bf16[512,128]{1,0:T(8,128)(2,1)S(1)} %collective-permute-done.4.refs_1_, ...), custom_call_target="tpu_custom_call" | custom-call | flops 12582912 | bytes 8388608 | tf_op jit(solution)/shard_map/grad_spectral/pallas_call | solution.py:472
  65.9 3.6 %collective-permute-done.13.refs_3_ = bf16[720,128]{1,0:T(8,128)(2,1)S(1)} collective-permute-done((bf16[720,128]{1,0:T(8,128)(2,1)S(1)}, bf16[720,128]{1,0:T(8,128)(2,1)S(1)}, u32[]{:S(2)}, u32[]{:S(2)}) %collective-permute-start.13) | collective-permute-done | bytes 184352 | tf_op jit(solution)/shard_map/ppermute | solution.py:671
  69.7 1.7 %collective-permute-done.14.refs_4_ = bf16[1440,128]{1,0:T(8,128)(2,1)S(1)} collective-permute-done((bf16[1440,128]{1,0:T(8,128)(2,1)S(1)}, bf16[1440,128]{1,0:T(8,128)(2,1)S(1)}, u32[]{:S(2)}, u32[]{:S(2)}) %collective-permute-start.14) | collective-permute-done | bytes 368672 | tf_op jit(solution)/shard_map/ppermute | solution.py:677
  71.4 3.0 %x_inverse_and_local.1 = (bf16[256,32,128]{2,1,0:T(8,128)(2,1)}, f32[128,128]{1,0:T(8,128)}, f32[1,128]{1,0:T(1,128)}) custom-call(bf16[720,128]{1,0:T(8,128)(2,1)S(1)} %get-tuple-element.83.refs_0_, bf16[720,128]{1,0:T(8,128)(2,1)S(1)} %collective-permute-done.11.refs_1_, bf16[720,128]{1,0:T(8,128)(2,1)S(1)} %collective-permute-done.12.refs_2_, ...), custom_call_target="tpu_custom_call" | custom-call | flops 436207616 | bytes 5242880 | tf_op jit(solution)/shard_map/x_inverse_and_local/pallas_call | solution.py:597
  (48 shorter events, 5.7 us)
Async XLA Ops:
  3.7 12.6 %collective-permute-start = (bf16[640,128]{1,0:T(8,128)(2,1)}, bf16[640,128]{1,0:T(8,128)(2,1)S(1)}, u32[]{:S(2)}, u32[]{:S(2)}) collective-permute-start(bf16[640,128]{1,0:T(8,128)(2,1)} %get-tuple-element.50), channel_id=1, source_target_pairs={{0,4},{2,6},{4,0},{6,2},{8,12},{10,14},{12,8},{14,10},{16,20},{18,... | collective-permute-start | bytes 491528 | tf_op jit(solution)/shard_map/ppermute | solution.py:671
  6.6 9.7 %collective-permute-start.1 = (bf16[640,128]{1,0:T(8,128)(2,1)}, bf16[640,128]{1,0:T(8,128)(2,1)S(1)}, u32[]{:S(2)}, u32[]{:S(2)}) collective-permute-start(bf16[640,128]{1,0:T(8,128)(2,1)} %get-tuple-element.51), channel_id=1, source_target_pairs={{0,8},{2,10},{4,12},{6,14},{8,0},{10,2},{12,4},{14,6},{16,24},{18,... | collective-permute-start | bytes 491528 | tf_op jit(solution)/shard_map/ppermute | solution.py:671
  8.2 8.1 %collective-permute-start.2 = (bf16[640,128]{1,0:T(8,128)(2,1)}, bf16[640,128]{1,0:T(8,128)(2,1)S(1)}, u32[]{:S(2)}, u32[]{:S(2)}) collective-permute-start(bf16[640,128]{1,0:T(8,128)(2,1)} %get-tuple-element.52), channel_id=1, source_target_pairs={{0,12},{2,14},{4,8},{6,10},{8,4},{10,6},{12,0},{14,2},{16,28},{18,... | collective-permute-start | bytes 491528 | tf_op jit(solution)/shard_map/ppermute | solution.py:671
  8.2 12.3 %copy-start.1 = (bf16[640,128]{1,0:T(8,128)(2,1)S(1)}, bf16[640,128]{1,0:T(8,128)(2,1)}, u32[]{:S(2)}) copy-start(bf16[640,128]{1,0:T(8,128)(2,1)} %get-tuple-element.54.refs_0_) | copy-start | bytes 491524
  16.3 15.3 %all-to-all-start = ((bf16[8,360,128]{2,1,0:T(8,128)(2,1)}), bf16[8,360,128]{2,1,0:T(8,128)(2,1)S(1)}, u32[]{:S(2)}, u32[]{:S(2)}) async-start(bf16[8,360,128]{2,1,0:T(8,128)(2,1)} %get-tuple-element.53), calls=%async_computation | async-start | bytes 1474560 | tf_op jit(solution)/shard_map/all_to_all | solution.py:663
  20.7 2.0 %collective-permute-start.3 = (bf16[1280,128]{1,0:T(8,128)(2,1)S(1)}, bf16[1280,128]{1,0:T(8,128)(2,1)S(1)}, u32[]{:S(2)}, u32[]{:S(2)}) collective-permute-start(bf16[1280,128]{1,0:T(8,128)(2,1)S(1)} %pad_maximum_fusion.1), channel_id=1, source_target_pairs={{0,2},{2,0},{4,6},{6,4},{8,10},{10,8},{12,14},{14,12},{16,18},{18,... | collective-permute-start | bytes 983048 | tf_op jit(solution)/shard_map/ppermute | solution.py:677
  23.2 5.6 %collective-permute-start.4 = (bf16[512,128]{1,0:T(8,128)(2,1)S(1)}, bf16[512,128]{1,0:T(8,128)(2,1)S(1)}, u32[]{:S(2)}, u32[]{:S(2)}) collective-permute-start(bf16[512,128]{1,0:T(8,128)(2,1)S(1)} %get-tuple-element.59), channel_id=1, source_target_pairs={{0,1},{1,0},{2,3},{3,2},{4,5},{5,4},{6,7},{7,6},{8,9},{9,8},{10,11... | collective-permute-start | bytes 393224 | tf_op jit(solution)/shard_map/ppermute | solution.py:726
  32.2 9.5 %collective-permute-start.6 = (bf16[552,128]{1,0:T(8,128)(2,1)S(1)}, bf16[552,128]{1,0:T(8,128)(2,1)S(1)}, u32[]{:S(2)}, u32[]{:S(2)}) collective-permute-start(bf16[552,128]{1,0:T(8,128)(2,1)S(1)} %pad_maximum_fusion.2), channel_id=1, source_target_pairs={{0,30},{1,31},{2,28},{3,29},{4,26},{5,27},{6,24},{7,25},{8,22},{9,... | collective-permute-start | bytes 423944 | tf_op jit(solution)/shard_map/ppermute | solution.py:700
  35.0 7.8 %collective-permute-start.5 = (bf16[296,128]{1,0:T(8,128)(2,1)S(1)}, bf16[296,128]{1,0:T(8,128)(2,1)S(1)}, u32[]{:S(2)}, u32[]{:S(2)}) collective-permute-start(bf16[296,128]{1,0:T(8,128)(2,1)S(1)} %get-tuple-element.68), channel_id=1, source_target_pairs={{0,31},{1,30},{2,29},{3,28},{4,27},{5,26},{6,25},{7,24},{8,23},{9,... | collective-permute-start | bytes 227336 | tf_op jit(solution)/shard_map/ppermute | solution.py:700
  37.7 6.0 %collective-permute-start.7 = (bf16[296,128]{1,0:T(8,128)(2,1)S(1)}, bf16[296,128]{1,0:T(8,128)(2,1)S(1)}, u32[]{:S(2)}, u32[]{:S(2)}) collective-permute-start(bf16[296,128]{1,0:T(8,128)(2,1)S(1)} %get-tuple-element.70), channel_id=1, source_target_pairs={{0,1},{1,0},{2,3},{3,2},{4,5},{5,4},{6,7},{7,6},{8,9},{9,8},{10,11... | collective-permute-start | bytes 227336 | tf_op jit(solution)/shard_map/ppermute | solution.py:700
  46.9 8.0 %collective-permute-start.10 = (bf16[4,64,128]{2,1,0:T(8,128)(2,1)S(1)}, bf16[4,64,128]{2,1,0:T(8,128)(2,1)S(1)}, u32[]{:S(2)}, u32[]{:S(2)}) collective-permute-start(bf16[4,64,128]{2,1,0:T(8,128)(2,1)S(1)} %get-tuple-element.72.refs_0_), channel_id=1, source_target_pairs={{0,31},{1,30},{2,29},{3,28},{4,27},{5,26},{6,25},{7,24},{8,23},{9,... | collective-permute-start | bytes 196616 | tf_op jit(solution)/shard_map/ppermute | solution.py:754
  49.7 6.5 %collective-permute-start.9 = (bf16[4,64,128]{2,1,0:T(8,128)(2,1)S(1)}, bf16[4,64,128]{2,1,0:T(8,128)(2,1)S(1)}, u32[]{:S(2)}, u32[]{:S(2)}) collective-permute-start(bf16[4,64,128]{2,1,0:T(8,128)(2,1)S(1)} %get-tuple-element.72.refs_0_), channel_id=1, source_target_pairs={{0,30},{1,31},{2,28},{3,29},{4,26},{5,27},{6,24},{7,25},{8,22},{9,... | collective-permute-start | bytes 196616 | tf_op jit(solution)/shard_map/ppermute | solution.py:754
  51.2 5.1 %collective-permute-start.8 = (bf16[4,64,128]{2,1,0:T(8,128)(2,1)S(1)}, bf16[4,64,128]{2,1,0:T(8,128)(2,1)S(1)}, u32[]{:S(2)}, u32[]{:S(2)}) collective-permute-start(bf16[4,64,128]{2,1,0:T(8,128)(2,1)S(1)} %get-tuple-element.72.refs_0_), channel_id=1, source_target_pairs={{0,1},{1,0},{2,3},{3,2},{4,5},{5,4},{6,7},{7,6},{8,9},{9,8},{10,11... | collective-permute-start | bytes 196616 | tf_op jit(solution)/shard_map/ppermute | solution.py:754
  56.7 9.1 %collective-permute-start.11 = (bf16[720,128]{1,0:T(8,128)(2,1)S(1)}, bf16[720,128]{1,0:T(8,128)(2,1)S(1)}, u32[]{:S(2)}, u32[]{:S(2)}) collective-permute-start(bf16[720,128]{1,0:T(8,128)(2,1)S(1)} %get-tuple-element.79), channel_id=1, source_target_pairs={{0,4},{2,6},{4,0},{6,2},{8,12},{10,14},{12,8},{14,10},{16,20},{18,... | collective-permute-start | bytes 552968 | tf_op jit(solution)/shard_map/ppermute | solution.py:671
  58.2 7.8 %collective-permute-start.12 = (bf16[720,128]{1,0:T(8,128)(2,1)S(1)}, bf16[720,128]{1,0:T(8,128)(2,1)S(1)}, u32[]{:S(2)}, u32[]{:S(2)}) collective-permute-start(bf16[720,128]{1,0:T(8,128)(2,1)S(1)} %get-tuple-element.80), channel_id=1, source_target_pairs={{0,8},{2,10},{4,12},{6,14},{8,0},{10,2},{12,4},{14,6},{16,24},{18,... | collective-permute-start | bytes 552968 | tf_op jit(solution)/shard_map/ppermute | solution.py:671
  60.5 9.1 %collective-permute-start.13 = (bf16[720,128]{1,0:T(8,128)(2,1)S(1)}, bf16[720,128]{1,0:T(8,128)(2,1)S(1)}, u32[]{:S(2)}, u32[]{:S(2)}) collective-permute-start(bf16[720,128]{1,0:T(8,128)(2,1)S(1)} %get-tuple-element.81), channel_id=1, source_target_pairs={{0,12},{2,14},{4,8},{6,10},{8,4},{10,6},{12,0},{14,2},{16,28},{18,... | collective-permute-start | bytes 552968 | tf_op jit(solution)/shard_map/ppermute | solution.py:671
  61.0 10.4 %copy-start = (bf16[256,32,128]{2,1,0:T(8,128)(2,1)S(1)}, bf16[256,32,128]{2,1,0:T(8,128)(2,1)}, u32[]{:S(2)}) copy-start(bf16[256,32,128]{2,1,0:T(8,128)(2,1)} %get-tuple-element.87.refs_5_) | copy-start | bytes 6291460
  61.0 10.4 %copy-start.2 = (bf16[128,128]{1,0:T(8,128)(2,1)S(1)}, bf16[128,128]{1,0:T(8,128)(2,1)}, u32[]{:S(2)}) copy-start(bf16[128,128]{1,0:T(8,128)(2,1)} %refs_6_.1) | copy-start | bytes 98308
  69.6 1.8 %collective-permute-start.14 = (bf16[1440,128]{1,0:T(8,128)(2,1)S(1)}, bf16[1440,128]{1,0:T(8,128)(2,1)S(1)}, u32[]{:S(2)}, u32[]{:S(2)}) collective-permute-start(bf16[1440,128]{1,0:T(8,128)(2,1)S(1)} %pad_maximum_fusion), channel_id=1, source_target_pairs={{0,2},{2,0},{4,6},{6,4},{8,10},{10,8},{12,14},{14,12},{16,18},{18,... | collective-permute-start | bytes 1105928 | tf_op jit(solution)/shard_map/ppermute | solution.py:677

commit v6 on v5

--- a/solution.py
+++ b/solution.py
@@ -95,23 +95,37 @@
 
 
 def extra_rows(channels, half):
-    return -(-(2 * (channels // half) + 2) // 8) * 8
+    return -(-2 * (channels // half) // 16) * 16
+
+
+def packed_rows(channels, half):
+    return -(-(2 * (channels // half) + 2) // 16) * 16
+
+
+def stacked(parts, rows):
+    parts = list(parts)
+    filled = sum(part.shape[0] for part in parts)
+    if rows > filled:
+        parts.append(jnp.zeros((rows - filled, parts[0].shape[1]), bf16))
+    return jnp.concatenate([part.astype(f32) for part in parts], axis=0).astype(bf16)
 
 
 def pack_share(share, bias):
     rows, channels = share.shape
-    filler = extra_rows(channels, channels // rows) - 2 * rows - 2
-    parts = list(two_terms(share) + two_terms(bias))
-    if filler:
-        parts.append(jnp.zeros((filler, channels), bf16))
-    return jnp.concatenate([part.astype(f32) for part in parts], axis=0).astype(bf16)
+    return stacked(two_terms(share) + two_terms(bias), packed_rows(channels, channels // rows))
+
+
+def unpack_terms(rows, message):
+    message = message.astype(f32)
+    return message[:rows] + message[rows : 2 * rows]
 
 
 def unpack_share(rows, message):
-    message = message.astype(f32)
-    share = message[:rows] + message[rows : 2 * rows]
-    bias = message[2 * rows : 2 * rows + 1] + message[2 * rows + 1 : 2 * rows + 2]
-    return share, bias
+    return unpack_terms(rows, message), unpack_terms(1, message[2 * rows : 2 * rows + 2])
+
+
+def bias_places(half, rows):
+    return (0, 1), (half - 1, rows - 1)
 
 
 def in_relative_order(pieces, half):
@@ -196,12 +210,19 @@
     @pl.when(block == pl.num_programs(0) - 1)
     def _():
         share = channels // half
-        total = bias[...]
         for target in range(half):
             mine = local[target * share : (target + 1) * share]
             mirrored = local[(half - 1 - target) * share : (half - target) * share]
-            rows = pack_share(jnp.where(upper, mirrored, mine), total)
-            out_ref[target, per_target * all_columns :] = rows
+            rows = two_terms(jnp.where(upper, mirrored, mine))
+            out_ref[target, per_target * all_columns :] = stacked(
+                rows, out_ref.shape[1] - per_target * all_columns
+            )
+        terms = stacked(two_terms(bias[...]), columns).astype(f32)
+        for in_upper, (member, row) in enumerate(bias_places(half, per_target)):
+            here = slice(row * all_columns, row * all_columns + columns)
+            old = out_ref[member, here].astype(f32)
+            ours = upper if in_upper else jnp.logical_not(upper)
+            out_ref[member, here] = jnp.where(ours, terms, old).astype(bf16)
 
 
 def delta_call(sizes, pre_act, cotangent, field_in):
@@ -297,15 +318,20 @@
     own = blocks // 2
     size = table_ref.shape[0] // blocks
     table = table_ref[...]
+    place = lax.axis_index("dp")
     for t in range(frequencies):
-        lines = jnp.concatenate(
-            [
-                rows_of(source, row * columns, (row + 1) * columns)
-                for row in (2 * t, 2 * t + 1)
-                for source in range(sources)
-            ],
-            axis=0,
-        )
+        pieces = [
+            rows_of(source, row * columns, (row + 1) * columns)
+            for row in (2 * t, 2 * t + 1)
+            for source in range(sources)
+        ]
+        for in_upper, (member, row) in enumerate(bias_places(sources, 2 * frequencies)):
+            if extra and row == 2 * t + 1:
+                keep = jnp.where(place == in_upper * (2 * sources - 1), 0.0, 1.0).astype(f32)
+                pieces[sources:] = [
+                    (piece.astype(f32) * keep).astype(bf16) for piece in pieces[sources:]
+                ]
+        lines = jnp.concatenate(pieces, axis=0)
         sums = jnp.dot(table, lines, preferred_element_type=f32).astype(bf16)
         for block in range(blocks):
             held = t if block < own else frequencies - 1 - t
@@ -315,20 +341,29 @@
                     block * size : (block + 1) * size
                 ]
     if extra:
-        rows = channels // sources
-        pieces = [
-            unpack_share(rows, rows_of(i, total_rows - extra, total_rows)) for i in range(sources)
+        share = channels // sources
+        shares = [
+            unpack_terms(share, rows_of(i, total_rows - extra, total_rows)) for i in range(sources)
         ]
-        packed = pack_share(sum(p[0] for p in pieces), sum(p[1] for p in pieces))
+        bias = 0.0
+        for in_upper, (member, row) in enumerate(bias_places(sources, 2 * frequencies)):
+            first = row * columns
+            total = sum(
+                unpack_terms(1, rows_of(i, first, first + min(16, columns))) for i in range(sources)
+            )
+            bias = bias + jnp.where(place == in_upper * (2 * sources - 1), total, 0.0)
+        packed = pack_share(sum(shares), bias)
         for out_ref in out_refs:
-            out_ref[out_ref.shape[0] - extra :] = packed
+            out_ref[out_ref.shape[0] - packed.shape[0] :] = packed
 
 
 def y_transform_call(table, lines, places, total_rows, blocks, outputs, columns, extra):
     channels = lines[0].shape[-1]
     held = (total_rows - extra) // columns // 2 - 1
     size = table.shape[0] // blocks
-    rows = blocks // outputs * held * size + extra
+    rows = blocks // outputs * held * size
+    if extra:
+        rows += packed_rows(channels, len(places))
     return pl.pallas_call(
         functools.partial(
             y_transform_kernel, columns, extra, blocks, total_rows, places, len(lines)
@@ -492,9 +527,9 @@
 def y_inverse_kernel(columns, parts, table_ref, share_ref, *refs):
     part_refs, out_refs = refs[:parts], refs[parts:]
     channels = share_ref.shape[1]
-    extra = share_ref.shape[0]
     message = out_refs[0].shape[0] // 2
     targets = 2 * len(out_refs)
+    extra = extra_rows(channels, targets)
     frequencies = (message - extra) // columns // 2
     own = parts // 2
     size = part_refs[0].shape[1]
@@ -524,13 +559,23 @@
                 ]
     for target in range(targets):
         last = (target % 2 + 1) * message
-        out_refs[target // 2][last - extra : last] = share_ref[...]
+        out_refs[target // 2][last - extra : last] = share_ref[:extra]
+    place = lax.axis_index("dp")
+    height = min(16, columns)
+    share = channels // targets
+    terms = share_ref[2 * share : 2 * share + height].astype(f32)
+    for in_upper, (member, row) in enumerate(bias_places(targets, 2 * frequencies)):
+        ours = place == in_upper * (2 * targets - 1)
+        for target in range(targets):
+            first = target % 2 * message + row * columns
+            old = out_refs[target // 2][first : first + height].astype(f32)
+            out_refs[target // 2][first : first + height] = jnp.where(ours, terms, old).astype(bf16)
 
 
 def y_inverse_call(table, share, parts, targets, columns):
     held, size, channels = parts[0].shape
     rows = 2 * (held + 1)
-    message = (2 * (rows * columns + share.shape[0]), channels)
+    message = (2 * (rows * columns + extra_rows(channels, targets)), channels)
     return pl.pallas_call(
         functools.partial(y_inverse_kernel, columns, len(parts)),
         out_shape=[jax.ShapeDtypeStruct(message, bf16)] * (targets // 2),
@@ -580,13 +625,20 @@
     def _():
         share = channels // half
         extra = extra_rows(channels, half)
-        pieces = []
+        upper = lax.axis_index("dp") >= half
+        rows_low, rows_high = (row for _, row in bias_places(half, per_source))
+        shares, biases = [], []
         for array, at in places:
             begin = at + per_source * all_columns
-            pieces.append(unpack_share(share, line_refs[array][begin : begin + extra]))
-        for source, rows in enumerate(in_relative_order([piece[0] for piece in pieces], half)):
+            shares.append(unpack_terms(share, line_refs[array][begin : begin + extra]))
+            low, high = (
+                unpack_terms(1, line_refs[array][at + row * all_columns : at + row * all_columns + columns])
+                for row in (rows_low, rows_high)
+            )
+            biases.append(jnp.where(upper, high, low))
+        for source, rows in enumerate(in_relative_order(shares, half)):
             local_ref[source * share : (source + 1) * share] = rows
-        bias_ref[...] = pieces[0][1]
+        bias_ref[...] = in_relative_order(biases, half)[0]
 
 
 def final_call(sizes, lines, places, delta, local_weight):

time: 74.6 us -> 74.3 us (level)
  no operation moved by 1% of the time
where the time goes in v6:
time: 74.3 us; the launch traced here: 74.1 us
  Pallas kernels  27.1 us (36%)
  starting transfers between devices  27 us (36%)
  waiting for transfers between devices  17.3 us (23%)
  other arithmetic  1.41 us (2%)
  between operations  0.9 us (1%)
    ppermute x6, starting transfers between devices, to_chips(): arrived.append(lax.ppermute(chips[pair], 'dp', moves))  8.69 us
    pallas_call x1, Pallas kernels, delta_call(): pl.pallas_call(functools.partial(delta_kernel, sizes), grid=(columns // b...  8.03 us
    ppermute x3, starting transfers between devices, gathered(): lax.ppermute(parts[mirror * space_count + shift], ('dp', 'space'), pairs(...  5.97 us
    ppermute x3, starting transfers between devices, on_device(): lax.ppermute(back, ('dp', 'space'), pairs(mirror, shift))  5.94 us
    pallas_call x1, Pallas kernels, outer_call(): pl.pallas_call(outer_kernel, grid=(held,), in_specs=[whole((rows, channel...  4.9 us
    all_to_all x1, starting transfers between devices, exchange(): lax.all_to_all(values, 'dp', split_axis=0, concat_axis=0, tiled=True, axi...  4.21 us
    ppermute x1, waiting for transfers between devices, on_device(): lax.ppermute(input_parts[shift], ('dp', 'space'), pairs(0, shift))  4.02 us
    ppermute x6, waiting for transfers between devices, to_chips(): arrived.append(lax.ppermute(chips[pair], 'dp', moves))  3.49 us
  transfers between devices with their start and end apart: 16, of which 10 were waited for; matrix products, arithmetic and copies ran while one was open for 2% of the time, Pallas kernels for 23%

profile of v6, /device:TPU:0, one launch (start us, length us, event | category | flops | bytes accessed | tf_op | source)
XLA Modules:
  0.0 74.1 jit_solution(12335106120703791833)
XLA Ops:
  0.6 3.1 %input_x_sums.1 = (bf16[640,128]{1,0:T(8,128)(2,1)}, bf16[640,128]{1,0:T(8,128)(2,1)}, bf16[640,128]{1,0:T(8,128)(2,1)}, bf16[640,128]{1,0:T(8,128)(2,1)}) custom-call(bf16[256,32,128]{2,1,0:T(8,128)(2,1)} %bitcast.10, bf16[256,32,128]{2,1,0:T(8,128)(2,1)} %bitcast.11, bf16[256,32,128]{2,1,0:T(8,128)(2,1)} %bitcast.12, bf16[256,32,128]{2,1,0:T(8,128)(2,1)} %bitcast.13), custom_call_target="tpu_custom_call" | custom-call | flops 167772160 | bytes 4194304 | tf_op jit(solution)/shard_map/input_x_sums/pallas_call | solution.py:289
  3.7 2.9 %collective-permute-start = (bf16[640,128]{1,0:T(8,128)(2,1)}, bf16[640,128]{1,0:T(8,128)(2,1)S(1)}, u32[]{:S(2)}, u32[]{:S(2)}) collective-permute-start(bf16[640,128]{1,0:T(8,128)(2,1)} %get-tuple-element.50), channel_id=1, source_target_pairs={{0,4},{2,6},{4,0},{6,2},{8,12},{10,14},{12,8},{14,10},{16,20},{18,... | collective-permute-start | bytes 491528 | tf_op jit(solution)/shard_map/ppermute | solution.py:723
  6.6 1.6 %collective-permute-start.1 = (bf16[640,128]{1,0:T(8,128)(2,1)}, bf16[640,128]{1,0:T(8,128)(2,1)S(1)}, u32[]{:S(2)}, u32[]{:S(2)}) collective-permute-start(bf16[640,128]{1,0:T(8,128)(2,1)} %get-tuple-element.51), channel_id=1, source_target_pairs={{0,8},{2,10},{4,12},{6,14},{8,0},{10,2},{12,4},{14,6},{16,24},{18,... | collective-permute-start | bytes 491528 | tf_op jit(solution)/shard_map/ppermute | solution.py:723
  8.3 8.0 %delta_and_x_sums.1 = (bf16[256,32,128]{2,1,0:T(8,128)(2,1)}, bf16[8,352,128]{2,1,0:T(8,128)(2,1)}) custom-call(bf16[256,32,128]{2,1,0:T(8,128)(2,1)} %bitcast.16, bf16[256,32,128]{2,1,0:T(8,128)(2,1)} %bitcast.17, bf16[256,32,128]{2,1,0:T(8,128)(2,1)} %bitcast.14), custom_call_target="tpu_custom_call" | custom-call | flops 335544320 | bytes 8388608 | tf_op jit(solution)/shard_map/delta_and_x_sums/pallas_call | solution.py:235
  16.3 4.2 %all-to-all-start = ((bf16[8,352,128]{2,1,0:T(8,128)(2,1)}), bf16[8,352,128]{2,1,0:T(8,128)(2,1)S(1)}, u32[]{:S(2)}, u32[]{:S(2)}) async-start(bf16[8,352,128]{2,1,0:T(8,128)(2,1)} %get-tuple-element.53), calls=%async_computation | async-start | bytes 1441792 | tf_op jit(solution)/shard_map/all_to_all | solution.py:715
  21.5 1.3 %fusion.1 = (bf16[256,512]{1,0:T(8,128)(2,1)S(1)}, bf16[256,512]{1,0:T(8,128)(2,1)S(1)}) fusion(s32[256,256]{1,0:T(8,128)S(1)} %broadcast_in_dim.17, s32[256,256]{1,0:T(8,128)S(1)} %broadcast_in_dim.16, s32[512]{0:T(512)S(1)} %pad_add_fusion.1, s32[256]{0:T(256)S(1)} %fusion.23, s32[512]{0:T(512)S(1)} %pad_add_fusion), kind=kLoop, calls=%fused_computation.3 | loop fusion | flops 9699328 | bytes 1053696 | tf_op jit(solution)/shard_map/convert_element_type | solution.py:44
  23.2 1.6 %collective-permute-start.4 = (bf16[512,128]{1,0:T(8,128)(2,1)S(1)}, bf16[512,128]{1,0:T(8,128)(2,1)S(1)}, u32[]{:S(2)}, u32[]{:S(2)}) collective-permute-start(bf16[512,128]{1,0:T(8,128)(2,1)S(1)} %get-tuple-element.59), channel_id=1, source_target_pairs={{0,1},{1,0},{2,3},{3,2},{4,5},{5,4},{6,7},{7,6},{8,9},{9,8},{10,11... | collective-permute-start | bytes 393224 | tf_op jit(solution)/shard_map/ppermute | solution.py:778
  24.8 4.0 %collective-permute-done.4.refs_1_ = bf16[512,128]{1,0:T(8,128)(2,1)S(1)} collective-permute-done((bf16[512,128]{1,0:T(8,128)(2,1)S(1)}, bf16[512,128]{1,0:T(8,128)(2,1)S(1)}, u32[]{:S(2)}, u32[]{:S(2)}) %collective-permute-start.4) | collective-permute-done | bytes 131104 | tf_op jit(solution)/shard_map/ppermute | solution.py:778
  28.9 2.6 %all-to-all-done = bf16[8,352,128]{2,1,0:T(8,128)(2,1)S(1)} async-done(((bf16[8,352,128]{2,1,0:T(8,128)(2,1)}), bf16[8,352,128]{2,1,0:T(8,128)(2,1)S(1)}, u32[]{:S(2)}, u32[]{:S(2)}) %all-to-all-start) | async-done | bytes 720928 | tf_op jit(solution)/shard_map/all_to_all | solution.py:715
  32.0 2.8 %collective-permute-start.6 = (bf16[560,128]{1,0:T(8,128)(2,1)S(1)}, bf16[560,128]{1,0:T(8,128)(2,1)S(1)}, u32[]{:S(2)}, u32[]{:S(2)}) collective-permute-start(bf16[560,128]{1,0:T(8,128)(2,1)S(1)} %pad_maximum_fusion.2), channel_id=1, source_target_pairs={{0,30},{1,31},{2,28},{3,29},{4,26},{5,27},{6,24},{7,25},{8,22},{9,... | collective-permute-start | bytes 430088 | tf_op jit(solution)/shard_map/ppermute | solution.py:752
  34.8 2.7 %collective-permute-start.5 = (bf16[304,128]{1,0:T(8,128)(2,1)S(1)}, bf16[304,128]{1,0:T(8,128)(2,1)S(1)}, u32[]{:S(2)}, u32[]{:S(2)}) collective-permute-start(bf16[304,128]{1,0:T(8,128)(2,1)S(1)} %get-tuple-element.68), channel_id=1, source_target_pairs={{0,31},{1,30},{2,29},{3,28},{4,27},{5,26},{6,25},{7,24},{8,23},{9,... | collective-permute-start | bytes 233480 | tf_op jit(solution)/shard_map/ppermute | solution.py:752
  38.0 3.5 %weights_to_vmem.1 = bf16[4,2,16,2,128,128]{5,4,3,2,1,0:T(8,128)(2,1)S(1)} custom-call(bf16[4,2,16,2,128,128]{5,4,3,2,1,0:T(8,128)(2,1)} %bitcast.15), custom_call_target="tpu_custom_call" | custom-call | bytes 16777216 | tf_op jit(solution)/shard_map/weights_to_vmem/pallas_call | solution.py:405
  43.6 3.2 %mode_back.1 = (bf16[4,64,128]{2,1,0:T(8,128)(2,1)S(1)}, bf16[4,64,128]{2,1,0:T(8,128)(2,1)S(1)}, bf16[48,128]{1,0:T(8,128)(2,1)S(1)}) custom-call(f32[64,128]{1,0:T(8,128)S(1)} %broadcast_in_dim.20.scale_ref, bf16[4,32,2,128,128]{4,3,2,1,0:T(8,128)(2,1)S(1)} %bitcast.8, bf16[304,128]{1,0:T(8,128)(2,1)S(1)} %get-tuple-element.67.refs_0_, ...), custom_call_target="tpu_custom_call" | custom-call | flops 16777216 | bytes 8388608 | tf_op jit(solution)/shard_map/mode_back/pallas_call | solution.py:457
  46.8 2.8 %collective-permute-start.10 = (bf16[4,64,128]{2,1,0:T(8,128)(2,1)S(1)}, bf16[4,64,128]{2,1,0:T(8,128)(2,1)S(1)}, u32[]{:S(2)}, u32[]{:S(2)}) collective-permute-start(bf16[4,64,128]{2,1,0:T(8,128)(2,1)S(1)} %get-tuple-element.72.refs_0_), channel_id=1, source_target_pairs={{0,31},{1,30},{2,29},{3,28},{4,27},{5,26},{6,25},{7,24},{8,23},{9,... | collective-permute-start | bytes 196616 | tf_op jit(solution)/shard_map/ppermute | solution.py:806
  49.6 1.4 %collective-permute-start.9 = (bf16[4,64,128]{2,1,0:T(8,128)(2,1)S(1)}, bf16[4,64,128]{2,1,0:T(8,128)(2,1)S(1)}, u32[]{:S(2)}, u32[]{:S(2)}) collective-permute-start(bf16[4,64,128]{2,1,0:T(8,128)(2,1)S(1)} %get-tuple-element.72.refs_0_), channel_id=1, source_target_pairs={{0,30},{1,31},{2,28},{3,29},{4,26},{5,27},{6,24},{7,25},{8,22},{9,... | collective-permute-start | bytes 196616 | tf_op jit(solution)/shard_map/ppermute | solution.py:806
  51.0 1.7 %collective-permute-start.8 = (bf16[4,64,128]{2,1,0:T(8,128)(2,1)S(1)}, bf16[4,64,128]{2,1,0:T(8,128)(2,1)S(1)}, u32[]{:S(2)}, u32[]{:S(2)}) collective-permute-start(bf16[4,64,128]{2,1,0:T(8,128)(2,1)S(1)} %get-tuple-element.72.refs_0_), channel_id=1, source_target_pairs={{0,1},{1,0},{2,3},{3,2},{4,5},{5,4},{6,7},{7,6},{8,9},{9,8},{10,11... | collective-permute-start | bytes 196616 | tf_op jit(solution)/shard_map/ppermute | solution.py:806
  52.7 2.1 %collective-permute-done.10.refs_3_ = bf16[4,64,128]{2,1,0:T(8,128)(2,1)S(1)} collective-permute-done((bf16[4,64,128]{2,1,0:T(8,128)(2,1)S(1)}, bf16[4,64,128]{2,1,0:T(8,128)(2,1)S(1)}, u32[]{:S(2)}, u32[]{:S(2)}) %collective-permute-start.10) | collective-permute-done | bytes 65568 | tf_op jit(solution)/shard_map/ppermute | solution.py:806
  54.8 1.3 %collective-permute-done.9.refs_2_ = bf16[4,64,128]{2,1,0:T(8,128)(2,1)S(1)} collective-permute-done((bf16[4,64,128]{2,1,0:T(8,128)(2,1)S(1)}, bf16[4,64,128]{2,1,0:T(8,128)(2,1)S(1)}, u32[]{:S(2)}, u32[]{:S(2)}) %collective-permute-start.9) | collective-permute-done | bytes 65568 | tf_op jit(solution)/shard_map/ppermute | solution.py:806
  56.6 1.4 %collective-permute-start.11 = (bf16[704,128]{1,0:T(8,128)(2,1)S(1)}, bf16[704,128]{1,0:T(8,128)(2,1)S(1)}, u32[]{:S(2)}, u32[]{:S(2)}) collective-permute-start(bf16[704,128]{1,0:T(8,128)(2,1)S(1)} %get-tuple-element.79), channel_id=1, source_target_pairs={{0,4},{2,6},{4,0},{6,2},{8,12},{10,14},{12,8},{14,10},{16,20},{18,... | collective-permute-start | bytes 540680 | tf_op jit(solution)/shard_map/ppermute | solution.py:723
  58.1 2.5 %collective-permute-start.12 = (bf16[704,128]{1,0:T(8,128)(2,1)S(1)}, bf16[704,128]{1,0:T(8,128)(2,1)S(1)}, u32[]{:S(2)}, u32[]{:S(2)}) collective-permute-start(bf16[704,128]{1,0:T(8,128)(2,1)S(1)} %get-tuple-element.80), channel_id=1, source_target_pairs={{0,8},{2,10},{4,12},{6,14},{8,0},{10,2},{12,4},{14,6},{16,24},{18,... | collective-permute-start | bytes 540680 | tf_op jit(solution)/shard_map/ppermute | solution.py:723
  60.8 4.9 %grad_spectral.1 = bf16[4,32,2,128,128]{4,3,2,1,0:T(8,128)(2,1)} custom-call(f32[64,128]{1,0:T(8,128)S(1)} %broadcast_in_dim.20.scale_ref, bf16[4,64,128]{2,1,0:T(8,128)(2,1)S(1)} %get-tuple-element.82.delta_ref, bf16[512,128]{1,0:T(8,128)(2,1)S(1)} %get-tuple-element.58.refs_0_, bf16[512,128]{1,0:T(8,128)(2,1)S(1)} %collective-permute-done.4.refs_1_, ...), custom_call_target="tpu_custom_call" | custom-call | flops 12582912 | bytes 8388608 | tf_op jit(solution)/shard_map/grad_spectral/pallas_call | solution.py:507
  66.0 3.2 %collective-permute-done.13.refs_3_ = bf16[704,128]{1,0:T(8,128)(2,1)S(1)} collective-permute-done((bf16[704,128]{1,0:T(8,128)(2,1)S(1)}, bf16[704,128]{1,0:T(8,128)(2,1)S(1)}, u32[]{:S(2)}, u32[]{:S(2)}) %collective-permute-start.13) | collective-permute-done | bytes 180256 | tf_op jit(solution)/shard_map/ppermute | solution.py:723
  69.4 1.7 %collective-permute-done.14.refs_4_ = bf16[1408,128]{1,0:T(8,128)(2,1)S(1)} collective-permute-done((bf16[1408,128]{1,0:T(8,128)(2,1)S(1)}, bf16[1408,128]{1,0:T(8,128)(2,1)S(1)}, u32[]{:S(2)}, u32[]{:S(2)}) %collective-permute-start.14) | collective-permute-done | bytes 360480 | tf_op jit(solution)/shard_map/ppermute | solution.py:729
  71.1 3.0 %x_inverse_and_local.1 = (bf16[256,32,128]{2,1,0:T(8,128)(2,1)}, f32[128,128]{1,0:T(8,128)}, f32[1,128]{1,0:T(1,128)}) custom-call(bf16[704,128]{1,0:T(8,128)(2,1)S(1)} %get-tuple-element.83.refs_0_, bf16[704,128]{1,0:T(8,128)(2,1)S(1)} %collective-permute-done.11.refs_1_, bf16[704,128]{1,0:T(8,128)(2,1)S(1)} %collective-permute-done.12.refs_2_, ...), custom_call_target="tpu_custom_call" | custom-call | flops 436207616 | bytes 5242880 | tf_op jit(solution)/shard_map/x_inverse_and_local/pallas_call | solution.py:649
  (48 shorter events, 5.7 us)
Async XLA Ops:
  3.7 12.6 %collective-permute-start = (bf16[640,128]{1,0:T(8,128)(2,1)}, bf16[640,128]{1,0:T(8,128)(2,1)S(1)}, u32[]{:S(2)}, u32[]{:S(2)}) collective-permute-start(bf16[640,128]{1,0:T(8,128)(2,1)} %get-tuple-element.50), channel_id=1, source_target_pairs={{0,4},{2,6},{4,0},{6,2},{8,12},{10,14},{12,8},{14,10},{16,20},{18,... | collective-permute-start | bytes 491528 | tf_op jit(solution)/shard_map/ppermute | solution.py:723
  6.6 9.7 %collective-permute-start.1 = (bf16[640,128]{1,0:T(8,128)(2,1)}, bf16[640,128]{1,0:T(8,128)(2,1)S(1)}, u32[]{:S(2)}, u32[]{:S(2)}) collective-permute-start(bf16[640,128]{1,0:T(8,128)(2,1)} %get-tuple-element.51), channel_id=1, source_target_pairs={{0,8},{2,10},{4,12},{6,14},{8,0},{10,2},{12,4},{14,6},{16,24},{18,... | collective-permute-start | bytes 491528 | tf_op jit(solution)/shard_map/ppermute | solution.py:723
  8.2 8.1 %collective-permute-start.2 = (bf16[640,128]{1,0:T(8,128)(2,1)}, bf16[640,128]{1,0:T(8,128)(2,1)S(1)}, u32[]{:S(2)}, u32[]{:S(2)}) collective-permute-start(bf16[640,128]{1,0:T(8,128)(2,1)} %get-tuple-element.52), channel_id=1, source_target_pairs={{0,12},{2,14},{4,8},{6,10},{8,4},{10,6},{12,0},{14,2},{16,28},{18,... | collective-permute-start | bytes 491528 | tf_op jit(solution)/shard_map/ppermute | solution.py:723
  8.2 12.3 %copy-start.1 = (bf16[640,128]{1,0:T(8,128)(2,1)S(1)}, bf16[640,128]{1,0:T(8,128)(2,1)}, u32[]{:S(2)}) copy-start(bf16[640,128]{1,0:T(8,128)(2,1)} %get-tuple-element.54.refs_0_) | copy-start | bytes 491524
  16.3 15.2 %all-to-all-start = ((bf16[8,352,128]{2,1,0:T(8,128)(2,1)}), bf16[8,352,128]{2,1,0:T(8,128)(2,1)S(1)}, u32[]{:S(2)}, u32[]{:S(2)}) async-start(bf16[8,352,128]{2,1,0:T(8,128)(2,1)} %get-tuple-element.53), calls=%async_computation | async-start | bytes 1441792 | tf_op jit(solution)/shard_map/all_to_all | solution.py:715
  20.7 2.0 %collective-permute-start.3 = (bf16[1280,128]{1,0:T(8,128)(2,1)S(1)}, bf16[1280,128]{1,0:T(8,128)(2,1)S(1)}, u32[]{:S(2)}, u32[]{:S(2)}) collective-permute-start(bf16[1280,128]{1,0:T(8,128)(2,1)S(1)} %pad_maximum_fusion.1), channel_id=1, source_target_pairs={{0,2},{2,0},{4,6},{6,4},{8,10},{10,8},{12,14},{14,12},{16,18},{18,... | collective-permute-start | bytes 983048 | tf_op jit(solution)/shard_map/ppermute | solution.py:729
  23.2 5.6 %collective-permute-start.4 = (bf16[512,128]{1,0:T(8,128)(2,1)S(1)}, bf16[512,128]{1,0:T(8,128)(2,1)S(1)}, u32[]{:S(2)}, u32[]{:S(2)}) collective-permute-start(bf16[512,128]{1,0:T(8,128)(2,1)S(1)} %get-tuple-element.59), channel_id=1, source_target_pairs={{0,1},{1,0},{2,3},{3,2},{4,5},{5,4},{6,7},{7,6},{8,9},{9,8},{10,11... | collective-permute-start | bytes 393224 | tf_op jit(solution)/shard_map/ppermute | solution.py:778
  32.0 9.5 %collective-permute-start.6 = (bf16[560,128]{1,0:T(8,128)(2,1)S(1)}, bf16[560,128]{1,0:T(8,128)(2,1)S(1)}, u32[]{:S(2)}, u32[]{:S(2)}) collective-permute-start(bf16[560,128]{1,0:T(8,128)(2,1)S(1)} %pad_maximum_fusion.2), channel_id=1, source_target_pairs={{0,30},{1,31},{2,28},{3,29},{4,26},{5,27},{6,24},{7,25},{8,22},{9,... | collective-permute-start | bytes 430088 | tf_op jit(solution)/shard_map/ppermute | solution.py:752
  34.8 7.8 %collective-permute-start.5 = (bf16[304,128]{1,0:T(8,128)(2,1)S(1)}, bf16[304,128]{1,0:T(8,128)(2,1)S(1)}, u32[]{:S(2)}, u32[]{:S(2)}) collective-permute-start(bf16[304,128]{1,0:T(8,128)(2,1)S(1)} %get-tuple-element.68), channel_id=1, source_target_pairs={{0,31},{1,30},{2,29},{3,28},{4,27},{5,26},{6,25},{7,24},{8,23},{9,... | collective-permute-start | bytes 233480 | tf_op jit(solution)/shard_map/ppermute | solution.py:752
  37.5 6.1 %collective-permute-start.7 = (bf16[304,128]{1,0:T(8,128)(2,1)S(1)}, bf16[304,128]{1,0:T(8,128)(2,1)S(1)}, u32[]{:S(2)}, u32[]{:S(2)}) collective-permute-start(bf16[304,128]{1,0:T(8,128)(2,1)S(1)} %get-tuple-element.70), channel_id=1, source_target_pairs={{0,1},{1,0},{2,3},{3,2},{4,5},{5,4},{6,7},{7,6},{8,9},{9,8},{10,11... | collective-permute-start | bytes 233480 | tf_op jit(solution)/shard_map/ppermute | solution.py:752
  46.8 8.0 %collective-permute-start.10 = (bf16[4,64,128]{2,1,0:T(8,128)(2,1)S(1)}, bf16[4,64,128]{2,1,0:T(8,128)(2,1)S(1)}, u32[]{:S(2)}, u32[]{:S(2)}) collective-permute-start(bf16[4,64,128]{2,1,0:T(8,128)(2,1)S(1)} %get-tuple-element.72.refs_0_), channel_id=1, source_target_pairs={{0,31},{1,30},{2,29},{3,28},{4,27},{5,26},{6,25},{7,24},{8,23},{9,... | collective-permute-start | bytes 196616 | tf_op jit(solution)/shard_map/ppermute | solution.py:806
  49.6 6.5 %collective-permute-start.9 = (bf16[4,64,128]{2,1,0:T(8,128)(2,1)S(1)}, bf16[4,64,128]{2,1,0:T(8,128)(2,1)S(1)}, u32[]{:S(2)}, u32[]{:S(2)}) collective-permute-start(bf16[4,64,128]{2,1,0:T(8,128)(2,1)S(1)} %get-tuple-element.72.refs_0_), channel_id=1, source_target_pairs={{0,30},{1,31},{2,28},{3,29},{4,26},{5,27},{6,24},{7,25},{8,22},{9,... | collective-permute-start | bytes 196616 | tf_op jit(solution)/shard_map/ppermute | solution.py:806
  51.0 5.2 %collective-permute-start.8 = (bf16[4,64,128]{2,1,0:T(8,128)(2,1)S(1)}, bf16[4,64,128]{2,1,0:T(8,128)(2,1)S(1)}, u32[]{:S(2)}, u32[]{:S(2)}) collective-permute-start(bf16[4,64,128]{2,1,0:T(8,128)(2,1)S(1)} %get-tuple-element.72.refs_0_), channel_id=1, source_target_pairs={{0,1},{1,0},{2,3},{3,2},{4,5},{5,4},{6,7},{7,6},{8,9},{9,8},{10,11... | collective-permute-start | bytes 196616 | tf_op jit(solution)/shard_map/ppermute | solution.py:806
  56.6 9.1 %collective-permute-start.11 = (bf16[704,128]{1,0:T(8,128)(2,1)S(1)}, bf16[704,128]{1,0:T(8,128)(2,1)S(1)}, u32[]{:S(2)}, u32[]{:S(2)}) collective-permute-start(bf16[704,128]{1,0:T(8,128)(2,1)S(1)} %get-tuple-element.79), channel_id=1, source_target_pairs={{0,4},{2,6},{4,0},{6,2},{8,12},{10,14},{12,8},{14,10},{16,20},{18,... | collective-permute-start | bytes 540680 | tf_op jit(solution)/shard_map/ppermute | solution.py:723
  58.1 7.9 %collective-permute-start.12 = (bf16[704,128]{1,0:T(8,128)(2,1)S(1)}, bf16[704,128]{1,0:T(8,128)(2,1)S(1)}, u32[]{:S(2)}, u32[]{:S(2)}) collective-permute-start(bf16[704,128]{1,0:T(8,128)(2,1)S(1)} %get-tuple-element.80), channel_id=1, source_target_pairs={{0,8},{2,10},{4,12},{6,14},{8,0},{10,2},{12,4},{14,6},{16,24},{18,... | collective-permute-start | bytes 540680 | tf_op jit(solution)/shard_map/ppermute | solution.py:723
  60.6 8.6 %collective-permute-start.13 = (bf16[704,128]{1,0:T(8,128)(2,1)S(1)}, bf16[704,128]{1,0:T(8,128)(2,1)S(1)}, u32[]{:S(2)}, u32[]{:S(2)}) collective-permute-start(bf16[704,128]{1,0:T(8,128)(2,1)S(1)} %get-tuple-element.81), channel_id=1, source_target_pairs={{0,12},{2,14},{4,8},{6,10},{8,4},{10,6},{12,0},{14,2},{16,28},{18,... | collective-permute-start | bytes 540680 | tf_op jit(solution)/shard_map/ppermute | solution.py:723
  60.8 10.2 %copy-start = (bf16[256,32,128]{2,1,0:T(8,128)(2,1)S(1)}, bf16[256,32,128]{2,1,0:T(8,128)(2,1)}, u32[]{:S(2)}) copy-start(bf16[256,32,128]{2,1,0:T(8,128)(2,1)} %get-tuple-element.87.refs_5_) | copy-start | bytes 6291460
  60.8 10.2 %copy-start.2 = (bf16[128,128]{1,0:T(8,128)(2,1)S(1)}, bf16[128,128]{1,0:T(8,128)(2,1)}, u32[]{:S(2)}) copy-start(bf16[128,128]{1,0:T(8,128)(2,1)} %refs_6_.1) | copy-start | bytes 98308
  69.3 1.7 %collective-permute-start.14 = (bf16[1408,128]{1,0:T(8,128)(2,1)S(1)}, bf16[1408,128]{1,0:T(8,128)(2,1)S(1)}, u32[]{:S(2)}, u32[]{:S(2)}) collective-permute-start(bf16[1408,128]{1,0:T(8,128)(2,1)S(1)} %pad_maximum_fusion), channel_id=1, source_target_pairs={{0,2},{2,0},{4,6},{6,4},{8,10},{10,8},{12,14},{14,12},{16,18},{18,... | collective-permute-start | bytes 1081352 | tf_op jit(solution)/shard_map/ppermute | solution.py:729

commit v7 on v6

--- a/solution.py
+++ b/solution.py
@@ -181,7 +181,7 @@
         lines[:, rows, :] = jnp.swapaxes(delta, 0, 1)
         return carry
 
-    lax.fori_loop(0, grid_rows // step, slab, 0, unroll=2)
+    lax.fori_loop(0, grid_rows // step, slab, 0)
     sums, totals = matrix_per_column(
         table[...], [lines[y] for y in range(columns)], (0, table.shape[0] - 2)
     )
@@ -388,31 +388,52 @@
 
 
 def load_kernel(source_ref, target_ref, semaphores):
+    held, modes = source_ref.shape[:2]
+    pieces = semaphores.shape[1]
+    rows = modes // pieces
     copies = [
-        pltpu.make_async_copy(source_ref.at[j, k], target_ref.at[j, k], semaphores.at[j, k])
-        for j in range(source_ref.shape[0])
-        for k in range(source_ref.shape[1])
+        [
+            pltpu.make_async_copy(
+                source_ref.at[j, pl.ds(k * rows, rows)],
+                target_ref.at[j, pl.ds(k * rows, rows)],
+                semaphores.at[j, k],
+            )
+            for k in range(pieces)
+        ]
+        for j in range(held)
     ]
-    for copy in copies:
+    for copy in sum(copies, []):
         copy.start()
-    for copy in copies:
-        copy.wait()
+    for j in range(held):
+        for copy in copies[j]:
+            copy.wait()
+        if j >= turned_count(held):
+            continue
+
+        def turn(mode, carry, j=j):
+            for part in range(2):
+                target_ref[j, mode, part] = target_ref[j, mode, part].T
+            return carry
+
+        lax.fori_loop(0, modes, turn, 0, unroll=4)
+
+
+def turned_count(held):
+    return held // 2
 
 
 def load_call(weight):
-    held, modes, _, channels, _ = weight.shape
-    parts = weight.reshape(held, 2, modes // 2, 2, channels, channels)
-    loaded = pl.pallas_call(
+    held = weight.shape[0]
+    return pl.pallas_call(
         load_kernel,
         in_specs=[pl.BlockSpec(memory_space=pl.ANY)],
-        out_specs=pl.BlockSpec(memory_space=pl.ANY),
-        out_shape=pltpu.VMEM(parts.shape, bf16),
+        out_specs=pl.BlockSpec(memory_space=pltpu.VMEM),
+        out_shape=pltpu.VMEM(weight.shape, bf16),
         scratch_shapes=[pltpu.SemaphoreType.DMA((held, 2))],
         compiler_params=params(50),
         cost_estimate=pl.CostEstimate(flops=0, bytes_accessed=4 * weight.size, transcendentals=0),
         name="weights_to_vmem",
-    )(parts)
-    return loaded.reshape(weight.shape)
+    )(weight)
 
 
 def back_kernel(share, scale_ref, weight_ref, *refs):
@@ -429,18 +450,25 @@
     delta = total.astype(bf16)
     delta_ref[j, inner] = delta
     both = turned(delta.astype(f32)).astype(bf16)
-    sums = []
-    for mode in range(block):
-        weight = jnp.concatenate([weight_ref[0, mode, 0], weight_ref[0, mode, 1]], axis=1)
-        sums.append(
-            lax.dot_general(
-                both[2 * mode : 2 * mode + 2],
-                weight,
-                (((1,), (1,)), ((), ())),
-                preferred_element_type=f32,
+
+    def products(is_turned):
+        sums = []
+        for mode in range(block):
+            weight = jnp.concatenate(
+                [weight_ref[0, mode, 0], weight_ref[0, mode, 1]], axis=0 if is_turned else 1
             )
-        )
-    back_ref[j, inner] = (jnp.concatenate(sums, axis=0) * scale_ref[inner]).astype(bf16)
+            sums.append(
+                lax.dot_general(
+                    both[2 * mode : 2 * mode + 2],
+                    weight,
+                    (((1,), (0 if is_turned else 1,)), ((), ())),
+                    preferred_element_type=f32,
+                )
+            )
+        back_ref[j, inner] = (jnp.concatenate(sums, axis=0) * scale_ref[inner]).astype(bf16)
+
+    pl.when(j < turned_count(held))(lambda: products(True))
+    pl.when(j >= turned_count(held))(lambda: products(False))
 
     @pl.when((j == 0) & (k == 0))
     def _():

time: 74.3 us -> 73.8 us (level)
  no operation moved by 1% of the time
where the time goes in v7:
time: 73.8 us; the launch traced here: 73.5 us
  starting transfers between devices  27 us (37%)
  Pallas kernels  26.7 us (36%)
  waiting for transfers between devices  17.2 us (23%)
  other arithmetic  1.41 us (2%)
  between operations  0.9 us (1%)
    ppermute x6, starting transfers between devices, to_chips(): arrived.append(lax.ppermute(chips[pair], 'dp', moves))  8.68 us
    pallas_call x1, Pallas kernels, delta_call(): pl.pallas_call(functools.partial(delta_kernel, sizes), grid=(columns // b...  7.95 us
    ppermute x3, starting transfers between devices, gathered(): lax.ppermute(parts[mirror * space_count + shift], ('dp', 'space'), pairs(...  5.97 us
    ppermute x3, starting transfers between devices, on_device(): lax.ppermute(back, ('dp', 'space'), pairs(mirror, shift))  5.95 us
    pallas_call x1, Pallas kernels, outer_call(): pl.pallas_call(outer_kernel, grid=(held,), in_specs=[whole((rows, channel...  4.9 us
    all_to_all x1, starting transfers between devices, exchange(): lax.all_to_all(values, 'dp', split_axis=0, concat_axis=0, tiled=True, axi...  4.21 us
    ppermute x1, waiting for transfers between devices, on_device(): lax.ppermute(input_parts[shift], ('dp', 'space'), pairs(0, shift))  4.02 us
    pallas_call x1, Pallas kernels, load_call(): pl.pallas_call(load_kernel, in_specs=[pl.BlockSpec(memory_space=pl.ANY)],...  3.57 us
  transfers between devices with their start and end apart: 16, of which 10 were waited for; matrix products, arithmetic and copies ran while one was open for 2% of the time, Pallas kernels for 23%

profile of v7, /device:TPU:0, one launch (start us, length us, event | category | flops | bytes accessed | tf_op | source)
XLA Modules:
  0.0 73.5 jit_solution(5704943852804507394)
XLA Ops:
  0.6 3.1 %input_x_sums.1 = (bf16[640,128]{1,0:T(8,128)(2,1)}, bf16[640,128]{1,0:T(8,128)(2,1)}, bf16[640,128]{1,0:T(8,128)(2,1)}, bf16[640,128]{1,0:T(8,128)(2,1)}) custom-call(bf16[256,32,128]{2,1,0:T(8,128)(2,1)} %bitcast.7, bf16[256,32,128]{2,1,0:T(8,128)(2,1)} %bitcast.8, bf16[256,32,128]{2,1,0:T(8,128)(2,1)} %bitcast.9, bf16[256,32,128]{2,1,0:T(8,128)(2,1)} %bitcast.10), custom_call_target="tpu_custom_call" | custom-call | flops 167772160 | bytes 4194304 | tf_op jit(solution)/shard_map/input_x_sums/pallas_call | solution.py:289
  3.7 2.9 %collective-permute-start = (bf16[640,128]{1,0:T(8,128)(2,1)}, bf16[640,128]{1,0:T(8,128)(2,1)S(1)}, u32[]{:S(2)}, u32[]{:S(2)}) collective-permute-start(bf16[640,128]{1,0:T(8,128)(2,1)} %get-tuple-element.50), channel_id=1, source_target_pairs={{0,4},{2,6},{4,0},{6,2},{8,12},{10,14},{12,8},{14,10},{16,20},{18,... | collective-permute-start | bytes 491528 | tf_op jit(solution)/shard_map/ppermute | solution.py:751
  6.6 1.6 %collective-permute-start.1 = (bf16[640,128]{1,0:T(8,128)(2,1)}, bf16[640,128]{1,0:T(8,128)(2,1)S(1)}, u32[]{:S(2)}, u32[]{:S(2)}) collective-permute-start(bf16[640,128]{1,0:T(8,128)(2,1)} %get-tuple-element.51), channel_id=1, source_target_pairs={{0,8},{2,10},{4,12},{6,14},{8,0},{10,2},{12,4},{14,6},{16,24},{18,... | collective-permute-start | bytes 491528 | tf_op jit(solution)/shard_map/ppermute | solution.py:751
  8.3 8.0 %delta_and_x_sums.1 = (bf16[256,32,128]{2,1,0:T(8,128)(2,1)}, bf16[8,352,128]{2,1,0:T(8,128)(2,1)}) custom-call(bf16[256,32,128]{2,1,0:T(8,128)(2,1)} %bitcast.12, bf16[256,32,128]{2,1,0:T(8,128)(2,1)} %bitcast.13, bf16[256,32,128]{2,1,0:T(8,128)(2,1)} %bitcast.11), custom_call_target="tpu_custom_call" | custom-call | flops 335544320 | bytes 8388608 | tf_op jit(solution)/shard_map/delta_and_x_sums/pallas_call | solution.py:235
  16.3 4.2 %all-to-all-start = ((bf16[8,352,128]{2,1,0:T(8,128)(2,1)}), bf16[8,352,128]{2,1,0:T(8,128)(2,1)S(1)}, u32[]{:S(2)}, u32[]{:S(2)}) async-start(bf16[8,352,128]{2,1,0:T(8,128)(2,1)} %get-tuple-element.53), calls=%async_computation | async-start | bytes 1441792 | tf_op jit(solution)/shard_map/all_to_all | solution.py:743
  21.4 1.3 %fusion.1 = (bf16[256,512]{1,0:T(8,128)(2,1)S(1)}, bf16[256,512]{1,0:T(8,128)(2,1)S(1)}) fusion(s32[256,256]{1,0:T(8,128)S(1)} %broadcast_in_dim.17, s32[256,256]{1,0:T(8,128)S(1)} %broadcast_in_dim.16, s32[512]{0:T(512)S(1)} %pad_add_fusion.1, s32[256]{0:T(256)S(1)} %fusion.23, s32[512]{0:T(512)S(1)} %pad_add_fusion), kind=kLoop, calls=%fused_computation.3 | loop fusion | flops 9699328 | bytes 1053696 | tf_op jit(solution)/shard_map/convert_element_type | solution.py:44
  23.2 1.6 %collective-permute-start.4 = (bf16[512,128]{1,0:T(8,128)(2,1)S(1)}, bf16[512,128]{1,0:T(8,128)(2,1)S(1)}, u32[]{:S(2)}, u32[]{:S(2)}) collective-permute-start(bf16[512,128]{1,0:T(8,128)(2,1)S(1)} %get-tuple-element.59), channel_id=1, source_target_pairs={{0,1},{1,0},{2,3},{3,2},{4,5},{5,4},{6,7},{7,6},{8,9},{9,8},{10,11... | collective-permute-start | bytes 393224 | tf_op jit(solution)/shard_map/ppermute | solution.py:806
  24.8 4.0 %collective-permute-done.4.refs_1_ = bf16[512,128]{1,0:T(8,128)(2,1)S(1)} collective-permute-done((bf16[512,128]{1,0:T(8,128)(2,1)S(1)}, bf16[512,128]{1,0:T(8,128)(2,1)S(1)}, u32[]{:S(2)}, u32[]{:S(2)}) %collective-permute-start.4) | collective-permute-done | bytes 131104 | tf_op jit(solution)/shard_map/ppermute | solution.py:806
  28.8 2.6 %all-to-all-done = bf16[8,352,128]{2,1,0:T(8,128)(2,1)S(1)} async-done(((bf16[8,352,128]{2,1,0:T(8,128)(2,1)}), bf16[8,352,128]{2,1,0:T(8,128)(2,1)S(1)}, u32[]{:S(2)}, u32[]{:S(2)}) %all-to-all-start) | async-done | bytes 720928 | tf_op jit(solution)/shard_map/all_to_all | solution.py:743
  31.9 2.8 %collective-permute-start.6 = (bf16[560,128]{1,0:T(8,128)(2,1)S(1)}, bf16[560,128]{1,0:T(8,128)(2,1)S(1)}, u32[]{:S(2)}, u32[]{:S(2)}) collective-permute-start(bf16[560,128]{1,0:T(8,128)(2,1)S(1)} %pad_maximum_fusion.2), channel_id=1, source_target_pairs={{0,30},{1,31},{2,28},{3,29},{4,26},{5,27},{6,24},{7,25},{8,22},{9,... | collective-permute-start | bytes 430088 | tf_op jit(solution)/shard_map/ppermute | solution.py:780
  34.7 2.7 %collective-permute-start.5 = (bf16[304,128]{1,0:T(8,128)(2,1)S(1)}, bf16[304,128]{1,0:T(8,128)(2,1)S(1)}, u32[]{:S(2)}, u32[]{:S(2)}) collective-permute-start(bf16[304,128]{1,0:T(8,128)(2,1)S(1)} %get-tuple-element.68), channel_id=1, source_target_pairs={{0,31},{1,30},{2,29},{3,28},{4,27},{5,26},{6,25},{7,24},{8,23},{9,... | collective-permute-start | bytes 233480 | tf_op jit(solution)/shard_map/ppermute | solution.py:780
  37.9 3.6 %weights_to_vmem.1.weight_ref = bf16[4,32,2,128,128]{4,3,2,1,0:T(8,128)(2,1)S(1)} custom-call(bf16[4,32,2,128,128]{4,3,2,1,0:T(8,128)(2,1)} %source_ref), custom_call_target="tpu_custom_call" | custom-call | bytes 16777216 | tf_op jit(solution)/shard_map/weights_to_vmem/pallas_call | solution.py:427
  43.5 2.7 %mode_back.1 = (bf16[4,64,128]{2,1,0:T(8,128)(2,1)S(1)}, bf16[4,64,128]{2,1,0:T(8,128)(2,1)S(1)}, bf16[48,128]{1,0:T(8,128)(2,1)S(1)}) custom-call(f32[64,128]{1,0:T(8,128)S(1)} %broadcast_in_dim.20.scale_ref, bf16[4,32,2,128,128]{4,3,2,1,0:T(8,128)(2,1)S(1)} %weights_to_vmem.1.weight_ref, bf16[304,128]{1,0:T(8,128)(2,1)S(1)} %get-tuple-element.67.refs_0_, ...), custom_call_target="tpu_custom_call" | custom-call | flops 16777216 | bytes 8388608 | tf_op jit(solution)/shard_map/mode_back/pallas_call | solution.py:485
  46.2 2.8 %collective-permute-start.10 = (bf16[4,64,128]{2,1,0:T(8,128)(2,1)S(1)}, bf16[4,64,128]{2,1,0:T(8,128)(2,1)S(1)}, u32[]{:S(2)}, u32[]{:S(2)}) collective-permute-start(bf16[4,64,128]{2,1,0:T(8,128)(2,1)S(1)} %get-tuple-element.72.refs_0_), channel_id=1, source_target_pairs={{0,31},{1,30},{2,29},{3,28},{4,27},{5,26},{6,25},{7,24},{8,23},{9,... | collective-permute-start | bytes 196616 | tf_op jit(solution)/shard_map/ppermute | solution.py:834
  49.0 1.4 %collective-permute-start.9 = (bf16[4,64,128]{2,1,0:T(8,128)(2,1)S(1)}, bf16[4,64,128]{2,1,0:T(8,128)(2,1)S(1)}, u32[]{:S(2)}, u32[]{:S(2)}) collective-permute-start(bf16[4,64,128]{2,1,0:T(8,128)(2,1)S(1)} %get-tuple-element.72.refs_0_), channel_id=1, source_target_pairs={{0,30},{1,31},{2,28},{3,29},{4,26},{5,27},{6,24},{7,25},{8,22},{9,... | collective-permute-start | bytes 196616 | tf_op jit(solution)/shard_map/ppermute | solution.py:834
  50.5 1.7 %collective-permute-start.8 = (bf16[4,64,128]{2,1,0:T(8,128)(2,1)S(1)}, bf16[4,64,128]{2,1,0:T(8,128)(2,1)S(1)}, u32[]{:S(2)}, u32[]{:S(2)}) collective-permute-start(bf16[4,64,128]{2,1,0:T(8,128)(2,1)S(1)} %get-tuple-element.72.refs_0_), channel_id=1, source_target_pairs={{0,1},{1,0},{2,3},{3,2},{4,5},{5,4},{6,7},{7,6},{8,9},{9,8},{10,11... | collective-permute-start | bytes 196616 | tf_op jit(solution)/shard_map/ppermute | solution.py:834
  52.2 2.1 %collective-permute-done.10.refs_3_ = bf16[4,64,128]{2,1,0:T(8,128)(2,1)S(1)} collective-permute-done((bf16[4,64,128]{2,1,0:T(8,128)(2,1)S(1)}, bf16[4,64,128]{2,1,0:T(8,128)(2,1)S(1)}, u32[]{:S(2)}, u32[]{:S(2)}) %collective-permute-start.10) | collective-permute-done | bytes 65568 | tf_op jit(solution)/shard_map/ppermute | solution.py:834
  54.3 1.3 %collective-permute-done.9.refs_2_ = bf16[4,64,128]{2,1,0:T(8,128)(2,1)S(1)} collective-permute-done((bf16[4,64,128]{2,1,0:T(8,128)(2,1)S(1)}, bf16[4,64,128]{2,1,0:T(8,128)(2,1)S(1)}, u32[]{:S(2)}, u32[]{:S(2)}) %collective-permute-start.9) | collective-permute-done | bytes 65568 | tf_op jit(solution)/shard_map/ppermute | solution.py:834
  56.1 1.4 %collective-permute-start.11 = (bf16[704,128]{1,0:T(8,128)(2,1)S(1)}, bf16[704,128]{1,0:T(8,128)(2,1)S(1)}, u32[]{:S(2)}, u32[]{:S(2)}) collective-permute-start(bf16[704,128]{1,0:T(8,128)(2,1)S(1)} %get-tuple-element.79), channel_id=1, source_target_pairs={{0,4},{2,6},{4,0},{6,2},{8,12},{10,14},{12,8},{14,10},{16,20},{18,... | collective-permute-start | bytes 540680 | tf_op jit(solution)/shard_map/ppermute | solution.py:751
  57.5 2.5 %collective-permute-start.12 = (bf16[704,128]{1,0:T(8,128)(2,1)S(1)}, bf16[704,128]{1,0:T(8,128)(2,1)S(1)}, u32[]{:S(2)}, u32[]{:S(2)}) collective-permute-start(bf16[704,128]{1,0:T(8,128)(2,1)S(1)} %get-tuple-element.80), channel_id=1, source_target_pairs={{0,8},{2,10},{4,12},{6,14},{8,0},{10,2},{12,4},{14,6},{16,24},{18,... | collective-permute-start | bytes 540680 | tf_op jit(solution)/shard_map/ppermute | solution.py:751
  60.3 4.9 %grad_spectral.1 = bf16[4,32,2,128,128]{4,3,2,1,0:T(8,128)(2,1)} custom-call(f32[64,128]{1,0:T(8,128)S(1)} %broadcast_in_dim.20.scale_ref, bf16[4,64,128]{2,1,0:T(8,128)(2,1)S(1)} %get-tuple-element.82.delta_ref, bf16[512,128]{1,0:T(8,128)(2,1)S(1)} %get-tuple-element.58.refs_0_, bf16[512,128]{1,0:T(8,128)(2,1)S(1)} %collective-permute-done.4.refs_1_, ...), custom_call_target="tpu_custom_call" | custom-call | flops 12582912 | bytes 8388608 | tf_op jit(solution)/shard_map/grad_spectral/pallas_call | solution.py:535
  65.4 3.2 %collective-permute-done.13.refs_3_ = bf16[704,128]{1,0:T(8,128)(2,1)S(1)} collective-permute-done((bf16[704,128]{1,0:T(8,128)(2,1)S(1)}, bf16[704,128]{1,0:T(8,128)(2,1)S(1)}, u32[]{:S(2)}, u32[]{:S(2)}) %collective-permute-start.13) | collective-permute-done | bytes 180256 | tf_op jit(solution)/shard_map/ppermute | solution.py:751
  68.8 1.7 %collective-permute-done.14.refs_4_ = bf16[1408,128]{1,0:T(8,128)(2,1)S(1)} collective-permute-done((bf16[1408,128]{1,0:T(8,128)(2,1)S(1)}, bf16[1408,128]{1,0:T(8,128)(2,1)S(1)}, u32[]{:S(2)}, u32[]{:S(2)}) %collective-permute-start.14) | collective-permute-done | bytes 360480 | tf_op jit(solution)/shard_map/ppermute | solution.py:757
  70.5 3.0 %x_inverse_and_local.1 = (bf16[256,32,128]{2,1,0:T(8,128)(2,1)}, f32[128,128]{1,0:T(8,128)}, f32[1,128]{1,0:T(1,128)}) custom-call(bf16[704,128]{1,0:T(8,128)(2,1)S(1)} %get-tuple-element.83.refs_0_, bf16[704,128]{1,0:T(8,128)(2,1)S(1)} %collective-permute-done.11.refs_1_, bf16[704,128]{1,0:T(8,128)(2,1)S(1)} %collective-permute-done.12.refs_2_, ...), custom_call_target="tpu_custom_call" | custom-call | flops 436207616 | bytes 5242880 | tf_op jit(solution)/shard_map/x_inverse_and_local/pallas_call | solution.py:677
  (48 shorter events, 5.6 us)
Async XLA Ops:
  3.7 12.5 %collective-permute-start = (bf16[640,128]{1,0:T(8,128)(2,1)}, bf16[640,128]{1,0:T(8,128)(2,1)S(1)}, u32[]{:S(2)}, u32[]{:S(2)}) collective-permute-start(bf16[640,128]{1,0:T(8,128)(2,1)} %get-tuple-element.50), channel_id=1, source_target_pairs={{0,4},{2,6},{4,0},{6,2},{8,12},{10,14},{12,8},{14,10},{16,20},{18,... | collective-permute-start | bytes 491528 | tf_op jit(solution)/shard_map/ppermute | solution.py:751
  6.6 9.6 %collective-permute-start.1 = (bf16[640,128]{1,0:T(8,128)(2,1)}, bf16[640,128]{1,0:T(8,128)(2,1)S(1)}, u32[]{:S(2)}, u32[]{:S(2)}) collective-permute-start(bf16[640,128]{1,0:T(8,128)(2,1)} %get-tuple-element.51), channel_id=1, source_target_pairs={{0,8},{2,10},{4,12},{6,14},{8,0},{10,2},{12,4},{14,6},{16,24},{18,... | collective-permute-start | bytes 491528 | tf_op jit(solution)/shard_map/ppermute | solution.py:751
  8.2 8.0 %collective-permute-start.2 = (bf16[640,128]{1,0:T(8,128)(2,1)}, bf16[640,128]{1,0:T(8,128)(2,1)S(1)}, u32[]{:S(2)}, u32[]{:S(2)}) collective-permute-start(bf16[640,128]{1,0:T(8,128)(2,1)} %get-tuple-element.52), channel_id=1, source_target_pairs={{0,12},{2,14},{4,8},{6,10},{8,4},{10,6},{12,0},{14,2},{16,28},{18,... | collective-permute-start | bytes 491528 | tf_op jit(solution)/shard_map/ppermute | solution.py:751
  8.2 12.3 %copy-start.1 = (bf16[640,128]{1,0:T(8,128)(2,1)S(1)}, bf16[640,128]{1,0:T(8,128)(2,1)}, u32[]{:S(2)}) copy-start(bf16[640,128]{1,0:T(8,128)(2,1)} %get-tuple-element.54.refs_0_) | copy-start | bytes 491524
  16.3 15.2 %all-to-all-start = ((bf16[8,352,128]{2,1,0:T(8,128)(2,1)}), bf16[8,352,128]{2,1,0:T(8,128)(2,1)S(1)}, u32[]{:S(2)}, u32[]{:S(2)}) async-start(bf16[8,352,128]{2,1,0:T(8,128)(2,1)} %get-tuple-element.53), calls=%async_computation | async-start | bytes 1441792 | tf_op jit(solution)/shard_map/all_to_all | solution.py:743
  20.6 2.0 %collective-permute-start.3 = (bf16[1280,128]{1,0:T(8,128)(2,1)S(1)}, bf16[1280,128]{1,0:T(8,128)(2,1)S(1)}, u32[]{:S(2)}, u32[]{:S(2)}) collective-permute-start(bf16[1280,128]{1,0:T(8,128)(2,1)S(1)} %pad_maximum_fusion.1), channel_id=1, source_target_pairs={{0,2},{2,0},{4,6},{6,4},{8,10},{10,8},{12,14},{14,12},{16,18},{18,... | collective-permute-start | bytes 983048 | tf_op jit(solution)/shard_map/ppermute | solution.py:757
  23.2 5.6 %collective-permute-start.4 = (bf16[512,128]{1,0:T(8,128)(2,1)S(1)}, bf16[512,128]{1,0:T(8,128)(2,1)S(1)}, u32[]{:S(2)}, u32[]{:S(2)}) collective-permute-start(bf16[512,128]{1,0:T(8,128)(2,1)S(1)} %get-tuple-element.59), channel_id=1, source_target_pairs={{0,1},{1,0},{2,3},{3,2},{4,5},{5,4},{6,7},{7,6},{8,9},{9,8},{10,11... | collective-permute-start | bytes 393224 | tf_op jit(solution)/shard_map/ppermute | solution.py:806
  31.9 9.6 %collective-permute-start.6 = (bf16[560,128]{1,0:T(8,128)(2,1)S(1)}, bf16[560,128]{1,0:T(8,128)(2,1)S(1)}, u32[]{:S(2)}, u32[]{:S(2)}) collective-permute-start(bf16[560,128]{1,0:T(8,128)(2,1)S(1)} %pad_maximum_fusion.2), channel_id=1, source_target_pairs={{0,30},{1,31},{2,28},{3,29},{4,26},{5,27},{6,24},{7,25},{8,22},{9,... | collective-permute-start | bytes 430088 | tf_op jit(solution)/shard_map/ppermute | solution.py:780
  34.7 7.8 %collective-permute-start.5 = (bf16[304,128]{1,0:T(8,128)(2,1)S(1)}, bf16[304,128]{1,0:T(8,128)(2,1)S(1)}, u32[]{:S(2)}, u32[]{:S(2)}) collective-permute-start(bf16[304,128]{1,0:T(8,128)(2,1)S(1)} %get-tuple-element.68), channel_id=1, source_target_pairs={{0,31},{1,30},{2,29},{3,28},{4,27},{5,26},{6,25},{7,24},{8,23},{9,... | collective-permute-start | bytes 233480 | tf_op jit(solution)/shard_map/ppermute | solution.py:780
  37.4 6.1 %collective-permute-start.7 = (bf16[304,128]{1,0:T(8,128)(2,1)S(1)}, bf16[304,128]{1,0:T(8,128)(2,1)S(1)}, u32[]{:S(2)}, u32[]{:S(2)}) collective-permute-start(bf16[304,128]{1,0:T(8,128)(2,1)S(1)} %get-tuple-element.70), channel_id=1, source_target_pairs={{0,1},{1,0},{2,3},{3,2},{4,5},{5,4},{6,7},{7,6},{8,9},{9,8},{10,11... | collective-permute-start | bytes 233480 | tf_op jit(solution)/shard_map/ppermute | solution.py:780
  46.2 8.0 %collective-permute-start.10 = (bf16[4,64,128]{2,1,0:T(8,128)(2,1)S(1)}, bf16[4,64,128]{2,1,0:T(8,128)(2,1)S(1)}, u32[]{:S(2)}, u32[]{:S(2)}) collective-permute-start(bf16[4,64,128]{2,1,0:T(8,128)(2,1)S(1)} %get-tuple-element.72.refs_0_), channel_id=1, source_target_pairs={{0,31},{1,30},{2,29},{3,28},{4,27},{5,26},{6,25},{7,24},{8,23},{9,... | collective-permute-start | bytes 196616 | tf_op jit(solution)/shard_map/ppermute | solution.py:834
  49.0 6.5 %collective-permute-start.9 = (bf16[4,64,128]{2,1,0:T(8,128)(2,1)S(1)}, bf16[4,64,128]{2,1,0:T(8,128)(2,1)S(1)}, u32[]{:S(2)}, u32[]{:S(2)}) collective-permute-start(bf16[4,64,128]{2,1,0:T(8,128)(2,1)S(1)} %get-tuple-element.72.refs_0_), channel_id=1, source_target_pairs={{0,30},{1,31},{2,28},{3,29},{4,26},{5,27},{6,24},{7,25},{8,22},{9,... | collective-permute-start | bytes 196616 | tf_op jit(solution)/shard_map/ppermute | solution.py:834
  50.5 5.2 %collective-permute-start.8 = (bf16[4,64,128]{2,1,0:T(8,128)(2,1)S(1)}, bf16[4,64,128]{2,1,0:T(8,128)(2,1)S(1)}, u32[]{:S(2)}, u32[]{:S(2)}) collective-permute-start(bf16[4,64,128]{2,1,0:T(8,128)(2,1)S(1)} %get-tuple-element.72.refs_0_), channel_id=1, source_target_pairs={{0,1},{1,0},{2,3},{3,2},{4,5},{5,4},{6,7},{7,6},{8,9},{9,8},{10,11... | collective-permute-start | bytes 196616 | tf_op jit(solution)/shard_map/ppermute | solution.py:834
  56.1 9.1 %collective-permute-start.11 = (bf16[704,128]{1,0:T(8,128)(2,1)S(1)}, bf16[704,128]{1,0:T(8,128)(2,1)S(1)}, u32[]{:S(2)}, u32[]{:S(2)}) collective-permute-start(bf16[704,128]{1,0:T(8,128)(2,1)S(1)} %get-tuple-element.79), channel_id=1, source_target_pairs={{0,4},{2,6},{4,0},{6,2},{8,12},{10,14},{12,8},{14,10},{16,20},{18,... | collective-permute-start | bytes 540680 | tf_op jit(solution)/shard_map/ppermute | solution.py:751
  57.5 7.9 %collective-permute-start.12 = (bf16[704,128]{1,0:T(8,128)(2,1)S(1)}, bf16[704,128]{1,0:T(8,128)(2,1)S(1)}, u32[]{:S(2)}, u32[]{:S(2)}) collective-permute-start(bf16[704,128]{1,0:T(8,128)(2,1)S(1)} %get-tuple-element.80), channel_id=1, source_target_pairs={{0,8},{2,10},{4,12},{6,14},{8,0},{10,2},{12,4},{14,6},{16,24},{18,... | collective-permute-start | bytes 540680 | tf_op jit(solution)/shard_map/ppermute | solution.py:751
  60.1 8.6 %collective-permute-start.13 = (bf16[704,128]{1,0:T(8,128)(2,1)S(1)}, bf16[704,128]{1,0:T(8,128)(2,1)S(1)}, u32[]{:S(2)}, u32[]{:S(2)}) collective-permute-start(bf16[704,128]{1,0:T(8,128)(2,1)S(1)} %get-tuple-element.81), channel_id=1, source_target_pairs={{0,12},{2,14},{4,8},{6,10},{8,4},{10,6},{12,0},{14,2},{16,28},{18,... | collective-permute-start | bytes 540680 | tf_op jit(solution)/shard_map/ppermute | solution.py:751
  60.3 10.2 %copy-start = (bf16[256,32,128]{2,1,0:T(8,128)(2,1)S(1)}, bf16[256,32,128]{2,1,0:T(8,128)(2,1)}, u32[]{:S(2)}) copy-start(bf16[256,32,128]{2,1,0:T(8,128)(2,1)} %get-tuple-element.87.refs_5_) | copy-start | bytes 6291460
  60.3 10.2 %copy-start.2 = (bf16[128,128]{1,0:T(8,128)(2,1)S(1)}, bf16[128,128]{1,0:T(8,128)(2,1)}, u32[]{:S(2)}) copy-start(bf16[128,128]{1,0:T(8,128)(2,1)} %refs_6_.1) | copy-start | bytes 98308
  68.8 1.7 %collective-permute-start.14 = (bf16[1408,128]{1,0:T(8,128)(2,1)S(1)}, bf16[1408,128]{1,0:T(8,128)(2,1)S(1)}, u32[]{:S(2)}, u32[]{:S(2)}) collective-permute-start(bf16[1408,128]{1,0:T(8,128)(2,1)S(1)} %pad_maximum_fusion), channel_id=1, source_target_pairs={{0,2},{2,0},{4,6},{6,4},{8,10},{10,8},{12,14},{14,12},{16,18},{18,... | collective-permute-start | bytes 1081352 | tf_op jit(solution)/shard_map/ppermute | solution.py:757

commit v8 on v7

--- a/solution.py
+++ b/solution.py
@@ -504,8 +504,13 @@
     )(scale_rows, weight, *parts)
 
 
-def outer_kernel(scale_ref, delta_ref, *refs):
-    part_refs, out_ref = refs[:-1], refs[-1]
+def outer_kernel(sizes, scale_ref, delta_ref, *refs):
+    part_refs, (out_ref, table_ref) = refs[:-2], refs[-2:]
+
+    @pl.when(pl.program_id(0) == 0)
+    def _():
+        table_ref[...] = x_table(sizes, transposed=True, relative=True)
+
     modes = out_ref.shape[1]
     channels = out_ref.shape[-1]
     total = part_refs[0][...].astype(f32)
@@ -528,20 +533,27 @@
             out_ref[0, first + i // 2, i % 2] = product[:, i * channels : (i + 1) * channels]
 
 
-def outer_call(scale_rows, delta, parts):
+def outer_call(sizes, scale_rows, delta, parts):
+    table = (sizes[2], 2 * sizes[0] * (sizes[1] + 1))
     held, rows, channels = delta.shape
     modes = rows // 2
     part = pl.BlockSpec((1, rows, channels), lambda j: (j, 0, 0))
     return pl.pallas_call(
-        outer_kernel,
+        functools.partial(outer_kernel, sizes),
         grid=(held,),
         in_specs=[whole((rows, channels)), part]
         + [
             pl.BlockSpec((rows, channels), lambda j, first=first: (j + first, 0))
             for _, first in parts
         ],
-        out_specs=pl.BlockSpec((1, modes, 2, channels, channels), lambda j: (j, 0, 0, 0, 0)),
-        out_shape=jax.ShapeDtypeStruct((held, modes, 2, channels, channels), bf16),
+        out_specs=[
+            pl.BlockSpec((1, modes, 2, channels, channels), lambda j: (j, 0, 0, 0, 0)),
+            whole(table),
+        ],
+        out_shape=[
+            jax.ShapeDtypeStruct((held, modes, 2, channels, channels), bf16),
+            jax.ShapeDtypeStruct(table, bf16),
+        ],
         compiler_params=params(),
         cost_estimate=pl.CostEstimate(
             flops=6 * held * modes * channels * channels,
@@ -617,19 +629,15 @@
     )(table, share, *parts)
 
 
-def final_kernel(sizes, places, arrays, *refs):
+def final_kernel(places, arrays, *refs):
     line_refs, refs = refs[:arrays], refs[arrays:]
-    delta_ref, weight_ref, out_ref, local_ref, bias_ref, table = refs
+    delta_ref, weight_ref, table, out_ref, local_ref, bias_ref = refs
     grid_rows, columns, channels = out_ref.shape
     half = len(places)
     block = pl.program_id(0)
     all_columns = columns * pl.num_programs(0)
     per_source = table.shape[1] // half
     first = pl.multiple_of(block * columns, columns)
-
-    @pl.when(block == 0)
-    def _():
-        table[...] = x_table(sizes, transposed=True, relative=True)
 
     lines = jnp.stack(
         [
@@ -669,28 +677,27 @@
         bias_ref[...] = in_relative_order(biases, half)[0]
 
 
-def final_call(sizes, lines, places, delta, local_weight):
+def final_call(table, lines, places, delta, local_weight):
     grid_rows, columns, channels = delta.shape
-    rows = 2 * sizes[0] * (sizes[1] + 1)
+    rows = table.shape[1]
     block = min(16, columns)
     field = pl.BlockSpec((grid_rows, block, channels), lambda i: (0, i, 0))
     return pl.pallas_call(
-        functools.partial(final_kernel, sizes, places, len(lines)),
+        functools.partial(final_kernel, places, len(lines)),
         grid=(columns // block,),
-        in_specs=[whole(line.shape) for line in lines] + [field, whole(local_weight.shape)],
+        in_specs=[whole(line.shape) for line in lines] + [field, whole(local_weight.shape), whole(table.shape)],
         out_specs=[field, whole((channels, channels)), whole((1, channels))],
         out_shape=[
             jax.ShapeDtypeStruct(delta.shape, bf16),
             jax.ShapeDtypeStruct((channels, channels), f32),
             jax.ShapeDtypeStruct((1, channels), f32),
         ],
-        scratch_shapes=[pltpu.VMEM((grid_rows, rows), bf16)],
         compiler_params=params(),
         cost_estimate=pl.CostEstimate(
             flops=2 * (rows + channels) * delta.size, bytes_accessed=5 * delta.size, transcendentals=0
         ),
         name="x_inverse_and_local",
-    )(*lines, delta, local_weight)
+    )(*lines, delta, local_weight, table)
 
 
 def on_device(field_in, pre_act, cotangent, spec_weight, local_weight):
@@ -838,10 +845,10 @@
     column_sums = y_inverse_call(relative_table, share_rows, modes, half, col_block)
     column_sums, delta_owned = tied((column_sums, delta_owned))
     columns = to_chips(column_sums)
-    grad_spectral = outer_call(scale_rows, delta_owned, input_held)
+    grad_spectral, x_basis = outer_call(sizes, scale_rows, delta_owned, input_held)
     columns, grad_spectral = tied((columns, grad_spectral))
     lines, places = between_cores(columns)
-    grad_input, grad_local, bias_rows = final_call(sizes, lines, places, delta, local_weight)
+    grad_input, grad_local, bias_rows = final_call(x_basis, lines, places, delta, local_weight)
     return (grad_input[None], grad_spectral, grad_local, bias_rows.reshape(channels))
 
 

time: 73.8 us -> 73.6 us (level)
  no operation moved by 1% of the time
where the time goes in v8:
time: 73.6 us; the launch traced here: 73.4 us
  starting transfers between devices  27.1 us (37%)
  Pallas kernels  26.6 us (36%)
  waiting for transfers between devices  17 us (23%)
  other arithmetic  1.41 us (2%)
  between operations  0.89 us (1%)
    ppermute x6, starting transfers between devices, to_chips(): arrived.append(lax.ppermute(chips[pair], 'dp', moves))  8.68 us
    pallas_call x1, Pallas kernels, delta_call(): pl.pallas_call(functools.partial(delta_kernel, sizes), grid=(columns // b...  7.95 us
    ppermute x3, starting transfers between devices, on_device(): lax.ppermute(back, ('dp', 'space'), pairs(mirror, shift))  5.98 us
    ppermute x3, starting transfers between devices, gathered(): lax.ppermute(parts[mirror * space_count + shift], ('dp', 'space'), pairs(...  5.97 us
    pallas_call x1, Pallas kernels, outer_call(): pl.pallas_call(functools.partial(outer_kernel, sizes), grid=(held,), in_s...  5.05 us
    all_to_all x1, starting transfers between devices, exchange(): lax.all_to_all(values, 'dp', split_axis=0, concat_axis=0, tiled=True, axi...  4.21 us
    ppermute x1, waiting for transfers between devices, on_device(): lax.ppermute(input_parts[shift], ('dp', 'space'), pairs(0, shift))  4.02 us
    pallas_call x1, Pallas kernels, load_call(): pl.pallas_call(load_kernel, in_specs=[pl.BlockSpec(memory_space=pl.ANY)],...  3.57 us
  transfers between devices with their start and end apart: 16, of which 10 were waited for; matrix products, arithmetic and copies ran while one was open for 2% of the time, Pallas kernels for 23%

profile of v8, /device:TPU:0, one launch (start us, length us, event | category | flops | bytes accessed | tf_op | source)
XLA Modules:
  0.0 73.4 jit_solution(3368001367287805183)
XLA Ops:
  0.6 3.1 %input_x_sums.1 = (bf16[640,128]{1,0:T(8,128)(2,1)}, bf16[640,128]{1,0:T(8,128)(2,1)}, bf16[640,128]{1,0:T(8,128)(2,1)}, bf16[640,128]{1,0:T(8,128)(2,1)}) custom-call(bf16[256,32,128]{2,1,0:T(8,128)(2,1)} %bitcast.7, bf16[256,32,128]{2,1,0:T(8,128)(2,1)} %bitcast.8, bf16[256,32,128]{2,1,0:T(8,128)(2,1)} %bitcast.9, bf16[256,32,128]{2,1,0:T(8,128)(2,1)} %bitcast.10), custom_call_target="tpu_custom_call" | custom-call | flops 167772160 | bytes 4194304 | tf_op jit(solution)/shard_map/input_x_sums/pallas_call | solution.py:289
  3.7 2.9 %collective-permute-start = (bf16[640,128]{1,0:T(8,128)(2,1)}, bf16[640,128]{1,0:T(8,128)(2,1)S(1)}, u32[]{:S(2)}, u32[]{:S(2)}) collective-permute-start(bf16[640,128]{1,0:T(8,128)(2,1)} %get-tuple-element.52), channel_id=1, source_target_pairs={{0,4},{2,6},{4,0},{6,2},{8,12},{10,14},{12,8},{14,10},{16,20},{18,... | collective-permute-start | bytes 491528 | tf_op jit(solution)/shard_map/ppermute | solution.py:758
  6.6 1.6 %collective-permute-start.1 = (bf16[640,128]{1,0:T(8,128)(2,1)}, bf16[640,128]{1,0:T(8,128)(2,1)S(1)}, u32[]{:S(2)}, u32[]{:S(2)}) collective-permute-start(bf16[640,128]{1,0:T(8,128)(2,1)} %get-tuple-element.53), channel_id=1, source_target_pairs={{0,8},{2,10},{4,12},{6,14},{8,0},{10,2},{12,4},{14,6},{16,24},{18,... | collective-permute-start | bytes 491528 | tf_op jit(solution)/shard_map/ppermute | solution.py:758
  8.2 7.9 %delta_and_x_sums.1 = (bf16[256,32,128]{2,1,0:T(8,128)(2,1)}, bf16[8,352,128]{2,1,0:T(8,128)(2,1)}) custom-call(bf16[256,32,128]{2,1,0:T(8,128)(2,1)} %bitcast.12, bf16[256,32,128]{2,1,0:T(8,128)(2,1)} %bitcast.13, bf16[256,32,128]{2,1,0:T(8,128)(2,1)} %bitcast.11), custom_call_target="tpu_custom_call" | custom-call | flops 335544320 | bytes 8388608 | tf_op jit(solution)/shard_map/delta_and_x_sums/pallas_call | solution.py:235
  16.3 4.2 %all-to-all-start = ((bf16[8,352,128]{2,1,0:T(8,128)(2,1)}), bf16[8,352,128]{2,1,0:T(8,128)(2,1)S(1)}, u32[]{:S(2)}, u32[]{:S(2)}) async-start(bf16[8,352,128]{2,1,0:T(8,128)(2,1)} %get-tuple-element.55), calls=%async_computation | async-start | bytes 1441792 | tf_op jit(solution)/shard_map/all_to_all | solution.py:750
  21.4 1.3 %fusion.1 = (bf16[256,512]{1,0:T(8,128)(2,1)S(1)}, bf16[256,512]{1,0:T(8,128)(2,1)S(1)}) fusion(s32[256,256]{1,0:T(8,128)S(1)} %broadcast_in_dim.17, s32[256,256]{1,0:T(8,128)S(1)} %broadcast_in_dim.16, s32[512]{0:T(512)S(1)} %pad_add_fusion.1, s32[256]{0:T(256)S(1)} %fusion.23, s32[512]{0:T(512)S(1)} %pad_add_fusion), kind=kLoop, calls=%fused_computation.3 | loop fusion | flops 9699328 | bytes 1053696 | tf_op jit(solution)/shard_map/convert_element_type | solution.py:44
  23.2 1.6 %collective-permute-start.4 = (bf16[512,128]{1,0:T(8,128)(2,1)S(1)}, bf16[512,128]{1,0:T(8,128)(2,1)S(1)}, u32[]{:S(2)}, u32[]{:S(2)}) collective-permute-start(bf16[512,128]{1,0:T(8,128)(2,1)S(1)} %get-tuple-element.61), channel_id=1, source_target_pairs={{0,1},{1,0},{2,3},{3,2},{4,5},{5,4},{6,7},{7,6},{8,9},{9,8},{10,11... | collective-permute-start | bytes 393224 | tf_op jit(solution)/shard_map/ppermute | solution.py:813
  24.7 4.0 %collective-permute-done.4.refs_1_ = bf16[512,128]{1,0:T(8,128)(2,1)S(1)} collective-permute-done((bf16[512,128]{1,0:T(8,128)(2,1)S(1)}, bf16[512,128]{1,0:T(8,128)(2,1)S(1)}, u32[]{:S(2)}, u32[]{:S(2)}) %collective-permute-start.4) | collective-permute-done | bytes 131104 | tf_op jit(solution)/shard_map/ppermute | solution.py:813
  28.8 2.6 %all-to-all-done = bf16[8,352,128]{2,1,0:T(8,128)(2,1)S(1)} async-done(((bf16[8,352,128]{2,1,0:T(8,128)(2,1)}), bf16[8,352,128]{2,1,0:T(8,128)(2,1)S(1)}, u32[]{:S(2)}, u32[]{:S(2)}) %all-to-all-start) | async-done | bytes 720928 | tf_op jit(solution)/shard_map/all_to_all | solution.py:750
  31.9 2.8 %collective-permute-start.6 = (bf16[560,128]{1,0:T(8,128)(2,1)S(1)}, bf16[560,128]{1,0:T(8,128)(2,1)S(1)}, u32[]{:S(2)}, u32[]{:S(2)}) collective-permute-start(bf16[560,128]{1,0:T(8,128)(2,1)S(1)} %pad_maximum_fusion.2), channel_id=1, source_target_pairs={{0,30},{1,31},{2,28},{3,29},{4,26},{5,27},{6,24},{7,25},{8,22},{9,... | collective-permute-start | bytes 430088 | tf_op jit(solution)/shard_map/ppermute | solution.py:787
  34.7 2.7 %collective-permute-start.5 = (bf16[304,128]{1,0:T(8,128)(2,1)S(1)}, bf16[304,128]{1,0:T(8,128)(2,1)S(1)}, u32[]{:S(2)}, u32[]{:S(2)}) collective-permute-start(bf16[304,128]{1,0:T(8,128)(2,1)S(1)} %get-tuple-element.70), channel_id=1, source_target_pairs={{0,31},{1,30},{2,29},{3,28},{4,27},{5,26},{6,25},{7,24},{8,23},{9,... | collective-permute-start | bytes 233480 | tf_op jit(solution)/shard_map/ppermute | solution.py:787
  37.9 3.6 %weights_to_vmem.1.weight_ref = bf16[4,32,2,128,128]{4,3,2,1,0:T(8,128)(2,1)S(1)} custom-call(bf16[4,32,2,128,128]{4,3,2,1,0:T(8,128)(2,1)} %source_ref), custom_call_target="tpu_custom_call" | custom-call | bytes 16777216 | tf_op jit(solution)/shard_map/weights_to_vmem/pallas_call | solution.py:427
  43.5 2.7 %mode_back.1 = (bf16[4,64,128]{2,1,0:T(8,128)(2,1)S(1)}, bf16[4,64,128]{2,1,0:T(8,128)(2,1)S(1)}, bf16[48,128]{1,0:T(8,128)(2,1)S(1)}) custom-call(f32[64,128]{1,0:T(8,128)S(1)} %broadcast_in_dim.20.scale_ref, bf16[4,32,2,128,128]{4,3,2,1,0:T(8,128)(2,1)S(1)} %weights_to_vmem.1.weight_ref, bf16[304,128]{1,0:T(8,128)(2,1)S(1)} %get-tuple-element.69.refs_0_, ...), custom_call_target="tpu_custom_call" | custom-call | flops 16777216 | bytes 8388608 | tf_op jit(solution)/shard_map/mode_back/pallas_call | solution.py:485
  46.2 2.8 %collective-permute-start.10 = (bf16[4,64,128]{2,1,0:T(8,128)(2,1)S(1)}, bf16[4,64,128]{2,1,0:T(8,128)(2,1)S(1)}, u32[]{:S(2)}, u32[]{:S(2)}) collective-permute-start(bf16[4,64,128]{2,1,0:T(8,128)(2,1)S(1)} %get-tuple-element.74.refs_0_), channel_id=1, source_target_pairs={{0,31},{1,30},{2,29},{3,28},{4,27},{5,26},{6,25},{7,24},{8,23},{9,... | collective-permute-start | bytes 196616 | tf_op jit(solution)/shard_map/ppermute | solution.py:841
  49.1 1.4 %collective-permute-start.9 = (bf16[4,64,128]{2,1,0:T(8,128)(2,1)S(1)}, bf16[4,64,128]{2,1,0:T(8,128)(2,1)S(1)}, u32[]{:S(2)}, u32[]{:S(2)}) collective-permute-start(bf16[4,64,128]{2,1,0:T(8,128)(2,1)S(1)} %get-tuple-element.74.refs_0_), channel_id=1, source_target_pairs={{0,30},{1,31},{2,28},{3,29},{4,26},{5,27},{6,24},{7,25},{8,22},{9,... | collective-permute-start | bytes 196616 | tf_op jit(solution)/shard_map/ppermute | solution.py:841
  50.5 1.7 %collective-permute-start.8 = (bf16[4,64,128]{2,1,0:T(8,128)(2,1)S(1)}, bf16[4,64,128]{2,1,0:T(8,128)(2,1)S(1)}, u32[]{:S(2)}, u32[]{:S(2)}) collective-permute-start(bf16[4,64,128]{2,1,0:T(8,128)(2,1)S(1)} %get-tuple-element.74.refs_0_), channel_id=1, source_target_pairs={{0,1},{1,0},{2,3},{3,2},{4,5},{5,4},{6,7},{7,6},{8,9},{9,8},{10,11... | collective-permute-start | bytes 196616 | tf_op jit(solution)/shard_map/ppermute | solution.py:841
  52.2 2.1 %collective-permute-done.10.refs_3_ = bf16[4,64,128]{2,1,0:T(8,128)(2,1)S(1)} collective-permute-done((bf16[4,64,128]{2,1,0:T(8,128)(2,1)S(1)}, bf16[4,64,128]{2,1,0:T(8,128)(2,1)S(1)}, u32[]{:S(2)}, u32[]{:S(2)}) %collective-permute-start.10) | collective-permute-done | bytes 65568 | tf_op jit(solution)/shard_map/ppermute | solution.py:841
  54.3 1.3 %collective-permute-done.9.refs_2_ = bf16[4,64,128]{2,1,0:T(8,128)(2,1)S(1)} collective-permute-done((bf16[4,64,128]{2,1,0:T(8,128)(2,1)S(1)}, bf16[4,64,128]{2,1,0:T(8,128)(2,1)S(1)}, u32[]{:S(2)}, u32[]{:S(2)}) %collective-permute-start.9) | collective-permute-done | bytes 65568 | tf_op jit(solution)/shard_map/ppermute | solution.py:841
  56.1 1.4 %collective-permute-start.11 = (bf16[704,128]{1,0:T(8,128)(2,1)S(1)}, bf16[704,128]{1,0:T(8,128)(2,1)S(1)}, u32[]{:S(2)}, u32[]{:S(2)}) collective-permute-start(bf16[704,128]{1,0:T(8,128)(2,1)S(1)} %get-tuple-element.81), channel_id=1, source_target_pairs={{0,4},{2,6},{4,0},{6,2},{8,12},{10,14},{12,8},{14,10},{16,20},{18,... | collective-permute-start | bytes 540680 | tf_op jit(solution)/shard_map/ppermute | solution.py:758
  57.5 2.5 %collective-permute-start.12 = (bf16[704,128]{1,0:T(8,128)(2,1)S(1)}, bf16[704,128]{1,0:T(8,128)(2,1)S(1)}, u32[]{:S(2)}, u32[]{:S(2)}) collective-permute-start(bf16[704,128]{1,0:T(8,128)(2,1)S(1)} %get-tuple-element.82), channel_id=1, source_target_pairs={{0,8},{2,10},{4,12},{6,14},{8,0},{10,2},{12,4},{14,6},{16,24},{18,... | collective-permute-start | bytes 540680 | tf_op jit(solution)/shard_map/ppermute | solution.py:758
  60.3 5.1 %grad_spectral.1 = (bf16[4,32,2,128,128]{4,3,2,1,0:T(8,128)(2,1)}, bf16[256,80]{1,0:T(8,128)(2,1)S(1)}) custom-call(f32[64,128]{1,0:T(8,128)S(1)} %broadcast_in_dim.20.scale_ref, bf16[4,64,128]{2,1,0:T(8,128)(2,1)S(1)} %get-tuple-element.84.delta_ref, bf16[512,128]{1,0:T(8,128)(2,1)S(1)} %get-tuple-element.60.refs_0_, ...), custom_call_target="tpu_custom_call" | custom-call | flops 12582912 | bytes 8388608 | tf_op jit(solution)/shard_map/grad_spectral/pallas_call | solution.py:541
  65.5 3.2 %collective-permute-done.13.refs_3_ = bf16[704,128]{1,0:T(8,128)(2,1)S(1)} collective-permute-done((bf16[704,128]{1,0:T(8,128)(2,1)S(1)}, bf16[704,128]{1,0:T(8,128)(2,1)S(1)}, u32[]{:S(2)}, u32[]{:S(2)}) %collective-permute-start.13) | collective-permute-done | bytes 180256 | tf_op jit(solution)/shard_map/ppermute | solution.py:758
  68.9 1.7 %collective-permute-done.14.refs_4_ = bf16[1408,128]{1,0:T(8,128)(2,1)S(1)} collective-permute-done((bf16[1408,128]{1,0:T(8,128)(2,1)S(1)}, bf16[1408,128]{1,0:T(8,128)(2,1)S(1)}, u32[]{:S(2)}, u32[]{:S(2)}) %collective-permute-start.14) | collective-permute-done | bytes 360480 | tf_op jit(solution)/shard_map/ppermute | solution.py:764
  70.5 2.9 %x_inverse_and_local.1 = (bf16[256,32,128]{2,1,0:T(8,128)(2,1)}, f32[128,128]{1,0:T(8,128)}, f32[1,128]{1,0:T(1,128)}) custom-call(bf16[704,128]{1,0:T(8,128)(2,1)S(1)} %get-tuple-element.86.refs_0_, bf16[704,128]{1,0:T(8,128)(2,1)S(1)} %collective-permute-done.11.refs_1_, bf16[704,128]{1,0:T(8,128)(2,1)S(1)} %collective-permute-done.12.refs_2_, ...), custom_call_target="tpu_custom_call" | custom-call | flops 436207616 | bytes 5242880 | tf_op jit(solution)/shard_map/x_inverse_and_local/pallas_call | solution.py:685
  (48 shorter events, 5.5 us)
Async XLA Ops:
  3.7 12.5 %collective-permute-start = (bf16[640,128]{1,0:T(8,128)(2,1)}, bf16[640,128]{1,0:T(8,128)(2,1)S(1)}, u32[]{:S(2)}, u32[]{:S(2)}) collective-permute-start(bf16[640,128]{1,0:T(8,128)(2,1)} %get-tuple-element.52), channel_id=1, source_target_pairs={{0,4},{2,6},{4,0},{6,2},{8,12},{10,14},{12,8},{14,10},{16,20},{18,... | collective-permute-start | bytes 491528 | tf_op jit(solution)/shard_map/ppermute | solution.py:758
  6.6 9.6 %collective-permute-start.1 = (bf16[640,128]{1,0:T(8,128)(2,1)}, bf16[640,128]{1,0:T(8,128)(2,1)S(1)}, u32[]{:S(2)}, u32[]{:S(2)}) collective-permute-start(bf16[640,128]{1,0:T(8,128)(2,1)} %get-tuple-element.53), channel_id=1, source_target_pairs={{0,8},{2,10},{4,12},{6,14},{8,0},{10,2},{12,4},{14,6},{16,24},{18,... | collective-permute-start | bytes 491528 | tf_op jit(solution)/shard_map/ppermute | solution.py:758
  8.2 8.0 %collective-permute-start.2 = (bf16[640,128]{1,0:T(8,128)(2,1)}, bf16[640,128]{1,0:T(8,128)(2,1)S(1)}, u32[]{:S(2)}, u32[]{:S(2)}) collective-permute-start(bf16[640,128]{1,0:T(8,128)(2,1)} %get-tuple-element.54), channel_id=1, source_target_pairs={{0,12},{2,14},{4,8},{6,10},{8,4},{10,6},{12,0},{14,2},{16,28},{18,... | collective-permute-start | bytes 491528 | tf_op jit(solution)/shard_map/ppermute | solution.py:758
  8.2 12.3 %copy-start.1 = (bf16[640,128]{1,0:T(8,128)(2,1)S(1)}, bf16[640,128]{1,0:T(8,128)(2,1)}, u32[]{:S(2)}) copy-start(bf16[640,128]{1,0:T(8,128)(2,1)} %get-tuple-element.56.refs_0_) | copy-start | bytes 491524
  16.3 15.2 %all-to-all-start = ((bf16[8,352,128]{2,1,0:T(8,128)(2,1)}), bf16[8,352,128]{2,1,0:T(8,128)(2,1)S(1)}, u32[]{:S(2)}, u32[]{:S(2)}) async-start(bf16[8,352,128]{2,1,0:T(8,128)(2,1)} %get-tuple-element.55), calls=%async_computation | async-start | bytes 1441792 | tf_op jit(solution)/shard_map/all_to_all | solution.py:750
  20.6 2.0 %collective-permute-start.3 = (bf16[1280,128]{1,0:T(8,128)(2,1)S(1)}, bf16[1280,128]{1,0:T(8,128)(2,1)S(1)}, u32[]{:S(2)}, u32[]{:S(2)}) collective-permute-start(bf16[1280,128]{1,0:T(8,128)(2,1)S(1)} %pad_maximum_fusion.1), channel_id=1, source_target_pairs={{0,2},{2,0},{4,6},{6,4},{8,10},{10,8},{12,14},{14,12},{16,18},{18,... | collective-permute-start | bytes 983048 | tf_op jit(solution)/shard_map/ppermute | solution.py:764
  23.2 5.6 %collective-permute-start.4 = (bf16[512,128]{1,0:T(8,128)(2,1)S(1)}, bf16[512,128]{1,0:T(8,128)(2,1)S(1)}, u32[]{:S(2)}, u32[]{:S(2)}) collective-permute-start(bf16[512,128]{1,0:T(8,128)(2,1)S(1)} %get-tuple-element.61), channel_id=1, source_target_pairs={{0,1},{1,0},{2,3},{3,2},{4,5},{5,4},{6,7},{7,6},{8,9},{9,8},{10,11... | collective-permute-start | bytes 393224 | tf_op jit(solution)/shard_map/ppermute | solution.py:813
  31.9 9.6 %collective-permute-start.6 = (bf16[560,128]{1,0:T(8,128)(2,1)S(1)}, bf16[560,128]{1,0:T(8,128)(2,1)S(1)}, u32[]{:S(2)}, u32[]{:S(2)}) collective-permute-start(bf16[560,128]{1,0:T(8,128)(2,1)S(1)} %pad_maximum_fusion.2), channel_id=1, source_target_pairs={{0,30},{1,31},{2,28},{3,29},{4,26},{5,27},{6,24},{7,25},{8,22},{9,... | collective-permute-start | bytes 430088 | tf_op jit(solution)/shard_map/ppermute | solution.py:787
  34.7 7.8 %collective-permute-start.5 = (bf16[304,128]{1,0:T(8,128)(2,1)S(1)}, bf16[304,128]{1,0:T(8,128)(2,1)S(1)}, u32[]{:S(2)}, u32[]{:S(2)}) collective-permute-start(bf16[304,128]{1,0:T(8,128)(2,1)S(1)} %get-tuple-element.70), channel_id=1, source_target_pairs={{0,31},{1,30},{2,29},{3,28},{4,27},{5,26},{6,25},{7,24},{8,23},{9,... | collective-permute-start | bytes 233480 | tf_op jit(solution)/shard_map/ppermute | solution.py:787
  37.4 6.1 %collective-permute-start.7 = (bf16[304,128]{1,0:T(8,128)(2,1)S(1)}, bf16[304,128]{1,0:T(8,128)(2,1)S(1)}, u32[]{:S(2)}, u32[]{:S(2)}) collective-permute-start(bf16[304,128]{1,0:T(8,128)(2,1)S(1)} %get-tuple-element.72), channel_id=1, source_target_pairs={{0,1},{1,0},{2,3},{3,2},{4,5},{5,4},{6,7},{7,6},{8,9},{9,8},{10,11... | collective-permute-start | bytes 233480 | tf_op jit(solution)/shard_map/ppermute | solution.py:787
  46.2 24.3 %copy-start = (bf16[256,32,128]{2,1,0:T(8,128)(2,1)S(1)}, bf16[256,32,128]{2,1,0:T(8,128)(2,1)}, u32[]{:S(2)}) copy-start(bf16[256,32,128]{2,1,0:T(8,128)(2,1)} %get-tuple-element.90.refs_5_) | copy-start | bytes 6291460
  46.2 24.3 %copy-start.2 = (bf16[128,128]{1,0:T(8,128)(2,1)S(1)}, bf16[128,128]{1,0:T(8,128)(2,1)}, u32[]{:S(2)}) copy-start(bf16[128,128]{1,0:T(8,128)(2,1)} %refs_6_.1) | copy-start | bytes 98308
  46.2 8.0 %collective-permute-start.10 = (bf16[4,64,128]{2,1,0:T(8,128)(2,1)S(1)}, bf16[4,64,128]{2,1,0:T(8,128)(2,1)S(1)}, u32[]{:S(2)}, u32[]{:S(2)}) collective-permute-start(bf16[4,64,128]{2,1,0:T(8,128)(2,1)S(1)} %get-tuple-element.74.refs_0_), channel_id=1, source_target_pairs={{0,31},{1,30},{2,29},{3,28},{4,27},{5,26},{6,25},{7,24},{8,23},{9,... | collective-permute-start | bytes 196616 | tf_op jit(solution)/shard_map/ppermute | solution.py:841
  49.1 6.5 %collective-permute-start.9 = (bf16[4,64,128]{2,1,0:T(8,128)(2,1)S(1)}, bf16[4,64,128]{2,1,0:T(8,128)(2,1)S(1)}, u32[]{:S(2)}, u32[]{:S(2)}) collective-permute-start(bf16[4,64,128]{2,1,0:T(8,128)(2,1)S(1)} %get-tuple-element.74.refs_0_), channel_id=1, source_target_pairs={{0,30},{1,31},{2,28},{3,29},{4,26},{5,27},{6,24},{7,25},{8,22},{9,... | collective-permute-start | bytes 196616 | tf_op jit(solution)/shard_map/ppermute | solution.py:841
  50.5 5.2 %collective-permute-start.8 = (bf16[4,64,128]{2,1,0:T(8,128)(2,1)S(1)}, bf16[4,64,128]{2,1,0:T(8,128)(2,1)S(1)}, u32[]{:S(2)}, u32[]{:S(2)}) collective-permute-start(bf16[4,64,128]{2,1,0:T(8,128)(2,1)S(1)} %get-tuple-element.74.refs_0_), channel_id=1, source_target_pairs={{0,1},{1,0},{2,3},{3,2},{4,5},{5,4},{6,7},{7,6},{8,9},{9,8},{10,11... | collective-permute-start | bytes 196616 | tf_op jit(solution)/shard_map/ppermute | solution.py:841
  56.1 9.2 %collective-permute-start.11 = (bf16[704,128]{1,0:T(8,128)(2,1)S(1)}, bf16[704,128]{1,0:T(8,128)(2,1)S(1)}, u32[]{:S(2)}, u32[]{:S(2)}) collective-permute-start(bf16[704,128]{1,0:T(8,128)(2,1)S(1)} %get-tuple-element.81), channel_id=1, source_target_pairs={{0,4},{2,6},{4,0},{6,2},{8,12},{10,14},{12,8},{14,10},{16,20},{18,... | collective-permute-start | bytes 540680 | tf_op jit(solution)/shard_map/ppermute | solution.py:758
  57.5 7.9 %collective-permute-start.12 = (bf16[704,128]{1,0:T(8,128)(2,1)S(1)}, bf16[704,128]{1,0:T(8,128)(2,1)S(1)}, u32[]{:S(2)}, u32[]{:S(2)}) collective-permute-start(bf16[704,128]{1,0:T(8,128)(2,1)S(1)} %get-tuple-element.82), channel_id=1, source_target_pairs={{0,8},{2,10},{4,12},{6,14},{8,0},{10,2},{12,4},{14,6},{16,24},{18,... | collective-permute-start | bytes 540680 | tf_op jit(solution)/shard_map/ppermute | solution.py:758
  60.1 8.6 %collective-permute-start.13 = (bf16[704,128]{1,0:T(8,128)(2,1)S(1)}, bf16[704,128]{1,0:T(8,128)(2,1)S(1)}, u32[]{:S(2)}, u32[]{:S(2)}) collective-permute-start(bf16[704,128]{1,0:T(8,128)(2,1)S(1)} %get-tuple-element.83), channel_id=1, source_target_pairs={{0,12},{2,14},{4,8},{6,10},{8,4},{10,6},{12,0},{14,2},{16,28},{18,... | collective-permute-start | bytes 540680 | tf_op jit(solution)/shard_map/ppermute | solution.py:758
  68.8 1.7 %collective-permute-start.14 = (bf16[1408,128]{1,0:T(8,128)(2,1)S(1)}, bf16[1408,128]{1,0:T(8,128)(2,1)S(1)}, u32[]{:S(2)}, u32[]{:S(2)}) collective-permute-start(bf16[1408,128]{1,0:T(8,128)(2,1)S(1)} %pad_maximum_fusion), channel_id=1, source_target_pairs={{0,2},{2,0},{4,6},{6,4},{8,10},{10,8},{12,14},{14,12},{16,18},{18,... | collective-permute-start | bytes 1081352 | tf_op jit(solution)/shard_map/ppermute | solution.py:764

commit v9 on v8

--- a/solution.py
+++ b/solution.py
@@ -752,11 +752,11 @@
         )
 
     def to_chips(chips):
-        arrived = [chips[0]]
-        for pair in range(1, half // 2):
+        arrived = {0: chips[0]}
+        for pair in reversed(range(1, half // 2)):
             moves = [(d, d ^ (2 * pair)) for d in range(data_count)]
-            arrived.append(lax.ppermute(chips[pair], "dp", moves))
-        return arrived
+            arrived[pair] = lax.ppermute(chips[pair], "dp", moves)
+        return [arrived[pair] for pair in range(half // 2)]
 
     def between_cores(arrived):
         rows = arrived[0].shape[0] // 2

time: 73.6 us -> 73.6 us (level)
  no operation moved by 1% of the time
where the time goes in v9:
time: 73.6 us; the launch traced here: 73.4 us
  starting transfers between devices  27.1 us (37%)
  Pallas kernels  26.6 us (36%)
  waiting for transfers between devices  17 us (23%)
  other arithmetic  1.41 us (2%)
  between operations  0.89 us (1%)
    ppermute x6, starting transfers between devices, to_chips(): arrived[pair] = lax.ppermute(chips[pair], 'dp', moves)  8.68 us
    pallas_call x1, Pallas kernels, delta_call(): pl.pallas_call(functools.partial(delta_kernel, sizes), grid=(columns // b...  7.95 us
    ppermute x3, starting transfers between devices, on_device(): lax.ppermute(back, ('dp', 'space'), pairs(mirror, shift))  5.98 us
    ppermute x3, starting transfers between devices, gathered(): lax.ppermute(parts[mirror * space_count + shift], ('dp', 'space'), pairs(...  5.97 us
    pallas_call x1, Pallas kernels, outer_call(): pl.pallas_call(functools.partial(outer_kernel, sizes), grid=(held,), in_s...  5.05 us
    all_to_all x1, starting transfers between devices, exchange(): lax.all_to_all(values, 'dp', split_axis=0, concat_axis=0, tiled=True, axi...  4.21 us
    ppermute x1, waiting for transfers between devices, on_device(): lax.ppermute(input_parts[shift], ('dp', 'space'), pairs(0, shift))  4.02 us
    pallas_call x1, Pallas kernels, load_call(): pl.pallas_call(load_kernel, in_specs=[pl.BlockSpec(memory_space=pl.ANY)],...  3.57 us
  transfers between devices with their start and end apart: 16, of which 10 were waited for; matrix products, arithmetic and copies ran while one was open for 2% of the time, Pallas kernels for 23%

profile of v9, /device:TPU:0, one launch (start us, length us, event | category | flops | bytes accessed | tf_op | source)
XLA Modules:
  0.0 73.4 jit_solution(3368001367287805183)
XLA Ops:
  0.6 3.1 %input_x_sums.1 = (bf16[640,128]{1,0:T(8,128)(2,1)}, bf16[640,128]{1,0:T(8,128)(2,1)}, bf16[640,128]{1,0:T(8,128)(2,1)}, bf16[640,128]{1,0:T(8,128)(2,1)}) custom-call(bf16[256,32,128]{2,1,0:T(8,128)(2,1)} %bitcast.7, bf16[256,32,128]{2,1,0:T(8,128)(2,1)} %bitcast.8, bf16[256,32,128]{2,1,0:T(8,128)(2,1)} %bitcast.9, bf16[256,32,128]{2,1,0:T(8,128)(2,1)} %bitcast.10), custom_call_target="tpu_custom_call" | custom-call | flops 167772160 | bytes 4194304 | tf_op jit(solution)/shard_map/input_x_sums/pallas_call | solution.py:289
  3.7 2.9 %collective-permute-start = (bf16[640,128]{1,0:T(8,128)(2,1)}, bf16[640,128]{1,0:T(8,128)(2,1)S(1)}, u32[]{:S(2)}, u32[]{:S(2)}) collective-permute-start(bf16[640,128]{1,0:T(8,128)(2,1)} %get-tuple-element.52), channel_id=1, source_target_pairs={{0,4},{2,6},{4,0},{6,2},{8,12},{10,14},{12,8},{14,10},{16,20},{18,... | collective-permute-start | bytes 491528 | tf_op jit(solution)/shard_map/ppermute | solution.py:758
  6.6 1.6 %collective-permute-start.1 = (bf16[640,128]{1,0:T(8,128)(2,1)}, bf16[640,128]{1,0:T(8,128)(2,1)S(1)}, u32[]{:S(2)}, u32[]{:S(2)}) collective-permute-start(bf16[640,128]{1,0:T(8,128)(2,1)} %get-tuple-element.53), channel_id=1, source_target_pairs={{0,8},{2,10},{4,12},{6,14},{8,0},{10,2},{12,4},{14,6},{16,24},{18,... | collective-permute-start | bytes 491528 | tf_op jit(solution)/shard_map/ppermute | solution.py:758
  8.2 7.9 %delta_and_x_sums.1 = (bf16[256,32,128]{2,1,0:T(8,128)(2,1)}, bf16[8,352,128]{2,1,0:T(8,128)(2,1)}) custom-call(bf16[256,32,128]{2,1,0:T(8,128)(2,1)} %bitcast.12, bf16[256,32,128]{2,1,0:T(8,128)(2,1)} %bitcast.13, bf16[256,32,128]{2,1,0:T(8,128)(2,1)} %bitcast.11), custom_call_target="tpu_custom_call" | custom-call | flops 335544320 | bytes 8388608 | tf_op jit(solution)/shard_map/delta_and_x_sums/pallas_call | solution.py:235
  16.3 4.2 %all-to-all-start = ((bf16[8,352,128]{2,1,0:T(8,128)(2,1)}), bf16[8,352,128]{2,1,0:T(8,128)(2,1)S(1)}, u32[]{:S(2)}, u32[]{:S(2)}) async-start(bf16[8,352,128]{2,1,0:T(8,128)(2,1)} %get-tuple-element.55), calls=%async_computation | async-start | bytes 1441792 | tf_op jit(solution)/shard_map/all_to_all | solution.py:750
  21.4 1.3 %fusion.1 = (bf16[256,512]{1,0:T(8,128)(2,1)S(1)}, bf16[256,512]{1,0:T(8,128)(2,1)S(1)}) fusion(s32[256,256]{1,0:T(8,128)S(1)} %broadcast_in_dim.17, s32[256,256]{1,0:T(8,128)S(1)} %broadcast_in_dim.16, s32[512]{0:T(512)S(1)} %pad_add_fusion.1, s32[256]{0:T(256)S(1)} %fusion.23, s32[512]{0:T(512)S(1)} %pad_add_fusion), kind=kLoop, calls=%fused_computation.3 | loop fusion | flops 9699328 | bytes 1053696 | tf_op jit(solution)/shard_map/convert_element_type | solution.py:44
  23.2 1.6 %collective-permute-start.4 = (bf16[512,128]{1,0:T(8,128)(2,1)S(1)}, bf16[512,128]{1,0:T(8,128)(2,1)S(1)}, u32[]{:S(2)}, u32[]{:S(2)}) collective-permute-start(bf16[512,128]{1,0:T(8,128)(2,1)S(1)} %get-tuple-element.61), channel_id=1, source_target_pairs={{0,1},{1,0},{2,3},{3,2},{4,5},{5,4},{6,7},{7,6},{8,9},{9,8},{10,11... | collective-permute-start | bytes 393224 | tf_op jit(solution)/shard_map/ppermute | solution.py:813
  24.7 4.0 %collective-permute-done.4.refs_1_ = bf16[512,128]{1,0:T(8,128)(2,1)S(1)} collective-permute-done((bf16[512,128]{1,0:T(8,128)(2,1)S(1)}, bf16[512,128]{1,0:T(8,128)(2,1)S(1)}, u32[]{:S(2)}, u32[]{:S(2)}) %collective-permute-start.4) | collective-permute-done | bytes 131104 | tf_op jit(solution)/shard_map/ppermute | solution.py:813
  28.8 2.6 %all-to-all-done = bf16[8,352,128]{2,1,0:T(8,128)(2,1)S(1)} async-done(((bf16[8,352,128]{2,1,0:T(8,128)(2,1)}), bf16[8,352,128]{2,1,0:T(8,128)(2,1)S(1)}, u32[]{:S(2)}, u32[]{:S(2)}) %all-to-all-start) | async-done | bytes 720928 | tf_op jit(solution)/shard_map/all_to_all | solution.py:750
  31.9 2.8 %collective-permute-start.6 = (bf16[560,128]{1,0:T(8,128)(2,1)S(1)}, bf16[560,128]{1,0:T(8,128)(2,1)S(1)}, u32[]{:S(2)}, u32[]{:S(2)}) collective-permute-start(bf16[560,128]{1,0:T(8,128)(2,1)S(1)} %pad_maximum_fusion.2), channel_id=1, source_target_pairs={{0,30},{1,31},{2,28},{3,29},{4,26},{5,27},{6,24},{7,25},{8,22},{9,... | collective-permute-start | bytes 430088 | tf_op jit(solution)/shard_map/ppermute | solution.py:787
  34.7 2.7 %collective-permute-start.5 = (bf16[304,128]{1,0:T(8,128)(2,1)S(1)}, bf16[304,128]{1,0:T(8,128)(2,1)S(1)}, u32[]{:S(2)}, u32[]{:S(2)}) collective-permute-start(bf16[304,128]{1,0:T(8,128)(2,1)S(1)} %get-tuple-element.70), channel_id=1, source_target_pairs={{0,31},{1,30},{2,29},{3,28},{4,27},{5,26},{6,25},{7,24},{8,23},{9,... | collective-permute-start | bytes 233480 | tf_op jit(solution)/shard_map/ppermute | solution.py:787
  37.9 3.6 %weights_to_vmem.1.weight_ref = bf16[4,32,2,128,128]{4,3,2,1,0:T(8,128)(2,1)S(1)} custom-call(bf16[4,32,2,128,128]{4,3,2,1,0:T(8,128)(2,1)} %source_ref), custom_call_target="tpu_custom_call" | custom-call | bytes 16777216 | tf_op jit(solution)/shard_map/weights_to_vmem/pallas_call | solution.py:427
  43.5 2.7 %mode_back.1 = (bf16[4,64,128]{2,1,0:T(8,128)(2,1)S(1)}, bf16[4,64,128]{2,1,0:T(8,128)(2,1)S(1)}, bf16[48,128]{1,0:T(8,128)(2,1)S(1)}) custom-call(f32[64,128]{1,0:T(8,128)S(1)} %broadcast_in_dim.20.scale_ref, bf16[4,32,2,128,128]{4,3,2,1,0:T(8,128)(2,1)S(1)} %weights_to_vmem.1.weight_ref, bf16[304,128]{1,0:T(8,128)(2,1)S(1)} %get-tuple-element.69.refs_0_, ...), custom_call_target="tpu_custom_call" | custom-call | flops 16777216 | bytes 8388608 | tf_op jit(solution)/shard_map/mode_back/pallas_call | solution.py:485
  46.2 2.8 %collective-permute-start.10 = (bf16[4,64,128]{2,1,0:T(8,128)(2,1)S(1)}, bf16[4,64,128]{2,1,0:T(8,128)(2,1)S(1)}, u32[]{:S(2)}, u32[]{:S(2)}) collective-permute-start(bf16[4,64,128]{2,1,0:T(8,128)(2,1)S(1)} %get-tuple-element.74.refs_0_), channel_id=1, source_target_pairs={{0,31},{1,30},{2,29},{3,28},{4,27},{5,26},{6,25},{7,24},{8,23},{9,... | collective-permute-start | bytes 196616 | tf_op jit(solution)/shard_map/ppermute | solution.py:841
  49.1 1.4 %collective-permute-start.9 = (bf16[4,64,128]{2,1,0:T(8,128)(2,1)S(1)}, bf16[4,64,128]{2,1,0:T(8,128)(2,1)S(1)}, u32[]{:S(2)}, u32[]{:S(2)}) collective-permute-start(bf16[4,64,128]{2,1,0:T(8,128)(2,1)S(1)} %get-tuple-element.74.refs_0_), channel_id=1, source_target_pairs={{0,30},{1,31},{2,28},{3,29},{4,26},{5,27},{6,24},{7,25},{8,22},{9,... | collective-permute-start | bytes 196616 | tf_op jit(solution)/shard_map/ppermute | solution.py:841
  50.5 1.7 %collective-permute-start.8 = (bf16[4,64,128]{2,1,0:T(8,128)(2,1)S(1)}, bf16[4,64,128]{2,1,0:T(8,128)(2,1)S(1)}, u32[]{:S(2)}, u32[]{:S(2)}) collective-permute-start(bf16[4,64,128]{2,1,0:T(8,128)(2,1)S(1)} %get-tuple-element.74.refs_0_), channel_id=1, source_target_pairs={{0,1},{1,0},{2,3},{3,2},{4,5},{5,4},{6,7},{7,6},{8,9},{9,8},{10,11... | collective-permute-start | bytes 196616 | tf_op jit(solution)/shard_map/ppermute | solution.py:841
  52.2 2.1 %collective-permute-done.10.refs_3_ = bf16[4,64,128]{2,1,0:T(8,128)(2,1)S(1)} collective-permute-done((bf16[4,64,128]{2,1,0:T(8,128)(2,1)S(1)}, bf16[4,64,128]{2,1,0:T(8,128)(2,1)S(1)}, u32[]{:S(2)}, u32[]{:S(2)}) %collective-permute-start.10) | collective-permute-done | bytes 65568 | tf_op jit(solution)/shard_map/ppermute | solution.py:841
  54.3 1.3 %collective-permute-done.9.refs_2_ = bf16[4,64,128]{2,1,0:T(8,128)(2,1)S(1)} collective-permute-done((bf16[4,64,128]{2,1,0:T(8,128)(2,1)S(1)}, bf16[4,64,128]{2,1,0:T(8,128)(2,1)S(1)}, u32[]{:S(2)}, u32[]{:S(2)}) %collective-permute-start.9) | collective-permute-done | bytes 65568 | tf_op jit(solution)/shard_map/ppermute | solution.py:841
  56.1 1.4 %collective-permute-start.11 = (bf16[704,128]{1,0:T(8,128)(2,1)S(1)}, bf16[704,128]{1,0:T(8,128)(2,1)S(1)}, u32[]{:S(2)}, u32[]{:S(2)}) collective-permute-start(bf16[704,128]{1,0:T(8,128)(2,1)S(1)} %get-tuple-element.81), channel_id=1, source_target_pairs={{0,4},{2,6},{4,0},{6,2},{8,12},{10,14},{12,8},{14,10},{16,20},{18,... | collective-permute-start | bytes 540680 | tf_op jit(solution)/shard_map/ppermute | solution.py:758
  57.5 2.5 %collective-permute-start.12 = (bf16[704,128]{1,0:T(8,128)(2,1)S(1)}, bf16[704,128]{1,0:T(8,128)(2,1)S(1)}, u32[]{:S(2)}, u32[]{:S(2)}) collective-permute-start(bf16[704,128]{1,0:T(8,128)(2,1)S(1)} %get-tuple-element.82), channel_id=1, source_target_pairs={{0,8},{2,10},{4,12},{6,14},{8,0},{10,2},{12,4},{14,6},{16,24},{18,... | collective-permute-start | bytes 540680 | tf_op jit(solution)/shard_map/ppermute | solution.py:758
  60.3 5.1 %grad_spectral.1 = (bf16[4,32,2,128,128]{4,3,2,1,0:T(8,128)(2,1)}, bf16[256,80]{1,0:T(8,128)(2,1)S(1)}) custom-call(f32[64,128]{1,0:T(8,128)S(1)} %broadcast_in_dim.20.scale_ref, bf16[4,64,128]{2,1,0:T(8,128)(2,1)S(1)} %get-tuple-element.84.delta_ref, bf16[512,128]{1,0:T(8,128)(2,1)S(1)} %get-tuple-element.60.refs_0_, ...), custom_call_target="tpu_custom_call" | custom-call | flops 12582912 | bytes 8388608 | tf_op jit(solution)/shard_map/grad_spectral/pallas_call | solution.py:541
  65.5 3.2 %collective-permute-done.13.refs_3_ = bf16[704,128]{1,0:T(8,128)(2,1)S(1)} collective-permute-done((bf16[704,128]{1,0:T(8,128)(2,1)S(1)}, bf16[704,128]{1,0:T(8,128)(2,1)S(1)}, u32[]{:S(2)}, u32[]{:S(2)}) %collective-permute-start.13) | collective-permute-done | bytes 180256 | tf_op jit(solution)/shard_map/ppermute | solution.py:758
  68.9 1.7 %collective-permute-done.14.refs_4_ = bf16[1408,128]{1,0:T(8,128)(2,1)S(1)} collective-permute-done((bf16[1408,128]{1,0:T(8,128)(2,1)S(1)}, bf16[1408,128]{1,0:T(8,128)(2,1)S(1)}, u32[]{:S(2)}, u32[]{:S(2)}) %collective-permute-start.14) | collective-permute-done | bytes 360480 | tf_op jit(solution)/shard_map/ppermute | solution.py:764
  70.5 2.9 %x_inverse_and_local.1 = (bf16[256,32,128]{2,1,0:T(8,128)(2,1)}, f32[128,128]{1,0:T(8,128)}, f32[1,128]{1,0:T(1,128)}) custom-call(bf16[704,128]{1,0:T(8,128)(2,1)S(1)} %get-tuple-element.86.refs_0_, bf16[704,128]{1,0:T(8,128)(2,1)S(1)} %collective-permute-done.11.refs_1_, bf16[704,128]{1,0:T(8,128)(2,1)S(1)} %collective-permute-done.12.refs_2_, ...), custom_call_target="tpu_custom_call" | custom-call | flops 436207616 | bytes 5242880 | tf_op jit(solution)/shard_map/x_inverse_and_local/pallas_call | solution.py:685
  (48 shorter events, 5.5 us)
Async XLA Ops:
  3.7 12.5 %collective-permute-start = (bf16[640,128]{1,0:T(8,128)(2,1)}, bf16[640,128]{1,0:T(8,128)(2,1)S(1)}, u32[]{:S(2)}, u32[]{:S(2)}) collective-permute-start(bf16[640,128]{1,0:T(8,128)(2,1)} %get-tuple-element.52), channel_id=1, source_target_pairs={{0,4},{2,6},{4,0},{6,2},{8,12},{10,14},{12,8},{14,10},{16,20},{18,... | collective-permute-start | bytes 491528 | tf_op jit(solution)/shard_map/ppermute | solution.py:758
  6.6 9.6 %collective-permute-start.1 = (bf16[640,128]{1,0:T(8,128)(2,1)}, bf16[640,128]{1,0:T(8,128)(2,1)S(1)}, u32[]{:S(2)}, u32[]{:S(2)}) collective-permute-start(bf16[640,128]{1,0:T(8,128)(2,1)} %get-tuple-element.53), channel_id=1, source_target_pairs={{0,8},{2,10},{4,12},{6,14},{8,0},{10,2},{12,4},{14,6},{16,24},{18,... | collective-permute-start | bytes 491528 | tf_op jit(solution)/shard_map/ppermute | solution.py:758
  8.2 8.0 %collective-permute-start.2 = (bf16[640,128]{1,0:T(8,128)(2,1)}, bf16[640,128]{1,0:T(8,128)(2,1)S(1)}, u32[]{:S(2)}, u32[]{:S(2)}) collective-permute-start(bf16[640,128]{1,0:T(8,128)(2,1)} %get-tuple-element.54), channel_id=1, source_target_pairs={{0,12},{2,14},{4,8},{6,10},{8,4},{10,6},{12,0},{14,2},{16,28},{18,... | collective-permute-start | bytes 491528 | tf_op jit(solution)/shard_map/ppermute | solution.py:758
  8.2 12.3 %copy-start.1 = (bf16[640,128]{1,0:T(8,128)(2,1)S(1)}, bf16[640,128]{1,0:T(8,128)(2,1)}, u32[]{:S(2)}) copy-start(bf16[640,128]{1,0:T(8,128)(2,1)} %get-tuple-element.56.refs_0_) | copy-start | bytes 491524
  16.3 15.2 %all-to-all-start = ((bf16[8,352,128]{2,1,0:T(8,128)(2,1)}), bf16[8,352,128]{2,1,0:T(8,128)(2,1)S(1)}, u32[]{:S(2)}, u32[]{:S(2)}) async-start(bf16[8,352,128]{2,1,0:T(8,128)(2,1)} %get-tuple-element.55), calls=%async_computation | async-start | bytes 1441792 | tf_op jit(solution)/shard_map/all_to_all | solution.py:750
  20.6 2.0 %collective-permute-start.3 = (bf16[1280,128]{1,0:T(8,128)(2,1)S(1)}, bf16[1280,128]{1,0:T(8,128)(2,1)S(1)}, u32[]{:S(2)}, u32[]{:S(2)}) collective-permute-start(bf16[1280,128]{1,0:T(8,128)(2,1)S(1)} %pad_maximum_fusion.1), channel_id=1, source_target_pairs={{0,2},{2,0},{4,6},{6,4},{8,10},{10,8},{12,14},{14,12},{16,18},{18,... | collective-permute-start | bytes 983048 | tf_op jit(solution)/shard_map/ppermute | solution.py:764
  23.2 5.6 %collective-permute-start.4 = (bf16[512,128]{1,0:T(8,128)(2,1)S(1)}, bf16[512,128]{1,0:T(8,128)(2,1)S(1)}, u32[]{:S(2)}, u32[]{:S(2)}) collective-permute-start(bf16[512,128]{1,0:T(8,128)(2,1)S(1)} %get-tuple-element.61), channel_id=1, source_target_pairs={{0,1},{1,0},{2,3},{3,2},{4,5},{5,4},{6,7},{7,6},{8,9},{9,8},{10,11... | collective-permute-start | bytes 393224 | tf_op jit(solution)/shard_map/ppermute | solution.py:813
  31.9 9.6 %collective-permute-start.6 = (bf16[560,128]{1,0:T(8,128)(2,1)S(1)}, bf16[560,128]{1,0:T(8,128)(2,1)S(1)}, u32[]{:S(2)}, u32[]{:S(2)}) collective-permute-start(bf16[560,128]{1,0:T(8,128)(2,1)S(1)} %pad_maximum_fusion.2), channel_id=1, source_target_pairs={{0,30},{1,31},{2,28},{3,29},{4,26},{5,27},{6,24},{7,25},{8,22},{9,... | collective-permute-start | bytes 430088 | tf_op jit(solution)/shard_map/ppermute | solution.py:787
  34.7 7.8 %collective-permute-start.5 = (bf16[304,128]{1,0:T(8,128)(2,1)S(1)}, bf16[304,128]{1,0:T(8,128)(2,1)S(1)}, u32[]{:S(2)}, u32[]{:S(2)}) collective-permute-start(bf16[304,128]{1,0:T(8,128)(2,1)S(1)} %get-tuple-element.70), channel_id=1, source_target_pairs={{0,31},{1,30},{2,29},{3,28},{4,27},{5,26},{6,25},{7,24},{8,23},{9,... | collective-permute-start | bytes 233480 | tf_op jit(solution)/shard_map/ppermute | solution.py:787
  37.4 6.1 %collective-permute-start.7 = (bf16[304,128]{1,0:T(8,128)(2,1)S(1)}, bf16[304,128]{1,0:T(8,128)(2,1)S(1)}, u32[]{:S(2)}, u32[]{:S(2)}) collective-permute-start(bf16[304,128]{1,0:T(8,128)(2,1)S(1)} %get-tuple-element.72), channel_id=1, source_target_pairs={{0,1},{1,0},{2,3},{3,2},{4,5},{5,4},{6,7},{7,6},{8,9},{9,8},{10,11... | collective-permute-start | bytes 233480 | tf_op jit(solution)/shard_map/ppermute | solution.py:787
  46.2 24.3 %copy-start = (bf16[256,32,128]{2,1,0:T(8,128)(2,1)S(1)}, bf16[256,32,128]{2,1,0:T(8,128)(2,1)}, u32[]{:S(2)}) copy-start(bf16[256,32,128]{2,1,0:T(8,128)(2,1)} %get-tuple-element.90.refs_5_) | copy-start | bytes 6291460
  46.2 24.3 %copy-start.2 = (bf16[128,128]{1,0:T(8,128)(2,1)S(1)}, bf16[128,128]{1,0:T(8,128)(2,1)}, u32[]{:S(2)}) copy-start(bf16[128,128]{1,0:T(8,128)(2,1)} %refs_6_.1) | copy-start | bytes 98308
  46.2 8.0 %collective-permute-start.10 = (bf16[4,64,128]{2,1,0:T(8,128)(2,1)S(1)}, bf16[4,64,128]{2,1,0:T(8,128)(2,1)S(1)}, u32[]{:S(2)}, u32[]{:S(2)}) collective-permute-start(bf16[4,64,128]{2,1,0:T(8,128)(2,1)S(1)} %get-tuple-element.74.refs_0_), channel_id=1, source_target_pairs={{0,31},{1,30},{2,29},{3,28},{4,27},{5,26},{6,25},{7,24},{8,23},{9,... | collective-permute-start | bytes 196616 | tf_op jit(solution)/shard_map/ppermute | solution.py:841
  49.1 6.5 %collective-permute-start.9 = (bf16[4,64,128]{2,1,0:T(8,128)(2,1)S(1)}, bf16[4,64,128]{2,1,0:T(8,128)(2,1)S(1)}, u32[]{:S(2)}, u32[]{:S(2)}) collective-permute-start(bf16[4,64,128]{2,1,0:T(8,128)(2,1)S(1)} %get-tuple-element.74.refs_0_), channel_id=1, source_target_pairs={{0,30},{1,31},{2,28},{3,29},{4,26},{5,27},{6,24},{7,25},{8,22},{9,... | collective-permute-start | bytes 196616 | tf_op jit(solution)/shard_map/ppermute | solution.py:841
  50.5 5.2 %collective-permute-start.8 = (bf16[4,64,128]{2,1,0:T(8,128)(2,1)S(1)}, bf16[4,64,128]{2,1,0:T(8,128)(2,1)S(1)}, u32[]{:S(2)}, u32[]{:S(2)}) collective-permute-start(bf16[4,64,128]{2,1,0:T(8,128)(2,1)S(1)} %get-tuple-element.74.refs_0_), channel_id=1, source_target_pairs={{0,1},{1,0},{2,3},{3,2},{4,5},{5,4},{6,7},{7,6},{8,9},{9,8},{10,11... | collective-permute-start | bytes 196616 | tf_op jit(solution)/shard_map/ppermute | solution.py:841
  56.1 9.2 %collective-permute-start.11 = (bf16[704,128]{1,0:T(8,128)(2,1)S(1)}, bf16[704,128]{1,0:T(8,128)(2,1)S(1)}, u32[]{:S(2)}, u32[]{:S(2)}) collective-permute-start(bf16[704,128]{1,0:T(8,128)(2,1)S(1)} %get-tuple-element.81), channel_id=1, source_target_pairs={{0,4},{2,6},{4,0},{6,2},{8,12},{10,14},{12,8},{14,10},{16,20},{18,... | collective-permute-start | bytes 540680 | tf_op jit(solution)/shard_map/ppermute | solution.py:758
  57.5 7.9 %collective-permute-start.12 = (bf16[704,128]{1,0:T(8,128)(2,1)S(1)}, bf16[704,128]{1,0:T(8,128)(2,1)S(1)}, u32[]{:S(2)}, u32[]{:S(2)}) collective-permute-start(bf16[704,128]{1,0:T(8,128)(2,1)S(1)} %get-tuple-element.82), channel_id=1, source_target_pairs={{0,8},{2,10},{4,12},{6,14},{8,0},{10,2},{12,4},{14,6},{16,24},{18,... | collective-permute-start | bytes 540680 | tf_op jit(solution)/shard_map/ppermute | solution.py:758
  60.1 8.6 %collective-permute-start.13 = (bf16[704,128]{1,0:T(8,128)(2,1)S(1)}, bf16[704,128]{1,0:T(8,128)(2,1)S(1)}, u32[]{:S(2)}, u32[]{:S(2)}) collective-permute-start(bf16[704,128]{1,0:T(8,128)(2,1)S(1)} %get-tuple-element.83), channel_id=1, source_target_pairs={{0,12},{2,14},{4,8},{6,10},{8,4},{10,6},{12,0},{14,2},{16,28},{18,... | collective-permute-start | bytes 540680 | tf_op jit(solution)/shard_map/ppermute | solution.py:758
  68.8 1.7 %collective-permute-start.14 = (bf16[1408,128]{1,0:T(8,128)(2,1)S(1)}, bf16[1408,128]{1,0:T(8,128)(2,1)S(1)}, u32[]{:S(2)}, u32[]{:S(2)}) collective-permute-start(bf16[1408,128]{1,0:T(8,128)(2,1)S(1)} %pad_maximum_fusion), channel_id=1, source_target_pairs={{0,2},{2,0},{4,6},{6,4},{8,10},{10,8},{12,14},{14,12},{16,18},{18,... | collective-permute-start | bytes 1081352 | tf_op jit(solution)/shard_map/ppermute | solution.py:764
